TPU v7x, 256 devices: a whole 4x4x8 slice. The times are simulated.
256 devices in a mesh: store: 32 (over z, x), head: 8 (over y, core).
Axes of the slice: x: 4, y: 4, z: 8, core: 2. Of those that a mesh axis runs over, the one named last changes fastest.
Arguments:
- queries: bfloat16 [2048, 8192], P('store', 'head'), may hold values from -16 to 16
- suffix_kv: bfloat16 [2048, 8, 256], P('store', 'head'), may hold values from -6 to 6
- kv_cache: bfloat16 [4096, 8, 64, 256], P('store', 'head'), may hold values from -16 to 16
- block_owner: int32 [32, 128], P('store'), may hold values from 0 to 31, as said below
- block_slot: int32 [32, 128], P('store'), may hold values from 0 to 127, as said below
- prefix_blocks: int32 [32], P('store'), may hold values from 1 to 128, as said below
- out_weight: bfloat16 [8192, 4096], P('head'), may hold values from -0.0625 to 0.0625
Outputs:
- projected: bfloat16 [2048, 4096], P(('store', 'head'))
Inputs may be any that keep to these rules, and one draw needn't show every extreme that they name: `block_owner`: entries j < prefix_blocks of a request name the owners of its cached blocks; a request has at most 4 live blocks at one owner, and some request has exactly 4 at every owner; later entries are arbitrary. `block_slot`: slot of each block at its owner; the live entries of all requests name distinct owner and slot pairs. `prefix_blocks`: the largest equals 128.
All inputs are finite; a program needn't handle non-finite values.
Results may differ from a plain program's by a relative error of at most 0.022.
Values may be sent and summed in bfloat16 or wider, within the bound.
No kernel may reach another device: no remote copies, remote signals or barrier semaphores. Data moves between devices by JAX's collectives and lax.ppermute only.
A program may use at most 128 MiB of HBM per device.

v0:
```python
import math

import jax
import jax.numpy as jnp
from jax import lax
from jax.sharding import PartitionSpec as P

HD = 128
SUF = 64
BLK = 64
CAP = 4
GROUP = 8


NEG_FILL = -1e30


def softmax_parts(scores, mask, axes):
    masked = jnp.where(mask, scores, NEG_FILL)
    row_peak = jnp.max(masked, axis=axes, keepdims=True)
    weights = jnp.where(mask, jnp.exp(masked - row_peak), 0.0)
    return (
        jnp.squeeze(row_peak, axis=axes),
        jnp.sum(weights, axis=axes),
        weights.astype(jnp.bfloat16),
    )


def local(queries, suffix_kv, kv_cache, block_owner, block_slot, prefix_blocks, out_weight):
    store_count = lax.axis_size("store")
    kv_here = suffix_kv.shape[1]
    row_count = SUF * GROUP
    inv_root = 1.0 / math.sqrt(HD)
    query_rows = (
        queries.reshape(SUF, kv_here, GROUP, HD)
        .transpose(1, 0, 2, 3)
        .reshape(kv_here, row_count, HD)
    )
    owner_list = block_owner[0]
    slot_list = block_slot[0]
    in_prefix = jnp.arange(owner_list.shape[0]) < prefix_blocks[0]
    at_owner = (owner_list[:, None] == jnp.arange(store_count)[None, :]) & in_prefix[:, None]
    ordinal = jnp.cumsum(at_owner.astype(jnp.int32), axis=0) - 1
    placed = at_owner[:, :, None] & (ordinal[:, :, None] == jnp.arange(CAP)[None, None, :])
    wanted = jnp.sum(jnp.where(placed, slot_list[:, None, None] + 1, 0), axis=0) - 1
    requested = lax.all_to_all(wanted, "store", split_axis=0, concat_axis=0, tiled=True)
    selected = kv_cache[jnp.maximum(requested, 0).reshape(-1)].reshape(
        store_count, CAP, kv_here, BLK, 2 * HD
    )
    suffix_heads = suffix_kv.transpose(1, 0, 2)
    token_of_row = jnp.arange(row_count) // GROUP
    causal = jnp.arange(SUF)[None, :] <= token_of_row[:, None]
    own_scores = (
        jnp.einsum(
            "grd,gkd->grk", query_rows, suffix_heads[:, :, :HD], preferred_element_type=jnp.float32
        )
        * inv_root
    )
    own_peak, own_sum, own_weights = softmax_parts(own_scores, causal[None], (2,))
    own_acc = jnp.einsum(
        "grk,gkd->grd", own_weights, suffix_heads[:, :, HD:], preferred_element_type=jnp.float32
    )
    everyone = lax.all_gather(queries, "store", axis=0, tiled=True)
    all_rows = (
        everyone.reshape(store_count, SUF, kv_here, GROUP, HD)
        .transpose(0, 2, 1, 3, 4)
        .reshape(store_count, kv_here, row_count, HD)
    )
    scores = (
        jnp.einsum(
            "hgrd,hcgbd->hgrcb", all_rows, selected[..., :HD], preferred_element_type=jnp.float32
        )
        * inv_root
    )
    usable = (requested >= 0)[:, None, None, :, None]
    far_peak, far_sum, far_weights = softmax_parts(scores, usable, (3, 4))
    far_acc = jnp.einsum(
        "hgrcb,hcgbd->hgrd", far_weights, selected[..., HD:], preferred_element_type=jnp.float32
    )
    back_acc, back_peak, back_sum = (
        lax.all_to_all(far_acc, "store", split_axis=0, concat_axis=0, tiled=True),
        lax.all_to_all(far_peak, "store", split_axis=0, concat_axis=0, tiled=True),
        lax.all_to_all(far_sum, "store", split_axis=0, concat_axis=0, tiled=True),
    )
    row_peak = jnp.maximum(own_peak, jnp.max(back_peak, axis=0))
    factor = jnp.exp(back_peak - row_peak[None])
    own_factor = jnp.exp(own_peak - row_peak)
    row_sum = own_sum * own_factor + jnp.sum(back_sum * factor, axis=0)
    summed = own_acc * own_factor[..., None] + jnp.sum(back_acc * factor[..., None], axis=0)
    attended = (summed / row_sum[..., None]).astype(jnp.bfloat16)
    flattened = (
        attended.reshape(kv_here, SUF, GROUP, HD)
        .transpose(1, 0, 2, 3)
        .reshape(SUF, kv_here * GROUP * HD)
    )
    my_rows = lax.psum_scatter(
        jnp.dot(flattened, out_weight, preferred_element_type=jnp.float32).astype(jnp.bfloat16),
        "head",
        scatter_dimension=0,
        tiled=True,
    )
    return my_rows


def solution(mesh):
    in_specs = (
        P("store", "head"),
        P("store", "head", None),
        P("store", "head", None, None),
        P("store", None),
        P("store", None),
        P("store"),
        P("head", None),
    )
    out_specs = P(("store", "head"), None)
    return jax.shard_map(local, mesh=mesh, in_specs=in_specs, out_specs=out_specs, check_vma=False)
```

profile of v0, /device:TPU:24, one launch (start us, length us, event | category | flops | bytes accessed | tf_op | source)
XLA Modules:
  0.0 381.1 jit_solution(1347518215454629966)
XLA Ops:
  6.5 0.7 all-gather.2.cloned.1.call-update
  7.9 0.8 fusion.27
  8.8 0.2 reduce_window_sum.11
  9.0 0.7 add_bitcast_fusion.1
  9.7 0.1 select_reduce_fusion
  9.9 20.8 %all_to_all.21 = s32[32,1,4]{2,1,0:T(1,128)S(1)} all-to-all(s32[32,1,4]{2,1,0:T(1,128)S(1)} %copy.21), channel_id=1, replica_groups=mesh['store'=32,'head'=8] {'store'}, dimensions={0} | all-to-all | bytes 1024 | tf_op jit(solution)/shard_map/all_to_all | solution.py:46
  31.2 5.0 %gather_fusion = bf16[128,64,256]{2,1,0:T(8,128)(2,1)} fusion(bf16[128,64,256]{2,1,0:T(8,128)(2,1)} %bitcast.60, s32[1024]{0:T(1024)S(1)} %pad_clamp_fusion), kind=kCustom, calls=%fused_computation | custom fusion | bytes 8389120 | tf_op jit(solution)/shard_map/gather | solution.py:47
  36.2 58.3 %all-gather.2.cloned.1.call-done = bf16[2048,1024]{1,0:T(8,128)(2,1)} async-done(((bf16[64,1024]{1,0:T(8,128)(2,1)}), bf16[2048,1024]{1,0:T(8,128)(2,1)}) %all-gather.2.cloned.1.call-update) | async-done | bytes 4194320 | tf_op jit(solution)/shard_map/all_gather | solution.py:63
  94.4 7.3 %reshape.274 = bf16[32,512,128,1]{2,1,0,3:T(8,128)(2,1)} reshape(bf16[2048,1024]{1,0:T(8,128)(2,1)} %all-gather.2.cloned.1.call-done) | data formatting | bytes 8388608 | tf_op jit(solution)/shard_map/reshape.10
  101.7 5.3 %bitcast_reduce_fusion = (f32[32,512]{1,0:T(8,128)S(1)}, f32[32,4,64,512]{3,2,1,0:T(8,128)S(1)}) fusion(pred[32,4]{1,0:T(8,128)(4,1)S(1)} %copy.23, bf16[32,512,128,1]{2,1,0,3:T(8,128)(2,1)} %reshape.274, bf16[32,4,1,64,256]{4,3,1,0,2:T(8,128)(2,1)} %bitcast.58), kind=kOutput, calls=%fused_computation.2 | convolution fusion | flops 1086308352 | bytes 23134336 | tf_op jit(solution)/shard_map/hgrd,hcgbd->hgrcb/dot_general | solution.py:70
  107.1 5.8 %fusion.2 = f32[32,512]{1,0:T(8,128)S(1)} fusion(f32[32,4,64,512]{3,2,1,0:T(8,128)S(1)} %get-tuple-element.12, f32[32,512]{1,0:T(8,128)S(1)} %get-tuple-element.11, pred[32,4]{1,0:T(8,128)(4,1)S(1)} %copy.23), kind=kLoop, calls=%fused_computation.6 | loop fusion | flops 20955136 | bytes 16908416 | tf_op jit(solution)/shard_map/reduce_sum | solution.py:24
  113.0 0.7 reduce_sum.51
  113.6 5.9 %all-to-all-start.3 = ((f32[32,1,512]{2,1,0:T(1,128)}), f32[32,1,512]{2,1,0:T(1,128)S(1)}, u32[]{:S(2)}, u32[]{:S(2)}) async-start(f32[32,1,512]{2,1,0:T(1,128)} %reduce_sum.51), calls=%async_computation.3 | async-start | bytes 131072 | tf_op jit(solution)/shard_map/all_to_all | solution.py:83
  119.5 0.7 reduce_max.31
  120.2 9.3 %all-to-all-done.3 = f32[32,1,512]{2,1,0:T(1,128)S(1)} async-done(((f32[32,1,512]{2,1,0:T(1,128)}), f32[32,1,512]{2,1,0:T(1,128)S(1)}, u32[]{:S(2)}, u32[]{:S(2)}) %all-to-all-start.3) | async-done | bytes 65568 | tf_op jit(solution)/shard_map/all_to_all | solution.py:83
  129.5 3.9 %all-to-all-start.1 = ((f32[32,1,512]{2,1,0:T(1,128)}), f32[32,1,512]{2,1,0:T(1,128)S(1)}, u32[]{:S(2)}, u32[]{:S(2)}) async-start(f32[32,1,512]{2,1,0:T(1,128)} %reduce_max.31), calls=%async_computation.1 | async-start | bytes 131072 | tf_op jit(solution)/shard_map/all_to_all | solution.py:82
  133.3 10.8 %fusion.14 = f32[32,1,512,128]{3,2,1,0:T(8,128)} fusion(f32[32,4,64,512]{3,2,1,0:T(8,128)} %copy-done, f32[32,512]{1,0:T(8,128)S(1)} %get-tuple-element.11, pred[32,4]{1,0:T(8,128)(4,1)S(1)} %copy.23, bf16[32,4,1,64,256]{4,3,1,0,2:T(8,128)(2,1)} %bitcast.59), kind=kOutput, calls=%fused_computation.19 | convolution fusion | flops 1094713344 | bytes 27336704 | tf_op jit(solution)/shard_map/hgrcb,hcgbd->hgrd/dot_general | solution.py:77
  144.1 10.1 %all-to-all-start.2 = ((f32[32,1,512,128]{3,2,1,0:T(8,128)}), f32[32,1,512,128]{3,2,1,0:T(8,128)}, u32[]{:S(2)}, u32[]{:S(2)}) async-start(f32[32,1,512,128]{3,2,1,0:T(8,128)} %fusion.14), calls=%async_computation.2 | async-start | bytes 16777216 | tf_op jit(solution)/shard_map/all_to_all | solution.py:81
  154.4 0.2 fusion.37
  154.8 178.6 %all-to-all-done.2 = f32[32,1,512,128]{3,2,1,0:T(8,128)} async-done(((f32[32,1,512,128]{3,2,1,0:T(8,128)}), f32[32,1,512,128]{3,2,1,0:T(8,128)}, u32[]{:S(2)}, u32[]{:S(2)}) %all-to-all-start.2) | async-done | bytes 8388640 | tf_op jit(solution)/shard_map/all_to_all | solution.py:81
  333.4 5.2 %multiply_reduce_fusion = f32[512,128]{1,0:T(8,128)S(1)} fusion(f32[32,1,512,128]{3,2,1,0:T(8,128)} %all-to-all-done.2, f32[32,512]{1,0:T(8,128)S(1)} %bitcast.61), kind=kLoop, calls=%fused_computation.9 | loop fusion | flops 4128768 | bytes 8716288 | tf_op jit(solution)/shard_map/reduce_sum | solution.py:89
  338.7 0.3 fusion.19
  339.0 5.7 %convolution_convert_fusion = bf16[64,4096]{1,0:T(8,128)(2,1)} fusion(bf16[64,1024]{1,0:T(8,128)(2,1)S(1)} %reshape_transpose_reshape.2, bf16[1024,4096]{1,0:T(8,128)(2,1)} %param.13), kind=kOutput, calls=%fused_computation.16 | convolution fusion | flops 537133056 | bytes 9043968 | tf_op jit(solution)/shard_map/dot_general | solution.py:97
  344.8 29.5 %reduce-scatter.2.cloned.1.call-done = bf16[8,4096]{1,0:T(8,128)(2,1)} async-done(((bf16[64,4096]{1,0:T(8,128)(2,1)}), bf16[8,4096]{1,0:T(8,128)(2,1)}) %reduce-scatter.2.cloned.1.call-update) | async-done | bytes 65552 | tf_op jit(solution)/shard_map/reduce_scatter | solution.py:96
  (31 shorter events, 1.1 us)
Async XLA Ops:
  6.5 87.9 %all-gather.2.cloned.1.call-start = ((), (), s32[]{:S(2)}) async-start(), calls=%async_computation.5 | async-start | bytes 4325376 | tf_op jit(solution)/shard_map/all_gather | solution.py:63
  107.1 5.9 %copy-start = (f32[32,4,64,512]{3,2,1,0:T(8,128)}, f32[32,4,64,512]{3,2,1,0:T(8,128)S(1)}, u32[]{:S(2)}) copy-start(f32[32,4,64,512]{3,2,1,0:T(8,128)S(1)} %get-tuple-element.12) | copy-start | bytes 50331652
  113.6 15.8 %all-to-all-start.3 = ((f32[32,1,512]{2,1,0:T(1,128)}), f32[32,1,512]{2,1,0:T(1,128)S(1)}, u32[]{:S(2)}, u32[]{:S(2)}) async-start(f32[32,1,512]{2,1,0:T(1,128)} %reduce_sum.51), calls=%async_computation.3 | async-start | bytes 131072 | tf_op jit(solution)/shard_map/all_to_all | solution.py:83
  129.5 14.7 %all-to-all-start.1 = ((f32[32,1,512]{2,1,0:T(1,128)}), f32[32,1,512]{2,1,0:T(1,128)S(1)}, u32[]{:S(2)}, u32[]{:S(2)}) async-start(f32[32,1,512]{2,1,0:T(1,128)} %reduce_max.31), calls=%async_computation.1 | async-start | bytes 131072 | tf_op jit(solution)/shard_map/all_to_all | solution.py:82
  144.1 10.1 %copy-start.1 = (bf16[64,1024]{1,0:T(8,128)(2,1)S(1)}, bf16[64,1024]{1,0:T(8,128)(2,1)}, u32[]{:S(2)}) copy-start(bf16[64,1024]{1,0:T(8,128)(2,1)} %param.7) | copy-start | bytes 393220
  144.1 10.2 %copy-start.2 = (bf16[64,1,256]{2,0,1:T(8,128)(2,1)S(1)}, bf16[64,1,256]{2,0,1:T(8,128)(2,1)}, u32[]{:S(2)}) copy-start(bf16[64,1,256]{2,0,1:T(8,128)(2,1)} %param.8) | copy-start | bytes 98308
  144.1 189.3 %all-to-all-start.2 = ((f32[32,1,512,128]{3,2,1,0:T(8,128)}), f32[32,1,512,128]{3,2,1,0:T(8,128)}, u32[]{:S(2)}, u32[]{:S(2)}) async-start(f32[32,1,512,128]{3,2,1,0:T(8,128)} %fusion.14), calls=%async_computation.2 | async-start | bytes 16777216 | tf_op jit(solution)/shard_map/all_to_all | solution.py:81
  154.2 220.1 %reduce-scatter.2.cloned.1.call-start = ((), (), s32[]{:S(2)}) async-start(), calls=%async_computation.6 | async-start | bytes 589824 | tf_op jit(solution)/shard_map/reduce_scatter | solution.py:96
Sparse Core Ops, SparseCore 0:
  9.9 84.4 all-gather.1
  344.9 29.3 reduce-scatter.1
where the time goes:
time: 385 us; the launch traced here: 381 us
  waiting for transfers between devices  276 us (72%)
  matrix products  22.3 us (6%)
  blocking collectives  20.8 us (5%)
  starting transfers between devices  19.8 us (5%)
  local copies, waits for them, and re-layouts  14.3 us (4%)
  between operations  14.2 us (4%)
  other arithmetic  13.2 us (3%)
    all_to_all x1, waiting for transfers between devices, local(): lax.all_to_all(far_acc, 'store', split_axis=0, concat_axis=0, tiled=True)  179 us
    all_gather x1, waiting for transfers between devices, local(): everyone = lax.all_gather(queries, 'store', axis=0, tiled=True)  58.3 us
    reduce_scatter x1, waiting for transfers between devices, local(): lax.psum_scatter(jnp.dot(flattened, out_weight, preferred_element_type=jn...  29.5 us
    all_to_all x1, blocking collectives, local(): lax.all_to_all(wanted, 'store', split_axis=0, concat_axis=0, tiled=True)  20.8 us
    dot_general x1, matrix products, local(): jnp.einsum('hgrcb,hcgbd->hgrd', far_weights, selected[..., HD:], preferre...  10.8 us
    all_to_all x1, starting transfers between devices, local(): lax.all_to_all(far_acc, 'store', split_axis=0, concat_axis=0, tiled=True)  10.1 us
    all_to_all x1, waiting for transfers between devices, local(): lax.all_to_all(far_sum, 'store', split_axis=0, concat_axis=0, tiled=True)  9.3 us
  transfers between devices with their start and end apart: 5, of which 4 were waited for; matrix products, arithmetic and copies ran while one was open for 5% of the time, Pallas kernels for 0%

commit v1 on v0

v1 whole, which is shorter than its diff:
```python
import functools
import math

import jax
import jax.numpy as jnp
from jax import lax
from jax.experimental import pallas as pl
from jax.experimental.pallas import tpu as pltpu
from jax.sharding import PartitionSpec as P

HD = 128
SUF = 64
BLK = 64
CAP = 4
GROUP = 8
ROWS = SUF * GROUP
STATS = 16
PACKET = HD + STATS
NX = 4
NZ = 8
NY = 4
CORES = 2

NEG_FILL = -1e30
FLOOR = -1e9
TO_LOG2 = math.log2(math.e) / math.sqrt(HD)
CHUNKS = ((4, 3, 5), (2, 6), (1, 7), (0,))
VMEM_LIMIT = 32 * 1024 * 1024

CONTRACT_LAST = (((1,), (1,)), ((), ()))
CONTRACT_FIRST = (((0,), (0,)), ((), ()))


def rem(a, n):
    return lax.rem(a + n, n)


def pick_kernel(shifts, place_ref, table_ref, cache_ref, *rest):
    outs, sems = rest[:NX], rest[NX]
    zo, xo = place_ref[0], place_ref[1]
    me = zo * NX + xo
    for k in range(NX):
        xr = rem(xo + k, NX)
        for n, shift in enumerate(shifts):
            home = rem(zo + shift, NZ) * NX + xr
            for c in range(CAP):
                slot = jnp.clip(table_ref[home, me * CAP + c], 0, cache_ref.shape[0] - 1)
                pltpu.make_async_copy(
                    cache_ref.at[pl.ds(slot, 1)],
                    outs[k].at[pl.ds(n * CAP + c, 1)],
                    sems.at[k],
                ).start()
    for k in range(NX):
        pltpu.make_async_copy(cache_ref.at[pl.ds(0, len(shifts) * CAP)], outs[k], sems.at[k]).wait()


def pick(shifts, place, table, cache):
    shape = jax.ShapeDtypeStruct((len(shifts) * CAP, BLK, 2 * HD), cache.dtype)
    return pl.pallas_call(
        functools.partial(pick_kernel, shifts),
        out_shape=[shape] * NX,
        in_specs=[
            pl.BlockSpec(memory_space=pltpu.SMEM),
            pl.BlockSpec(memory_space=pltpu.SMEM),
            pl.BlockSpec(memory_space=pl.ANY),
        ],
        out_specs=[pl.BlockSpec(memory_space=pl.ANY)] * NX,
        scratch_shapes=[pltpu.SemaphoreType.DMA((NX,))],
        compiler_params=pltpu.CompilerParams(vmem_limit_bytes=VMEM_LIMIT),
        name="pick_blocks",
    )(place, table, cache)


def head_rows(block):
    return jnp.concatenate([block[:, i * HD : (i + 1) * HD] for i in range(GROUP)], axis=0)


def partial_packet(score_parts, value_parts):
    peak = functools.reduce(
        jnp.maximum, [jnp.max(part, axis=0, keepdims=True) for part in score_parts]
    )
    shift = jnp.maximum(peak * TO_LOG2, FLOOR).astype(jnp.bfloat16).astype(jnp.float32)
    total = jnp.zeros((1, ROWS), jnp.float32)
    acc = jnp.zeros((HD, ROWS), jnp.float32)
    for part, values in zip(score_parts, value_parts):
        expo = jnp.exp2(part * TO_LOG2 - shift)
        total += jnp.sum(expo, axis=0, keepdims=True)
        acc += lax.dot_general(
            values, expo.astype(jnp.bfloat16), CONTRACT_FIRST, preferred_element_type=jnp.float32
        )
    high = total.astype(jnp.bfloat16).astype(jnp.float32)
    line = lax.broadcasted_iota(jnp.int32, (STATS, ROWS), 0)
    stats = jnp.where(line == 0, shift, jnp.where(line == 1, high, jnp.where(line == 2, total - high, 0.0)))
    return acc.astype(jnp.bfloat16), stats.astype(jnp.bfloat16)


def attend_kernel(shifts, place_ref, table_ref, query_ref, *rest):
    blocks, outs = rest[:NX], rest[NX:]
    zo, xr = place_ref[0], place_ref[1]
    for n, shift in enumerate(shifts):
        zr = rem(zo + shift, NZ)
        rows = head_rows(query_ref[pl.ds(zr * SUF, SUF), :])
        score_parts, value_parts = [], []
        for k in range(NX):
            owner = zo * NX + rem(xr - k, NX)
            both = blocks[k][n * CAP : (n + 1) * CAP].reshape(CAP * BLK, 2 * HD)
            scores = lax.dot_general(
                both[:, :HD], rows, CONTRACT_LAST, preferred_element_type=jnp.float32
            )
            live = [
                jnp.where(
                    table_ref[zr * NX + xr, owner * CAP + c] >= 0,
                    scores[c * BLK : (c + 1) * BLK],
                    NEG_FILL,
                )
                for c in range(CAP)
            ]
            score_parts.append(jnp.concatenate(live, axis=0))
            value_parts.append(both[:, HD:])
        acc, stats = partial_packet(score_parts, value_parts)
        outs[n][:HD, :] = acc
        outs[n][HD:, :] = stats


def attend(shifts, place, table, queries, blocks):
    keys = len(shifts) * NX * CAP * BLK
    return pl.pallas_call(
        functools.partial(attend_kernel, shifts),
        out_shape=[jax.ShapeDtypeStruct((PACKET, ROWS), jnp.bfloat16)] * len(shifts),
        in_specs=[pl.BlockSpec(memory_space=pltpu.SMEM)] * 2
        + [pl.BlockSpec(memory_space=pltpu.VMEM)] * (1 + NX),
        out_specs=[pl.BlockSpec(memory_space=pltpu.VMEM)] * len(shifts),
        compiler_params=pltpu.CompilerParams(vmem_limit_bytes=VMEM_LIMIT),
        cost_estimate=pl.CostEstimate(
            flops=4 * keys * ROWS * HD, bytes_accessed=4 * keys * HD, transcendentals=keys * ROWS
        ),
        name="attend_chunk",
    )(place, table, queries, *blocks)


def own_kernel(query_ref, suffix_ref, out_ref):
    rows = head_rows(query_ref[...])
    both = suffix_ref[...]
    scores = lax.dot_general(both[:, :HD], rows, CONTRACT_LAST, preferred_element_type=jnp.float32)
    key = lax.broadcasted_iota(jnp.int32, (SUF, ROWS), 0)
    token = lax.rem(lax.broadcasted_iota(jnp.int32, (SUF, ROWS), 1), SUF)
    acc, stats = partial_packet([jnp.where(key <= token, scores, NEG_FILL)], [both[:, HD:]])
    out_ref[:HD, :] = acc
    out_ref[HD:, :] = stats


def own_part(queries, suffix):
    return pl.pallas_call(
        own_kernel,
        out_shape=jax.ShapeDtypeStruct((PACKET, ROWS), jnp.bfloat16),
        compiler_params=pltpu.CompilerParams(vmem_limit_bytes=VMEM_LIMIT),
        name="attend_suffix",
    )(queries, suffix)


def project_kernel(*refs):
    packets, weight_ref, out_ref = refs[:-2], refs[-2], refs[-1]
    stats = [ref[HD:, :].astype(jnp.float32) for ref in packets]
    top = functools.reduce(jnp.maximum, [s[0:1] for s in stats])
    factors = [jnp.exp2(s[0:1] - top) for s in stats]
    row_sum = sum(f * (s[1:2] + s[2:3]) for f, s in zip(factors, stats))
    summed = sum(f * ref[:HD, :].astype(jnp.float32) for f, ref in zip(factors, packets))
    rows = (summed / row_sum).T.astype(jnp.bfloat16)
    attended = jnp.concatenate([rows[i * SUF : (i + 1) * SUF] for i in range(GROUP)], axis=1)
    out_ref[...] = jnp.dot(
        attended, weight_ref[...], preferred_element_type=jnp.float32
    ).astype(jnp.bfloat16)


def project(packets, weight):
    return pl.pallas_call(
        project_kernel,
        out_shape=jax.ShapeDtypeStruct((SUF, weight.shape[1]), jnp.bfloat16),
        compiler_params=pltpu.CompilerParams(vmem_limit_bytes=VMEM_LIMIT),
        cost_estimate=pl.CostEstimate(
            flops=2 * SUF * weight.size, bytes_accessed=2 * weight.size, transcendentals=0
        ),
        name="merge_project",
    )(*packets, weight)


def x_permute(a, step):
    pairs = [
        (z * NX + x, z * NX + (x + step) % NX) for z in range(NZ) for x in range(NX)
    ]
    return lax.ppermute(a, "store", pairs)


def z_permute(a, step):
    pairs = [
        (z * NX + x, ((z + step) % NZ) * NX + x) for z in range(NZ) for x in range(NX)
    ]
    return lax.ppermute(a, "store", pairs)


def y_permute(a, step):
    pairs = [
        (y * CORES + c, ((y + step) % NY) * CORES + c) for y in range(NY) for c in range(CORES)
    ]
    return lax.ppermute(a, "head", pairs)


def core_swap(a):
    return lax.ppermute(a, "head", [(h, h ^ 1) for h in range(NY * CORES)])


def sum_heads(partial):
    core = lax.rem(lax.axis_index("head"), CORES)
    y = lax.axis_index("head") // CORES
    parts = partial.reshape(NY, CORES, SUF // (NY * CORES), partial.shape[1])
    pick_core = lambda which: lax.dynamic_index_in_dim(parts, which, 1, keepdims=False)
    other = core_swap(pick_core(1 - core))
    both = pick_core(core).astype(jnp.float32) + other.astype(jnp.float32)
    pick_y = lambda step: lax.dynamic_index_in_dim(both, rem(y + step, NY), 0, keepdims=False)
    arrived = [y_permute(pick_y(step).astype(jnp.bfloat16), step) for step in (2, 1, 3)]
    return (pick_y(0) + sum(a.astype(jnp.float32) for a in arrived)).astype(jnp.bfloat16)


def local(queries, suffix_kv, kv_cache, block_owner, block_slot, prefix_blocks, out_weight):
    store_count = lax.axis_size("store")
    me = lax.axis_index("store")
    place = jnp.stack([me // NX, lax.rem(me, NX)]).astype(jnp.int32)
    owner_list = block_owner[0]
    slot_list = block_slot[0]
    in_prefix = jnp.arange(owner_list.shape[0]) < prefix_blocks[0]
    at_owner = (owner_list[:, None] == jnp.arange(store_count)[None, :]) & in_prefix[:, None]
    ordinal = jnp.cumsum(at_owner.astype(jnp.int32), axis=0) - 1
    placed = at_owner[:, :, None] & (ordinal[:, :, None] == jnp.arange(CAP)[None, None, :])
    wanted = jnp.sum(jnp.where(placed, slot_list[:, None, None] + 1, 0), axis=0) - 1
    copies = jnp.broadcast_to(wanted.reshape(1, -1), (store_count, store_count * CAP))
    table = lax.all_to_all(copies, "store", split_axis=0, concat_axis=0, tiled=True)
    z_groups = [[z * NX + x for z in range(NZ)] for x in range(NX)]
    z_queries = lax.all_gather(queries, "store", axis=0, tiled=True, axis_index_groups=z_groups)
    cache = kv_cache.reshape(kv_cache.shape[0], BLK, 2 * HD)
    own = own_part(queries, suffix_kv.reshape(SUF, 2 * HD))
    packets = []
    for shifts in CHUNKS:
        picked = pick(shifts, place, table, cache)
        blocks = [picked[0]] + [x_permute(picked[k], k) for k in range(1, NX)]
        for shift, packet in zip(shifts, attend(shifts, place, table, z_queries, blocks)):
            packets.append(z_permute(packet, shift) if shift else packet)
    return sum_heads(project(packets + [own], out_weight))


def solution(mesh):
    in_specs = (
        P("store", "head"),
        P("store", "head", None),
        P("store", "head", None, None),
        P("store", None),
        P("store", None),
        P("store"),
        P("head", None),
    )
    out_specs = P(("store", "head"), None)
    return jax.shard_map(local, mesh=mesh, in_specs=in_specs, out_specs=out_specs, check_vma=False)
```

time: 385 us -> 151 us (0.39)
  waiting for transfers between devices: 276 us -> 38.2 us
  Pallas kernels: 0 us -> 24.1 us
  starting transfers between devices: 19.8 us -> 43.6 us
  matrix products: 22.3 us -> 0 us
  blocking collectives: 20.8 us -> 0 us
  local copies, waits for them, and re-layouts: 14.3 us -> 27 us
  other arithmetic: 13.2 us -> 2.55 us
    all_to_all x3 -> x1, waiting for transfers between devices: 188 us -> 9.68 us  [local(): lax.all_to_all(copies, 'store', split_axis=0, concat_axis=0, tiled=True)]
    all_gather x1, waiting for transfers between devices: 58.3 us -> 0.01 us  [local(): lax.all_gather(queries, 'store', axis=0, tiled=True, axis_index_groups=z_...]
    ppermute x0 -> x23, starting transfers between devices: none -> 32.3 us  [the longest x12 15.2 us: x_permute(): return lax.ppermute(a, 'store', pairs)]
    reduce_scatter x1 -> x0, waiting for transfers between devices: 29.5 us -> none  [local(): lax.psum_scatter(jnp.dot(flattened, out_weight, preferred_element_type=jn...]
    ppermute x0 -> x23, waiting for transfers between devices: none -> 27.9 us  [the longest x12 20.6 us: x_permute(): return lax.ppermute(a, 'store', pairs)]
    unnamed x7 -> x56, local copies, waits for them, and re-layouts: 0.02 us -> 26 us
    pallas_call x0 -> x10, Pallas kernels: none -> 24.1 us  [the longest x4 12.2 us: attend(): pl.pallas_call(functools.partial(attend_kernel, shifts), out_shape=[jax.S...]
    dot_general x5 -> x0, matrix products: 22.3 us -> none  [the longest x1 10.8 us: local(): jnp.einsum('hgrcb,hcgbd->hgrd', far_weights, selected[..., HD:], preferre...]
  transfers between devices with their start and end apart: 5 -> 25, of which waited for: 4 -> 6; matrix products, arithmetic and copies ran while one was open for 5% -> 2% of each run, Pallas kernels for 0% -> 15%
where the time goes in v1:
time: 151 us; the launch traced here: 150 us
  starting transfers between devices  43.6 us (29%)
  waiting for transfers between devices  38.2 us (25%)
  local copies, waits for them, and re-layouts  27 us (18%)
  Pallas kernels  24.1 us (16%)
  between operations  14.4 us (10%)
  other arithmetic  2.55 us (2%)
    unnamed x56, local copies, waits for them, and re-layouts  26 us
    ppermute x12, waiting for transfers between devices, x_permute(): return lax.ppermute(a, 'store', pairs)  20.6 us
    ppermute x12, starting transfers between devices, x_permute(): return lax.ppermute(a, 'store', pairs)  15.2 us
    ppermute x7, starting transfers between devices, z_permute(): return lax.ppermute(a, 'store', pairs)  13.4 us
    pallas_call x4, Pallas kernels, attend(): pl.pallas_call(functools.partial(attend_kernel, shifts), out_shape=[jax.S...  12.2 us
    all_to_all x1, starting transfers between devices, local(): lax.all_to_all(copies, 'store', split_axis=0, concat_axis=0, tiled=True)  11.3 us
    pallas_call x4, Pallas kernels, pick(): pl.pallas_call(functools.partial(pick_kernel, shifts), out_shape=[shape]...  9.73 us
    all_to_all x1, waiting for transfers between devices, local(): lax.all_to_all(copies, 'store', split_axis=0, concat_axis=0, tiled=True)  9.68 us
  transfers between devices with their start and end apart: 25, of which 6 were waited for; matrix products, arithmetic and copies ran while one was open for 2% of the time, Pallas kernels for 15%

profile of v1, /device:TPU:24, one launch (start us, length us, event | category | flops | bytes accessed | tf_op | source)
XLA Modules:
  0.0 149.9 jit_solution(3017204736500167749)
XLA Ops:
  10.7 11.3 %all-to-all-start = ((s32[32,1,128]{2,1,0:T(1,128)}), s32[32,1,128]{2,1,0:T(1,128)S(1)}, u32[]{:S(2)}, u32[]{:S(2)}) async-start(s32[32,1,128]{2,1,0:T(1,128)} %broadcast_in_dim.24), calls=%async_computation | async-start | bytes 32768 | tf_op jit(solution)/shard_map/all_to_all | solution.py:236
  22.1 9.7 %all-to-all-done = s32[32,1,128]{2,1,0:T(1,128)S(1)} async-done(((s32[32,1,128]{2,1,0:T(1,128)}), s32[32,1,128]{2,1,0:T(1,128)S(1)}, u32[]{:S(2)}, u32[]{:S(2)}) %all-to-all-start) | async-done | bytes 16416 | tf_op jit(solution)/shard_map/all_to_all | solution.py:236
  31.8 2.2 %copy-done = bf16[128,1,64,256]{3,2,1,0:T(8,128)(2,1)S(1)} copy-done((bf16[128,1,64,256]{3,2,1,0:T(8,128)(2,1)S(1)}, bf16[128,1,64,256]{3,2,1,0:T(8,128)(2,1)}, u32[]{:S(2)}) %copy-start) | copy-done | bytes 4194328
  34.0 3.5 %pick_blocks.4 = (bf16[12,64,256]{2,1,0:T(8,128)(2,1)S(1)}, bf16[12,64,256]{2,1,0:T(8,128)(2,1)S(1)}, bf16[12,64,256]{2,1,0:T(8,128)(2,1)S(1)}, bf16[12,64,256]{2,1,0:T(8,128)(2,1)S(1)}) custom-call(s32[2]{0:T(128)S(1)} %pad_add_fusion.place_ref, s32[32,128]{1,0:T(8,128)S(1)} %bitcast.34, bf16[128,64,256]{2,1,0:T(8,128)(2,1)S(1)} %bitcast.28), custom_call_target="tpu_custom_call" | custom-call | tf_op jit(solution)/shard_map/pick_blocks/pallas_call | solution.py:59
  38.8 2.1 %collective-permute-start.1 = (bf16[12,64,256]{2,1,0:T(8,128)(2,1)S(1)}, bf16[12,64,256]{2,1,0:T(8,128)(2,1)S(1)}, u32[]{:S(2)}, u32[]{:S(2)}) collective-permute-start(bf16[12,64,256]{2,1,0:T(8,128)(2,1)S(1)} %get-tuple-element.30), channel_id=1, source_target_pairs={{0,16},{8,24},{16,0},{24,8},{32,48},{40,56},{48,32},{56,40},{64,80... | collective-permute-start | bytes 1179656 | tf_op jit(solution)/shard_map/ppermute | solution.py:191
  42.0 2.5 %pick_blocks.5 = (bf16[8,64,256]{2,1,0:T(8,128)(2,1)S(1)}, bf16[8,64,256]{2,1,0:T(8,128)(2,1)S(1)}, bf16[8,64,256]{2,1,0:T(8,128)(2,1)}, bf16[8,64,256]{2,1,0:T(8,128)(2,1)}) custom-call(s32[2]{0:T(128)S(1)} %pad_add_fusion.place_ref, s32[32,128]{1,0:T(8,128)S(1)} %bitcast.35, bf16[128,64,256]{2,1,0:T(8,128)(2,1)S(1)} %bitcast.29), custom_call_target="tpu_custom_call" | custom-call | tf_op jit(solution)/shard_map/pick_blocks/pallas_call | solution.py:59
  47.1 20.6 %collective-permute-done.6.rest_1_ = bf16[8,64,256]{2,1,0:T(8,128)(2,1)S(1)} collective-permute-done((bf16[8,64,256]{2,1,0:T(8,128)(2,1)S(1)}, bf16[8,64,256]{2,1,0:T(8,128)(2,1)S(1)}, u32[]{:S(2)}, u32[]{:S(2)}) %collective-permute-start.6) | collective-permute-done | bytes 262176 | tf_op jit(solution)/shard_map/ppermute | solution.py:191
  67.7 2.2 %pick_blocks.6 = (bf16[8,64,256]{2,1,0:T(8,128)(2,1)S(1)}, bf16[8,64,256]{2,1,0:T(8,128)(2,1)}, bf16[8,64,256]{2,1,0:T(8,128)(2,1)}, bf16[8,64,256]{2,1,0:T(8,128)(2,1)}) custom-call(s32[2]{0:T(128)S(1)} %pad_add_fusion.place_ref, s32[32,128]{1,0:T(8,128)S(1)} %bitcast.36, bf16[128,64,256]{2,1,0:T(8,128)(2,1)S(1)} %bitcast.30), custom_call_target="tpu_custom_call" | custom-call | tf_op jit(solution)/shard_map/pick_blocks/pallas_call | solution.py:59
  70.6 2.0 %collective-permute-start.11 = (bf16[8,64,256]{2,1,0:T(8,128)(2,1)}, bf16[8,64,256]{2,1,0:T(8,128)(2,1)S(1)}, u32[]{:S(2)}, u32[]{:S(2)}) collective-permute-start(bf16[8,64,256]{2,1,0:T(8,128)(2,1)} %get-tuple-element.42), channel_id=1, source_target_pairs={{0,8},{8,16},{16,24},{24,0},{32,40},{40,48},{48,56},{56,32},{64,72... | collective-permute-start | bytes 786440 | tf_op jit(solution)/shard_map/ppermute | solution.py:191
  74.2 2.7 %collective-permute-start.13 = (bf16[8,64,256]{2,1,0:T(8,128)(2,1)}, bf16[8,64,256]{2,1,0:T(8,128)(2,1)S(1)}, u32[]{:S(2)}, u32[]{:S(2)}) collective-permute-start(bf16[8,64,256]{2,1,0:T(8,128)(2,1)} %get-tuple-element.44), channel_id=1, source_target_pairs={{0,24},{8,0},{16,8},{24,16},{32,56},{40,32},{48,40},{56,48},{64,88... | collective-permute-start | bytes 786440 | tf_op jit(solution)/shard_map/ppermute | solution.py:191
  82.1 4.2 %attend_chunk.4 = (bf16[144,512]{1,0:T(8,128)(2,1)S(1)}, bf16[144,512]{1,0:T(8,128)(2,1)S(1)}, bf16[144,512]{1,0:T(8,128)(2,1)}) custom-call(s32[2]{0:T(128)S(1)} %pad_add_fusion.place_ref, s32[32,128]{1,0:T(8,128)S(1)} %bitcast.37, bf16[512,1024]{1,0:T(8,128)(2,1)S(1)} %copy-done.2, bf16[12,64,256]{2,1,0:T(8,128)(2,1)S(1)} %copy-done.21, ...), custom_call_target="tpu_custom_call" | custom-call | flops 805306368 | bytes 1572864 | tf_op jit(solution)/shard_map/attend_chunk/pallas_call | solution.py:127
  87.3 3.2 %collective-permute-start.4 = (bf16[144,512]{1,0:T(8,128)(2,1)S(1)}, bf16[144,512]{1,0:T(8,128)(2,1)S(1)}, u32[]{:S(2)}, u32[]{:S(2)}) collective-permute-start(bf16[144,512]{1,0:T(8,128)(2,1)S(1)} %get-tuple-element.33), channel_id=1, source_target_pairs={{0,96},{8,104},{16,112},{24,120},{32,128},{40,136},{48,144},{56,15... | collective-permute-start | bytes 442376 | tf_op jit(solution)/shard_map/ppermute | solution.py:198
  90.5 2.2 %copy-done.1 = bf16[128,1,64,256]{3,2,1,0:T(8,128)(2,1)S(1)} copy-done((bf16[128,1,64,256]{3,2,1,0:T(8,128)(2,1)S(1)}, bf16[128,1,64,256]{3,2,1,0:T(8,128)(2,1)}, u32[]{:S(2)}) %copy-start.1) | copy-done | bytes 4194328
  94.5 2.9 %collective-permute-start.17 = (bf16[4,64,256]{2,1,0:T(8,128)(2,1)S(1)}, bf16[4,64,256]{2,1,0:T(8,128)(2,1)S(1)}, u32[]{:S(2)}, u32[]{:S(2)}) collective-permute-start(bf16[4,64,256]{2,1,0:T(8,128)(2,1)S(1)} %get-tuple-element.49), channel_id=1, source_target_pairs={{0,16},{8,24},{16,0},{24,8},{32,48},{40,56},{48,32},{56,40},{64,80... | collective-permute-start | bytes 393224 | tf_op jit(solution)/shard_map/ppermute | solution.py:191
  99.8 3.4 %attend_chunk.5 = (bf16[144,512]{1,0:T(8,128)(2,1)}, bf16[144,512]{1,0:T(8,128)(2,1)}) custom-call(s32[2]{0:T(128)S(1)} %pad_add_fusion.place_ref, s32[32,128]{1,0:T(8,128)S(1)} %bitcast.39, bf16[512,1024]{1,0:T(8,128)(2,1)S(1)} %copy-done.3, bf16[8,64,256]{2,1,0:T(8,128)(2,1)S(1)} %get-tuple-element.35.rest_0_, ...), custom_call_target="tpu_custom_call" | custom-call | flops 536870912 | bytes 1048576 | tf_op jit(solution)/shard_map/attend_chunk/pallas_call | solution.py:127
  103.2 2.7 %attend_chunk.6 = (bf16[144,512]{1,0:T(8,128)(2,1)S(1)}, bf16[144,512]{1,0:T(8,128)(2,1)S(1)}) custom-call(s32[2]{0:T(128)S(1)} %pad_add_fusion.place_ref, s32[32,128]{1,0:T(8,128)S(1)} %bitcast.40, bf16[512,1024]{1,0:T(8,128)(2,1)S(1)} %copy-done.3, bf16[8,64,256]{2,1,0:T(8,128)(2,1)S(1)} %get-tuple-element.41.rest_0_, ...), custom_call_target="tpu_custom_call" | custom-call | flops 536870912 | bytes 1048576 | tf_op jit(solution)/shard_map/attend_chunk/pallas_call | solution.py:127
  109.0 2.2 %collective-permute-start.9 = (bf16[144,512]{1,0:T(8,128)(2,1)}, bf16[144,512]{1,0:T(8,128)(2,1)S(1)}, u32[]{:S(2)}, u32[]{:S(2)}) collective-permute-start(bf16[144,512]{1,0:T(8,128)(2,1)} %get-tuple-element.39), channel_id=1, source_target_pairs={{0,64},{8,72},{16,80},{24,88},{32,96},{40,104},{48,112},{56,120},{... | collective-permute-start | bytes 442376 | tf_op jit(solution)/shard_map/ppermute | solution.py:198
  111.9 2.0 %collective-permute-start.10 = (bf16[144,512]{1,0:T(8,128)(2,1)}, bf16[144,512]{1,0:T(8,128)(2,1)S(1)}, u32[]{:S(2)}, u32[]{:S(2)}) collective-permute-start(bf16[144,512]{1,0:T(8,128)(2,1)} %get-tuple-element.40), channel_id=1, source_target_pairs={{0,192},{8,200},{16,208},{24,216},{32,224},{40,232},{48,240},{56,2... | collective-permute-start | bytes 442376 | tf_op jit(solution)/shard_map/ppermute | solution.py:198
  116.5 1.8 %collective-permute-start.15 = (bf16[144,512]{1,0:T(8,128)(2,1)S(1)}, bf16[144,512]{1,0:T(8,128)(2,1)S(1)}, u32[]{:S(2)}, u32[]{:S(2)}) collective-permute-start(bf16[144,512]{1,0:T(8,128)(2,1)S(1)} %get-tuple-element.46), channel_id=1, source_target_pairs={{0,224},{8,232},{16,240},{24,248},{32,0},{40,8},{48,16},{56,24},{6... | collective-permute-start | bytes 442376 | tf_op jit(solution)/shard_map/ppermute | solution.py:198
  122.4 1.9 %attend_chunk.7.refs_7_ = bf16[144,512]{1,0:T(8,128)(2,1)S(1)} custom-call(s32[2]{0:T(128)S(1)} %pad_add_fusion.place_ref, s32[32,128]{1,0:T(8,128)S(1)} %bitcast.41, bf16[512,1024]{1,0:T(8,128)(2,1)S(1)} %copy-done.4, bf16[4,64,256]{2,1,0:T(8,128)(2,1)S(1)} %copy-done.12, bf16[4,64,256]{2,1,0:T(8,128)(2,1)S(1)} %copy-done.14, ...), custom_call_target="tpu_custom_call" | custom-call | flops 268435456 | bytes 524288 | tf_op jit(solution)/shard_map/attend_chunk/pallas_call | solution.py:127
  124.3 3.4 %copy-done.5 = bf16[1024,4096]{1,0:T(8,128)(2,1)S(1)} copy-done((bf16[1024,4096]{1,0:T(8,128)(2,1)S(1)}, bf16[1024,4096]{1,0:T(8,128)(2,1)}, u32[]{:S(2)}) %copy-start.5) | copy-done | bytes 8388632
  134.1 2.5 %collective-permute-start.21 = (bf16[8,4096]{1,0:T(8,128)(2,1)S(1)}, bf16[8,4096]{1,0:T(8,128)(2,1)S(1)}, u32[]{:S(2)}, u32[]{:S(2)}) collective-permute-start(bf16[8,4096]{1,0:T(8,128)(2,1)S(1)} %get-tuple-element.53), channel_id=1, source_target_pairs={{0,2},{1,3},{2,4},{3,5},{4,6},{5,7},{6,0},{7,1},{8,10},{9,11},{10,... | collective-permute-start | bytes 196616 | tf_op jit(solution)/shard_map/ppermute | solution.py:205
  136.7 2.2 %collective-permute-done.22 = bf16[8,4096]{1,0:T(8,128)(2,1)S(1)} collective-permute-done((bf16[8,4096]{1,0:T(8,128)(2,1)S(1)}, bf16[8,4096]{1,0:T(8,128)(2,1)S(1)}, u32[]{:S(2)}, u32[]{:S(2)}) %collective-permute-start.22) | collective-permute-done | bytes 65568 | tf_op jit(solution)/shard_map/ppermute | solution.py:205
  139.4 3.0 %collective-permute-done.20 = bf16[8,4096]{1,0:T(8,128)(2,1)S(1)} collective-permute-done((bf16[8,4096]{1,0:T(8,128)(2,1)S(1)}, bf16[8,4096]{1,0:T(8,128)(2,1)S(1)}, u32[]{:S(2)}, u32[]{:S(2)}) %collective-permute-start.20) | collective-permute-done | bytes 65568 | tf_op jit(solution)/shard_map/ppermute | solution.py:205
  (110 shorter events, 39.4 us)
Async XLA Ops:
  6.5 70.3 %all-gather.2.cloned.1.call-start = ((), (), s32[]{:S(2)}) async-start(), calls=%async_computation.1 | async-start | bytes 1179648 | tf_op jit(solution)/shard_map/all_gather | solution.py:238
  10.7 21.1 %all-to-all-start = ((s32[32,1,128]{2,1,0:T(1,128)}), s32[32,1,128]{2,1,0:T(1,128)S(1)}, u32[]{:S(2)}, u32[]{:S(2)}) async-start(s32[32,1,128]{2,1,0:T(1,128)} %broadcast_in_dim.24), calls=%async_computation | async-start | bytes 32768 | tf_op jit(solution)/shard_map/all_to_all | solution.py:236
  38.2 31.6 %collective-permute-start = (bf16[12,64,256]{2,1,0:T(8,128)(2,1)S(1)}, bf16[12,64,256]{2,1,0:T(8,128)(2,1)S(1)}, u32[]{:S(2)}, u32[]{:S(2)}) collective-permute-start(bf16[12,64,256]{2,1,0:T(8,128)(2,1)S(1)} %get-tuple-element.29), channel_id=1, source_target_pairs={{0,8},{8,16},{16,24},{24,0},{32,40},{40,48},{48,56},{56,32},{64,72... | collective-permute-start | bytes 1179656 | tf_op jit(solution)/shard_map/ppermute | solution.py:191
  38.8 33.8 %collective-permute-start.1 = (bf16[12,64,256]{2,1,0:T(8,128)(2,1)S(1)}, bf16[12,64,256]{2,1,0:T(8,128)(2,1)S(1)}, u32[]{:S(2)}, u32[]{:S(2)}) collective-permute-start(bf16[12,64,256]{2,1,0:T(8,128)(2,1)S(1)} %get-tuple-element.30), channel_id=1, source_target_pairs={{0,16},{8,24},{16,0},{24,8},{32,48},{40,56},{48,32},{56,40},{64,80... | collective-permute-start | bytes 1179656 | tf_op jit(solution)/shard_map/ppermute | solution.py:191
  40.9 32.5 %collective-permute-start.2 = (bf16[12,64,256]{2,1,0:T(8,128)(2,1)S(1)}, bf16[12,64,256]{2,1,0:T(8,128)(2,1)S(1)}, u32[]{:S(2)}, u32[]{:S(2)}) collective-permute-start(bf16[12,64,256]{2,1,0:T(8,128)(2,1)S(1)} %get-tuple-element.31), channel_id=1, source_target_pairs={{0,24},{8,0},{16,8},{24,16},{32,56},{40,32},{48,40},{56,48},{64,88... | collective-permute-start | bytes 1179656 | tf_op jit(solution)/shard_map/ppermute | solution.py:191
  44.5 23.1 %collective-permute-start.6 = (bf16[8,64,256]{2,1,0:T(8,128)(2,1)S(1)}, bf16[8,64,256]{2,1,0:T(8,128)(2,1)S(1)}, u32[]{:S(2)}, u32[]{:S(2)}) collective-permute-start(bf16[8,64,256]{2,1,0:T(8,128)(2,1)S(1)} %get-tuple-element.36), channel_id=1, source_target_pairs={{0,8},{8,16},{16,24},{24,0},{32,40},{40,48},{48,56},{56,32},{64,72... | collective-permute-start | bytes 786440 | tf_op jit(solution)/shard_map/ppermute | solution.py:191
  45.5 40.8 %collective-permute-start.7 = (bf16[8,64,256]{2,1,0:T(8,128)(2,1)}, bf16[8,64,256]{2,1,0:T(8,128)(2,1)S(1)}, u32[]{:S(2)}, u32[]{:S(2)}) collective-permute-start(bf16[8,64,256]{2,1,0:T(8,128)(2,1)} %get-tuple-element.37), channel_id=1, source_target_pairs={{0,16},{8,24},{16,0},{24,8},{32,48},{40,56},{48,32},{56,40},{64,80... | collective-permute-start | bytes 786440 | tf_op jit(solution)/shard_map/ppermute | solution.py:191
  67.7 19.7 %collective-permute-start.8 = (bf16[8,64,256]{2,1,0:T(8,128)(2,1)}, bf16[8,64,256]{2,1,0:T(8,128)(2,1)S(1)}, u32[]{:S(2)}, u32[]{:S(2)}) collective-permute-start(bf16[8,64,256]{2,1,0:T(8,128)(2,1)} %get-tuple-element.38), channel_id=1, source_target_pairs={{0,24},{8,0},{16,8},{24,16},{32,56},{40,32},{48,40},{56,48},{64,88... | collective-permute-start | bytes 786440 | tf_op jit(solution)/shard_map/ppermute | solution.py:191
  70.6 23.8 %collective-permute-start.11 = (bf16[8,64,256]{2,1,0:T(8,128)(2,1)}, bf16[8,64,256]{2,1,0:T(8,128)(2,1)S(1)}, u32[]{:S(2)}, u32[]{:S(2)}) collective-permute-start(bf16[8,64,256]{2,1,0:T(8,128)(2,1)} %get-tuple-element.42), channel_id=1, source_target_pairs={{0,8},{8,16},{16,24},{24,0},{32,40},{40,48},{48,56},{56,32},{64,72... | collective-permute-start | bytes 786440 | tf_op jit(solution)/shard_map/ppermute | solution.py:191
  73.4 21.1 %collective-permute-start.12 = (bf16[8,64,256]{2,1,0:T(8,128)(2,1)}, bf16[8,64,256]{2,1,0:T(8,128)(2,1)S(1)}, u32[]{:S(2)}, u32[]{:S(2)}) collective-permute-start(bf16[8,64,256]{2,1,0:T(8,128)(2,1)} %get-tuple-element.43), channel_id=1, source_target_pairs={{0,16},{8,24},{16,0},{24,8},{32,48},{40,56},{48,32},{56,40},{64,80... | collective-permute-start | bytes 786440 | tf_op jit(solution)/shard_map/ppermute | solution.py:191
  74.2 23.2 %collective-permute-start.13 = (bf16[8,64,256]{2,1,0:T(8,128)(2,1)}, bf16[8,64,256]{2,1,0:T(8,128)(2,1)S(1)}, u32[]{:S(2)}, u32[]{:S(2)}) collective-permute-start(bf16[8,64,256]{2,1,0:T(8,128)(2,1)} %get-tuple-element.44), channel_id=1, source_target_pairs={{0,24},{8,0},{16,8},{24,16},{32,56},{40,32},{48,40},{56,48},{64,88... | collective-permute-start | bytes 786440 | tf_op jit(solution)/shard_map/ppermute | solution.py:191
  86.3 27.5 %collective-permute-start.3 = (bf16[144,512]{1,0:T(8,128)(2,1)S(1)}, bf16[144,512]{1,0:T(8,128)(2,1)S(1)}, u32[]{:S(2)}, u32[]{:S(2)}) collective-permute-start(bf16[144,512]{1,0:T(8,128)(2,1)S(1)} %get-tuple-element.32), channel_id=1, source_target_pairs={{0,128},{8,136},{16,144},{24,152},{32,160},{40,168},{48,176},{56,1... | collective-permute-start | bytes 442376 | tf_op jit(solution)/shard_map/ppermute | solution.py:198
  87.3 28.6 %collective-permute-start.4 = (bf16[144,512]{1,0:T(8,128)(2,1)S(1)}, bf16[144,512]{1,0:T(8,128)(2,1)S(1)}, u32[]{:S(2)}, u32[]{:S(2)}) collective-permute-start(bf16[144,512]{1,0:T(8,128)(2,1)S(1)} %get-tuple-element.33), channel_id=1, source_target_pairs={{0,96},{8,104},{16,112},{24,120},{32,128},{40,136},{48,144},{56,15... | collective-permute-start | bytes 442376 | tf_op jit(solution)/shard_map/ppermute | solution.py:198
  94.4 11.5 %collective-permute-start.16 = (bf16[4,64,256]{2,1,0:T(8,128)(2,1)S(1)}, bf16[4,64,256]{2,1,0:T(8,128)(2,1)S(1)}, u32[]{:S(2)}, u32[]{:S(2)}) collective-permute-start(bf16[4,64,256]{2,1,0:T(8,128)(2,1)S(1)} %get-tuple-element.48), channel_id=1, source_target_pairs={{0,8},{8,16},{16,24},{24,0},{32,40},{40,48},{48,56},{56,32},{64,72... | collective-permute-start | bytes 393224 | tf_op jit(solution)/shard_map/ppermute | solution.py:191
  94.5 13.9 %collective-permute-start.17 = (bf16[4,64,256]{2,1,0:T(8,128)(2,1)S(1)}, bf16[4,64,256]{2,1,0:T(8,128)(2,1)S(1)}, u32[]{:S(2)}, u32[]{:S(2)}) collective-permute-start(bf16[4,64,256]{2,1,0:T(8,128)(2,1)S(1)} %get-tuple-element.49), channel_id=1, source_target_pairs={{0,16},{8,24},{16,0},{24,8},{32,48},{40,56},{48,32},{56,40},{64,80... | collective-permute-start | bytes 393224 | tf_op jit(solution)/shard_map/ppermute | solution.py:191
  97.4 13.8 %collective-permute-start.18 = (bf16[4,64,256]{2,1,0:T(8,128)(2,1)S(1)}, bf16[4,64,256]{2,1,0:T(8,128)(2,1)S(1)}, u32[]{:S(2)}, u32[]{:S(2)}) collective-permute-start(bf16[4,64,256]{2,1,0:T(8,128)(2,1)S(1)} %get-tuple-element.50), channel_id=1, source_target_pairs={{0,24},{8,0},{16,8},{24,16},{32,56},{40,32},{48,40},{56,48},{64,88... | collective-permute-start | bytes 393224 | tf_op jit(solution)/shard_map/ppermute | solution.py:191
  106.5 17.7 %collective-permute-start.5 = (bf16[144,512]{1,0:T(8,128)(2,1)}, bf16[144,512]{1,0:T(8,128)(2,1)S(1)}, u32[]{:S(2)}, u32[]{:S(2)}) collective-permute-start(bf16[144,512]{1,0:T(8,128)(2,1)} %get-tuple-element.34), channel_id=1, source_target_pairs={{0,160},{8,168},{16,176},{24,184},{32,192},{40,200},{48,208},{56,2... | collective-permute-start | bytes 442376 | tf_op jit(solution)/shard_map/ppermute | solution.py:198
  109.0 15.2 %collective-permute-start.9 = (bf16[144,512]{1,0:T(8,128)(2,1)}, bf16[144,512]{1,0:T(8,128)(2,1)S(1)}, u32[]{:S(2)}, u32[]{:S(2)}) collective-permute-start(bf16[144,512]{1,0:T(8,128)(2,1)} %get-tuple-element.39), channel_id=1, source_target_pairs={{0,64},{8,72},{16,80},{24,88},{32,96},{40,104},{48,112},{56,120},{... | collective-permute-start | bytes 442376 | tf_op jit(solution)/shard_map/ppermute | solution.py:198
  111.9 12.4 %collective-permute-start.10 = (bf16[144,512]{1,0:T(8,128)(2,1)}, bf16[144,512]{1,0:T(8,128)(2,1)S(1)}, u32[]{:S(2)}, u32[]{:S(2)}) collective-permute-start(bf16[144,512]{1,0:T(8,128)(2,1)} %get-tuple-element.40), channel_id=1, source_target_pairs={{0,192},{8,200},{16,208},{24,216},{32,224},{40,232},{48,240},{56,2... | collective-permute-start | bytes 442376 | tf_op jit(solution)/shard_map/ppermute | solution.py:198
  114.5 9.8 %collective-permute-start.14 = (bf16[144,512]{1,0:T(8,128)(2,1)S(1)}, bf16[144,512]{1,0:T(8,128)(2,1)S(1)}, u32[]{:S(2)}, u32[]{:S(2)}) collective-permute-start(bf16[144,512]{1,0:T(8,128)(2,1)S(1)} %get-tuple-element.45), channel_id=1, source_target_pairs={{0,32},{8,40},{16,48},{24,56},{32,64},{40,72},{48,80},{56,88},{64,... | collective-permute-start | bytes 442376 | tf_op jit(solution)/shard_map/ppermute | solution.py:198
  116.5 7.8 %collective-permute-start.15 = (bf16[144,512]{1,0:T(8,128)(2,1)S(1)}, bf16[144,512]{1,0:T(8,128)(2,1)S(1)}, u32[]{:S(2)}, u32[]{:S(2)}) collective-permute-start(bf16[144,512]{1,0:T(8,128)(2,1)S(1)} %get-tuple-element.46), channel_id=1, source_target_pairs={{0,224},{8,232},{16,240},{24,248},{32,0},{40,8},{48,16},{56,24},{6... | collective-permute-start | bytes 442376 | tf_op jit(solution)/shard_map/ppermute | solution.py:198
  133.3 5.6 %collective-permute-start.22 = (bf16[8,4096]{1,0:T(8,128)(2,1)S(1)}, bf16[8,4096]{1,0:T(8,128)(2,1)S(1)}, u32[]{:S(2)}, u32[]{:S(2)}) collective-permute-start(bf16[8,4096]{1,0:T(8,128)(2,1)S(1)} %get-tuple-element.52), channel_id=1, source_target_pairs={{0,6},{1,7},{2,0},{3,1},{4,2},{5,3},{6,4},{7,5},{8,14},{9,15},{10,... | collective-permute-start | bytes 196616 | tf_op jit(solution)/shard_map/ppermute | solution.py:205
  134.1 5.3 %collective-permute-start.21 = (bf16[8,4096]{1,0:T(8,128)(2,1)S(1)}, bf16[8,4096]{1,0:T(8,128)(2,1)S(1)}, u32[]{:S(2)}, u32[]{:S(2)}) collective-permute-start(bf16[8,4096]{1,0:T(8,128)(2,1)S(1)} %get-tuple-element.53), channel_id=1, source_target_pairs={{0,2},{1,3},{2,4},{3,5},{4,6},{5,7},{6,0},{7,1},{8,10},{9,11},{10,... | collective-permute-start | bytes 196616 | tf_op jit(solution)/shard_map/ppermute | solution.py:205
  136.6 5.8 %collective-permute-start.20 = (bf16[8,4096]{1,0:T(8,128)(2,1)S(1)}, bf16[8,4096]{1,0:T(8,128)(2,1)S(1)}, u32[]{:S(2)}, u32[]{:S(2)}) collective-permute-start(bf16[8,4096]{1,0:T(8,128)(2,1)S(1)} %get-tuple-element.51), channel_id=1, source_target_pairs={{0,4},{1,5},{2,6},{3,7},{4,0},{5,1},{6,2},{7,3},{8,12},{9,13},{10,... | collective-permute-start | bytes 196616 | tf_op jit(solution)/shard_map/ppermute | solution.py:205
  (29 other events, 233.8 us)
Sparse Core Ops, SparseCore 0:
  9.1 41.3 all-gather.1

commit v2 on v1

v2 whole, which is shorter than its diff:
```python
import functools
import math

import jax
import jax.numpy as jnp
from jax import lax
from jax.experimental import pallas as pl
from jax.experimental.pallas import tpu as pltpu
from jax.sharding import PartitionSpec as P

HD = 128
SUF = 64
BLK = 64
CAP = 4
GROUP = 8
ROWS = SUF * GROUP
STATS = 16
PACKET = HD + STATS
NX = 4
NZ = 8
NY = 4
CORES = 2
HEAD_ROWS = SUF // (NY * CORES)

NEG_FILL = -1e30
FLOOR = -1e9
TO_LOG2 = math.log2(math.e) / math.sqrt(HD)
CHUNKS = ((4, 3, 5, 2), (6, 7, 1), (0,))
AHEAD = 2
VMEM_LIMIT = 40 * 1024 * 1024

CONTRACT_LAST = (((1,), (1,)), ((), ()))
CONTRACT_FIRST = (((0,), (0,)), ((), ()))

IN_SMEM = pl.BlockSpec(memory_space=pltpu.SMEM)
IN_VMEM = pl.BlockSpec(memory_space=pltpu.VMEM)
IN_HBM = pl.BlockSpec(memory_space=pltpu.HBM)


def keep_in_hbm(a):
    return pltpu.with_memory_space_constraint(a, pltpu.HBM)


def rem(a, n):
    return lax.rem(a + n, n)


def coordinates(me_ref):
    return lax.div(me_ref[0], NX), lax.rem(me_ref[0], NX)


def wanted_kernel(length_ref, owner_ref, slot_ref, out_ref):
    count = owner_ref.shape[1]
    owners = count // CAP
    entry = lax.broadcasted_iota(jnp.int32, (1, count), 1)
    owner = jnp.where(entry < length_ref[0], owner_ref[...], owners)
    at_owner = lax.broadcasted_iota(jnp.int32, (owners, count), 0) == owner
    hits = jnp.where(at_owner, 1.0, 0.0)
    earlier = lax.broadcasted_iota(jnp.int32, (count, count), 0) < lax.broadcasted_iota(
        jnp.int32, (count, count), 1
    )
    before = jnp.dot(
        hits.astype(jnp.bfloat16),
        jnp.where(earlier, 1.0, 0.0).astype(jnp.bfloat16),
        preferred_element_type=jnp.float32,
    )
    ordinal = jnp.sum(before * hits, axis=0, keepdims=True).astype(jnp.int32)
    target = jnp.where(ordinal < CAP, owner * CAP + ordinal, count)
    chosen = jnp.where(lax.broadcasted_iota(jnp.int32, (count, count), 0) == target, 1.0, 0.0)
    slots = jnp.broadcast_to((slot_ref[...] + 1).astype(jnp.float32), (8, count))
    row = lax.dot_general(
        slots.astype(jnp.bfloat16),
        chosen.astype(jnp.bfloat16),
        CONTRACT_LAST,
        preferred_element_type=jnp.float32,
    )
    out_ref[...] = jnp.broadcast_to(
        (row[0:1].astype(jnp.int32) - 1).reshape(1, 1, count), out_ref.shape
    )


def wanted_slots(prefix_blocks, block_owner, block_slot, store_count):
    return pl.pallas_call(
        wanted_kernel,
        out_shape=jax.ShapeDtypeStruct((store_count, 1, block_owner.shape[1]), jnp.int32),
        in_specs=[IN_SMEM, IN_VMEM, IN_VMEM],
        out_specs=IN_VMEM,
        compiler_params=pltpu.CompilerParams(vmem_limit_bytes=VMEM_LIMIT),
        name="wanted_slots",
    )(prefix_blocks, block_owner, block_slot)


def slot_of(table_ref, home, owner, c, cache_ref):
    return jnp.clip(table_ref[home, 0, owner * CAP + c], 0, cache_ref.shape[0] - 1)


def start_picks(shifts, me_ref, table_ref, cache_ref, outs, sems):
    zo, xo = coordinates(me_ref)
    for k in range(1, NX):
        for n, shift in enumerate(shifts):
            home = rem(zo + shift, NZ) * NX + rem(xo + k, NX)
            for c in range(CAP):
                slot = slot_of(table_ref, home, me_ref[0], c, cache_ref)
                pltpu.make_async_copy(
                    cache_ref.at[pl.ds(slot, 1)],
                    outs[k - 1].at[pl.ds(n * CAP + c, 1)],
                    sems.at[k - 1],
                ).start()


def wait_picks(shifts, cache_ref, outs, sems):
    for k in range(1, NX):
        pltpu.make_async_copy(
            cache_ref.at[pl.ds(0, len(shifts) * CAP)], outs[k - 1], sems.at[k - 1]
        ).wait()


def start_own_blocks(shifts, me_ref, table_ref, cache_ref, here_ref, sem):
    zo, xo = coordinates(me_ref)
    for n, shift in enumerate(shifts):
        for c in range(CAP):
            slot = slot_of(table_ref, rem(zo + shift, NZ) * NX + xo, me_ref[0], c, cache_ref)
            pltpu.make_async_copy(
                cache_ref.at[pl.ds(slot, 1)], here_ref.at[pl.ds(n * CAP + c, 1)], sem
            ).start()


def wait_own_blocks(shifts, cache_ref, here_ref, sem):
    pltpu.make_async_copy(cache_ref.at[pl.ds(0, len(shifts) * CAP)], here_ref, sem).wait()


def picked_shapes(shifts, dtype):
    return [jax.ShapeDtypeStruct((len(shifts) * CAP, BLK, 2 * HD), dtype)] * (NX - 1)


def pick_kernel(shifts, me_ref, table_ref, cache_ref, *rest):
    outs, sems = rest[:-1], rest[-1]
    start_picks(shifts, me_ref, table_ref, cache_ref, outs, sems)
    wait_picks(shifts, cache_ref, outs, sems)


def pick(shifts, me, table, cache):
    shapes = picked_shapes(shifts, cache.dtype)
    return pl.pallas_call(
        functools.partial(pick_kernel, shifts),
        out_shape=shapes,
        in_specs=[IN_SMEM, IN_SMEM, IN_HBM],
        out_specs=[IN_HBM] * len(shapes),
        scratch_shapes=[pltpu.SemaphoreType.DMA((NX - 1,))],
        compiler_params=pltpu.CompilerParams(vmem_limit_bytes=VMEM_LIMIT),
        name="pick_blocks",
    )(me, table, cache)


def head_rows(block):
    return jnp.concatenate([block[:, i * HD : (i + 1) * HD] for i in range(GROUP)], axis=0)


def partial_sums(score_parts, value_parts):
    peak = functools.reduce(
        jnp.maximum, [jnp.max(part, axis=0, keepdims=True) for part in score_parts]
    )
    shift = jnp.maximum(peak * TO_LOG2, FLOOR).astype(jnp.bfloat16).astype(jnp.float32)
    total = jnp.zeros((1, ROWS), jnp.float32)
    acc = jnp.zeros((HD, ROWS), jnp.float32)
    for part, values in zip(score_parts, value_parts):
        expo = jnp.exp2(part * TO_LOG2 - shift)
        total += jnp.sum(expo, axis=0, keepdims=True)
        acc += lax.dot_general(
            values, expo.astype(jnp.bfloat16), CONTRACT_FIRST, preferred_element_type=jnp.float32
        )
    return shift, total, acc


def write_packet(out_ref, shift, total, acc):
    high = total.astype(jnp.bfloat16).astype(jnp.float32)
    line = lax.broadcasted_iota(jnp.int32, (STATS, ROWS), 0)
    stats = jnp.where(line == 0, shift, jnp.where(line == 1, high, jnp.where(line == 2, total - high, 0.0)))
    out_ref[:HD, :] = acc.astype(jnp.bfloat16)
    out_ref[HD:, :] = stats.astype(jnp.bfloat16)


def read_packet(ref):
    stats = ref[HD:, :].astype(jnp.float32)
    return stats[0:1], stats[1:2] + stats[2:3], ref[:HD, :].astype(jnp.float32)


def cached_part(shift, n, me_ref, table_ref, rows, blocks):
    zo, xr = coordinates(me_ref)
    home = rem(zo + shift, NZ) * NX + xr
    score_parts, value_parts = [], []
    for k in (1, 2, 3, 0):
        owner = zo * NX + rem(xr - k, NX)
        both = blocks[k][n * CAP : (n + 1) * CAP].reshape(CAP * BLK, 2 * HD)
        scores = lax.dot_general(both[:, :HD], rows, CONTRACT_LAST, preferred_element_type=jnp.float32)
        live = [
            jnp.where(
                table_ref[home, 0, owner * CAP + c] >= 0,
                scores[c * BLK : (c + 1) * BLK],
                NEG_FILL,
            )
            for c in range(CAP)
        ]
        score_parts.append(jnp.concatenate(live, axis=0))
        value_parts.append(both[:, HD:])
    return partial_sums(score_parts, value_parts)


def suffix_part(rows, both):
    scores = lax.dot_general(both[:, :HD], rows, CONTRACT_LAST, preferred_element_type=jnp.float32)
    key = lax.broadcasted_iota(jnp.int32, (SUF, ROWS), 0)
    token = lax.rem(lax.broadcasted_iota(jnp.int32, (SUF, ROWS), 1), SUF)
    return partial_sums([jnp.where(key <= token, scores, NEG_FILL)], [both[:, HD:]])


def blocks_here(shifts):
    return pltpu.VMEM((NX, len(shifts) * CAP, BLK, 2 * HD), jnp.bfloat16)


def attend_kernel(shifts, later, with_suffix, *refs):
    refs = list(refs)
    take = lambda n: [refs.pop(0) for _ in range(n)]
    me_ref, table_ref, cache_ref, z_query_ref = take(4)
    arrived = take(NX - 1)
    own_refs = take(2) if with_suffix else None
    packet_refs = take(len(shifts) + with_suffix)
    picked = take(NX - 1) if later else []
    here, query_here, packet_here = take(3)
    block_sems, query_sems, packet_sems, pick_sems = take(4)
    zo, _ = coordinates(me_ref)
    start_own_blocks(shifts, me_ref, table_ref, cache_ref, here.at[0], block_sems.at[0])
    fetches = []
    for n, shift in enumerate(shifts):
        start = pl.multiple_of(rem(zo + shift, NZ) * SUF, SUF)
        fetches.append(
            pltpu.make_async_copy(z_query_ref.at[pl.ds(start, SUF), :], query_here.at[n], query_sems.at[n])
        )
    fetches += [
        pltpu.make_async_copy(arrived[k - 1], here.at[k], block_sems.at[k]) for k in range(1, NX)
    ]
    for fetch in fetches:
        fetch.start()
    if later:
        start_picks(later, me_ref, table_ref, cache_ref, picked, pick_sems)
    sends = [
        pltpu.make_async_copy(packet_here.at[n], ref, packet_sems.at[n])
        for n, ref in enumerate(packet_refs)
    ]
    if with_suffix:
        last = len(shifts)
        part = suffix_part(head_rows(own_refs[0][...]), own_refs[1][...])
        write_packet(packet_here.at[last], *part)
        sends[last].start()
    for fetch in fetches:
        fetch.wait()
    wait_own_blocks(shifts, cache_ref, here.at[0], block_sems.at[0])
    for n, shift in enumerate(shifts):
        rows = head_rows(query_here[n])
        blocks = [here.at[k] for k in range(NX)]
        write_packet(packet_here.at[n], *cached_part(shift, n, me_ref, table_ref, rows, blocks))
        sends[n].start()
    for send in sends:
        send.wait()
    if later:
        wait_picks(later, cache_ref, picked, pick_sems)


def attend(shifts, later, me, table, cache, z_queries, arrived, own):
    keys = len(shifts) * NX * CAP * BLK
    own = list(own)
    picked = picked_shapes(later, cache.dtype) if later else []
    n_packets = len(shifts) + bool(own)
    outs = pl.pallas_call(
        functools.partial(attend_kernel, shifts, later, bool(own)),
        out_shape=[jax.ShapeDtypeStruct((PACKET, ROWS), jnp.bfloat16)] * n_packets + picked,
        in_specs=[IN_SMEM] * 2 + [IN_HBM] * (NX + 1) + [IN_VMEM] * len(own),
        out_specs=[IN_HBM] * (n_packets + len(picked)),
        scratch_shapes=[
            blocks_here(shifts),
            pltpu.VMEM((len(shifts), SUF, GROUP * HD), jnp.bfloat16),
            pltpu.VMEM((n_packets, PACKET, ROWS), jnp.bfloat16),
            pltpu.SemaphoreType.DMA((NX,)),
            pltpu.SemaphoreType.DMA((len(shifts),)),
            pltpu.SemaphoreType.DMA((n_packets,)),
            pltpu.SemaphoreType.DMA((NX - 1,)),
        ],
        compiler_params=pltpu.CompilerParams(vmem_limit_bytes=VMEM_LIMIT),
        cost_estimate=pl.CostEstimate(
            flops=4 * keys * ROWS * HD, bytes_accessed=4 * keys * HD, transcendentals=keys * ROWS
        ),
        name="attend_chunk",
    )(me, table, cache, z_queries, *arrived, *own)
    return outs[: len(shifts)], outs[len(shifts) : n_packets], outs[n_packets:]


def finish_kernel(shifts, me_ref, table_ref, cache_ref, weight_ref, query_ref, *rest):
    arrived, packet_refs = rest[: NX - 1], rest[NX - 1 : -7]
    out_ref, here, packet_here, wide, block_sems, packet_sems, wide_sem = rest[-7:]
    start_own_blocks(shifts, me_ref, table_ref, cache_ref, here.at[0], block_sems.at[0])
    fetches = [
        pltpu.make_async_copy(arrived[k - 1], here.at[k], block_sems.at[k]) for k in range(1, NX)
    ]
    packets = [
        pltpu.make_async_copy(ref, packet_here.at[n], packet_sems.at[n])
        for n, ref in enumerate(packet_refs)
    ]
    weight = pltpu.make_async_copy(weight_ref, wide, wide_sem)
    for copy in fetches + packets + [weight]:
        copy.start()
    rows = head_rows(query_ref[...])
    for fetch in fetches:
        fetch.wait()
    wait_own_blocks(shifts, cache_ref, here.at[0], block_sems.at[0])
    parts = [cached_part(0, 0, me_ref, table_ref, rows, [here.at[k] for k in range(NX)])]
    for packet in packets:
        packet.wait()
    parts += [read_packet(packet_here.at[n]) for n in range(len(packets))]
    top = functools.reduce(jnp.maximum, [part[0] for part in parts])
    factors = [jnp.exp2(part[0] - top) for part in parts]
    row_sum = sum(f * part[1] for f, part in zip(factors, parts))
    summed = sum(f * part[2] for f, part in zip(factors, parts))
    rows = (summed / row_sum).T.astype(jnp.bfloat16)
    attended = jnp.concatenate([rows[i * SUF : (i + 1) * SUF] for i in range(GROUP)], axis=1)
    weight.wait()
    out_ref[...] = jnp.dot(attended, wide[...], preferred_element_type=jnp.float32).astype(jnp.bfloat16)


def finish(shifts, me, table, cache, weight, queries, arrived, packets):
    return pl.pallas_call(
        functools.partial(finish_kernel, shifts),
        out_shape=jax.ShapeDtypeStruct((SUF, weight.shape[1]), jnp.bfloat16),
        in_specs=[IN_SMEM] * 2 + [IN_HBM] * 2 + [IN_VMEM] + [IN_HBM] * (NX - 1 + len(packets)),
        out_specs=IN_VMEM,
        scratch_shapes=[
            blocks_here(shifts),
            pltpu.VMEM((len(packets), PACKET, ROWS), jnp.bfloat16),
            pltpu.VMEM(weight.shape, weight.dtype),
            pltpu.SemaphoreType.DMA((NX,)),
            pltpu.SemaphoreType.DMA((len(packets),)),
            pltpu.SemaphoreType.DMA,
        ],
        compiler_params=pltpu.CompilerParams(vmem_limit_bytes=VMEM_LIMIT),
        cost_estimate=pl.CostEstimate(
            flops=2 * SUF * weight.size, bytes_accessed=2 * weight.size, transcendentals=0
        ),
        name="merge_project",
    )(me, table, cache, weight, queries, *arrived, *packets)


def x_permute(a, step):
    pairs = [(z * NX + x, z * NX + (x + step) % NX) for z in range(NZ) for x in range(NX)]
    return lax.ppermute(a, "store", pairs)


def z_permute(a, step):
    pairs = [(z * NX + x, ((z + step) % NZ) * NX + x) for z in range(NZ) for x in range(NX)]
    return lax.ppermute(a, "store", pairs)


def y_permute(a, step):
    pairs = [
        (y * CORES + c, ((y + step) % NY) * CORES + c) for y in range(NY) for c in range(CORES)
    ]
    return lax.ppermute(a, "head", pairs)


def core_swap(a):
    return lax.ppermute(a, "head", [(h, h ^ 1) for h in range(NY * CORES)])


def sum_heads(partial):
    core = lax.rem(lax.axis_index("head"), CORES)
    y = lax.div(lax.axis_index("head"), CORES)
    parts = partial.reshape(NY, CORES, HEAD_ROWS, partial.shape[1])
    pick_core = lambda which: lax.dynamic_index_in_dim(parts, which, 1, keepdims=False)
    other = core_swap(pick_core(1 - core))
    both = pick_core(core).astype(jnp.float32) + other.astype(jnp.float32)
    pick_y = lambda step: lax.dynamic_index_in_dim(both, rem(y + step, NY), 0, keepdims=False)
    arrived = [y_permute(pick_y(step).astype(jnp.bfloat16), step) for step in (2, 1, 3)]
    return (pick_y(0) + sum(a.astype(jnp.float32) for a in arrived)).astype(jnp.bfloat16)


def local(queries, suffix_kv, kv_cache, block_owner, block_slot, prefix_blocks, out_weight):
    store_count = lax.axis_size("store")
    me = lax.axis_index("store").astype(jnp.int32).reshape(1)
    wanted = wanted_slots(prefix_blocks, block_owner, block_slot, store_count)
    table = lax.all_to_all(wanted, "store", split_axis=0, concat_axis=0, tiled=True)
    z_groups = [[z * NX + x for z in range(NZ)] for x in range(NX)]
    z_queries = lax.all_gather(queries, "store", axis=0, tiled=True, axis_index_groups=z_groups)
    z_queries = keep_in_hbm(z_queries)
    cache = keep_in_hbm(kv_cache.reshape(kv_cache.shape[0], BLK, 2 * HD))
    suffix = suffix_kv.reshape(SUF, 2 * HD)
    picked = [pick(shifts, me, table, cache) for shifts in CHUNKS[:AHEAD]]
    packets = []
    for g, shifts in enumerate(CHUNKS[:-1]):
        arrived = [x_permute(a, k) for k, a in enumerate(picked[g], 1)]
        later = CHUNKS[g + AHEAD] if g + AHEAD < len(CHUNKS) else ()
        own = () if g else (queries, suffix)
        mine, own, more = attend(shifts, later, me, table, cache, z_queries, arrived, own)
        packets += [z_permute(packet, s) for s, packet in zip(shifts, mine)] + list(own)
        picked.append(more)
    arrived = [x_permute(a, k) for k, a in enumerate(picked[len(CHUNKS) - 1], 1)]
    return sum_heads(finish(CHUNKS[-1], me, table, cache, keep_in_hbm(out_weight), queries, arrived, packets))


def solution(mesh):
    in_specs = (
        P("store", "head"),
        P("store", "head", None),
        P("store", "head", None, None),
        P("store", None),
        P("store", None),
        P("store"),
        P("head", None),
    )
    out_specs = P(("store", "head"), None)
    return jax.shard_map(local, mesh=mesh, in_specs=in_specs, out_specs=out_specs, check_vma=False)
```

time: 151 us -> 140 us (0.927)
  Pallas kernels: 24.1 us -> 50.9 us
  local copies, waits for them, and re-layouts: 27 us -> 1.37 us
  starting transfers between devices: 43.6 us -> 37.9 us
  waiting for transfers between devices: 38.2 us -> 34.8 us
  other arithmetic: 2.55 us -> 0.72 us
    pallas_call x10 -> x6, Pallas kernels: 24.1 us -> 50.9 us  [the longest x2 28.5 us: pick(): pl.pallas_call(functools.partial(pick_kernel, shifts), out_shape=shapes,...]
    unnamed x56 -> x8, local copies, waits for them, and re-layouts: 26 us -> 1.31 us
    ppermute x12 -> x9, waiting for transfers between devices: 20.6 us -> 3.25 us  [x_permute(): return lax.ppermute(a, 'store', pairs)]
    ppermute x7, waiting for transfers between devices: 0.02 us -> 14.1 us  [z_permute(): return lax.ppermute(a, 'store', pairs)]
    ppermute x7, starting transfers between devices: 13.4 us -> 10.5 us  [z_permute(): return lax.ppermute(a, 'store', pairs)]
    ppermute x12 -> x9, starting transfers between devices: 15.2 us -> 12.5 us  [x_permute(): return lax.ppermute(a, 'store', pairs)]
  transfers between devices with their start and end apart: 25 -> 22, of which waited for: 6 -> 8; matrix products, arithmetic and copies ran while one was open for 2% -> 0% of each run, Pallas kernels for 15% -> 30%
where the time goes in v2:
time: 140 us
  Pallas kernels  50.9 us (36%)
  starting transfers between devices  37.9 us (27%)
  waiting for transfers between devices  34.8 us (25%)
  between operations  14.2 us (10%)
    pallas_call x2, Pallas kernels, pick(): pl.pallas_call(functools.partial(pick_kernel, shifts), out_shape=shapes,...  28.5 us
    ppermute x7, waiting for transfers between devices, z_permute(): return lax.ppermute(a, 'store', pairs)  14.1 us
    pallas_call x2, Pallas kernels, attend(): pl.pallas_call(functools.partial(attend_kernel, shifts, later, bool(own))...  13.3 us
    ppermute x9, starting transfers between devices, x_permute(): return lax.ppermute(a, 'store', pairs)  12.5 us
    all_to_all x1, starting transfers between devices, local(): lax.all_to_all(wanted, 'store', split_axis=0, concat_axis=0, tiled=True)  11.3 us
    ppermute x7, starting transfers between devices, z_permute(): return lax.ppermute(a, 'store', pairs)  10.5 us
    all_to_all x1, waiting for transfers between devices, local(): lax.all_to_all(wanted, 'store', split_axis=0, concat_axis=0, tiled=True)  9.76 us
    pallas_call x1, Pallas kernels, finish(): pl.pallas_call(functools.partial(finish_kernel, shifts), out_shape=jax.Sh...  8.29 us
  transfers between devices with their start and end apart: 22, of which 8 were waited for; matrix products, arithmetic and copies ran while one was open for 0% of the time, Pallas kernels for 30%

profile of v2, /device:TPU:24, one launch (start us, length us, event | category | flops | bytes accessed | tf_op | source)
XLA Modules:
  0.0 139.9 jit_solution(3147730415772734806)
XLA Ops:
  10.1 11.3 %all-to-all-start = ((s32[32,1,128]{2,1,0:T(1,128)}), s32[32,1,128]{2,1,0:T(1,128)S(1)}, u32[]{:S(2)}, u32[]{:S(2)}) async-start(s32[32,1,128]{2,1,0:T(1,128)} %wanted_slots.1), calls=%async_computation | async-start | bytes 32768 | tf_op jit(solution)/shard_map/all_to_all | solution.py:387
  21.5 9.8 %all-to-all-done.table_ref.refs_1_ = s32[32,1,128]{2,1,0:T(1,128)S(1)} async-done(((s32[32,1,128]{2,1,0:T(1,128)}), s32[32,1,128]{2,1,0:T(1,128)S(1)}, u32[]{:S(2)}, u32[]{:S(2)}) %all-to-all-start) | async-done | bytes 16416 | tf_op jit(solution)/shard_map/all_to_all | solution.py:387
  31.2 2.7 %pick_blocks.2 = (bf16[16,64,256]{2,1,0:T(8,128)(2,1)S(1)}, bf16[16,64,256]{2,1,0:T(8,128)(2,1)S(1)}, bf16[16,64,256]{2,1,0:T(8,128)(2,1)S(1)}) custom-call(s32[1]{0:T(128)} %bitcast.me_ref.refs_0_, s32[32,1,128]{2,1,0:T(1,128)S(1)} %all-to-all-done.table_ref.refs_1_, bf16[128,64,256]{2,1,0:T(8,128)(2,1)} %bitcast.24), custom_call_target="tpu_custom_call" | custom-call | tf_op jit(solution)/shard_map/pick_blocks/pallas_call | solution.py:144
  34.6 2.2 %collective-permute-start.1 = (bf16[16,64,256]{2,1,0:T(8,128)(2,1)S(1)}, bf16[16,64,256]{2,1,0:T(8,128)(2,1)S(1)}, u32[]{:S(2)}, u32[]{:S(2)}) collective-permute-start(bf16[16,64,256]{2,1,0:T(8,128)(2,1)S(1)} %get-tuple-element.23), channel_id=1, source_target_pairs={{0,16},{8,24},{16,0},{24,8},{32,48},{40,56},{48,32},{56,40},{64,80... | collective-permute-start | bytes 1572872 | tf_op jit(solution)/shard_map/ppermute | solution.py:352
  37.8 25.8 %pick_blocks.3 = (bf16[12,64,256]{2,1,0:T(8,128)(2,1)S(1)}, bf16[12,64,256]{2,1,0:T(8,128)(2,1)}, bf16[12,64,256]{2,1,0:T(8,128)(2,1)}) custom-call(s32[1]{0:T(128)} %bitcast.me_ref.refs_0_, s32[32,1,128]{2,1,0:T(1,128)S(1)} %all-to-all-done.table_ref.refs_1_, bf16[128,64,256]{2,1,0:T(8,128)(2,1)} %bitcast.25), custom_call_target="tpu_custom_call" | custom-call | tf_op jit(solution)/shard_map/pick_blocks/pallas_call | solution.py:144
  64.7 1.4 %collective-permute-start.11 = (bf16[12,64,256]{2,1,0:T(8,128)(2,1)}, bf16[12,64,256]{2,1,0:T(8,128)(2,1)S(1)}, u32[]{:S(2)}, u32[]{:S(2)}) collective-permute-start(bf16[12,64,256]{2,1,0:T(8,128)(2,1)} %get-tuple-element.34), channel_id=1, source_target_pairs={{0,16},{8,24},{16,0},{24,8},{32,48},{40,56},{48,32},{56,40},{64,80... | collective-permute-start | bytes 1179656 | tf_op jit(solution)/shard_map/ppermute | solution.py:352
  66.1 2.5 %collective-permute-start.12 = (bf16[12,64,256]{2,1,0:T(8,128)(2,1)}, bf16[12,64,256]{2,1,0:T(8,128)(2,1)S(1)}, u32[]{:S(2)}, u32[]{:S(2)}) collective-permute-start(bf16[12,64,256]{2,1,0:T(8,128)(2,1)} %get-tuple-element.35), channel_id=1, source_target_pairs={{0,24},{8,0},{16,8},{24,16},{32,56},{40,32},{48,40},{56,48},{64,88... | collective-permute-start | bytes 1179656 | tf_op jit(solution)/shard_map/ppermute | solution.py:352
  68.7 7.4 %attend_chunk.2 = (bf16[144,512]{1,0:T(8,128)(2,1)S(1)}, bf16[144,512]{1,0:T(8,128)(2,1)S(1)}, bf16[144,512]{1,0:T(8,128)(2,1)}, bf16[144,512]{1,0:T(8,128)(2,1)...) custom-call(s32[1]{0:T(128)} %bitcast.me_ref.refs_0_, ...), custom_call_target="tpu_custom_call" | custom-call | flops 1073741824 | bytes 2097152 | tf_op jit(solution)/shard_map/attend_chunk/pallas_call | solution.py:273
  76.6 3.3 %collective-permute-start.7 = (bf16[144,512]{1,0:T(8,128)(2,1)S(1)}, bf16[144,512]{1,0:T(8,128)(2,1)S(1)}, u32[]{:S(2)}, u32[]{:S(2)}) collective-permute-start(bf16[144,512]{1,0:T(8,128)(2,1)S(1)} %get-tuple-element.29), channel_id=1, source_target_pairs={{0,96},{8,104},{16,112},{24,120},{32,128},{40,136},{48,144},{56,15... | collective-permute-start | bytes 442376 | tf_op jit(solution)/shard_map/ppermute | solution.py:357
  79.9 3.2 %collective-permute-done.11.refs_5_ = bf16[12,64,256]{2,1,0:T(8,128)(2,1)S(1)} collective-permute-done((bf16[12,64,256]{2,1,0:T(8,128)(2,1)}, bf16[12,64,256]{2,1,0:T(8,128)(2,1)S(1)}, u32[]{:S(2)}, u32[]{:S(2)}) %collective-permute-start.11) | collective-permute-done | bytes 393248 | tf_op jit(solution)/shard_map/ppermute | solution.py:352
  83.1 2.1 %collective-permute-start.4 = (bf16[4,64,256]{2,1,0:T(8,128)(2,1)S(1)}, bf16[4,64,256]{2,1,0:T(8,128)(2,1)S(1)}, u32[]{:S(2)}, u32[]{:S(2)}) collective-permute-start(bf16[4,64,256]{2,1,0:T(8,128)(2,1)S(1)} %get-tuple-element.26), channel_id=1, source_target_pairs={{0,16},{8,24},{16,0},{24,8},{32,48},{40,56},{48,32},{56,40},{64,80... | collective-permute-start | bytes 393224 | tf_op jit(solution)/shard_map/ppermute | solution.py:352
  85.3 1.4 collective-permute-start.5
  86.7 5.9 %attend_chunk.3 = (bf16[144,512]{1,0:T(8,128)(2,1)S(1)}, bf16[144,512]{1,0:T(8,128)(2,1)S(1)}, bf16[144,512]{1,0:T(8,128)(2,1)S(1)}) custom-call(s32[1]{0:T(128)} %bitcast.me_ref.refs_0_, s32[32,1,128]{2,1,0:T(1,128)S(1)} %all-to-all-done.table_ref.refs_1_, bf16[128,64,256]{2,1,0:T(8,128)(2,1)} %bitcast.27, ...), custom_call_target="tpu_custom_call" | custom-call | flops 805306368 | bytes 1572864 | tf_op jit(solution)/shard_map/attend_chunk/pallas_call | solution.py:273
  93.1 2.2 %collective-permute-start.9 = (bf16[144,512]{1,0:T(8,128)(2,1)}, bf16[144,512]{1,0:T(8,128)(2,1)S(1)}, u32[]{:S(2)}, u32[]{:S(2)}) collective-permute-start(bf16[144,512]{1,0:T(8,128)(2,1)} %get-tuple-element.31), channel_id=1, source_target_pairs={{0,64},{8,72},{16,80},{24,88},{32,96},{40,104},{48,112},{56,120},{... | collective-permute-start | bytes 442376 | tf_op jit(solution)/shard_map/ppermute | solution.py:357
  95.3 2.0 %collective-permute-start.13 = (bf16[144,512]{1,0:T(8,128)(2,1)S(1)}, bf16[144,512]{1,0:T(8,128)(2,1)S(1)}, u32[]{:S(2)}, u32[]{:S(2)}) collective-permute-start(bf16[144,512]{1,0:T(8,128)(2,1)S(1)} %get-tuple-element.36), channel_id=1, source_target_pairs={{0,192},{8,200},{16,208},{24,216},{32,224},{40,232},{48,240},{56,2... | collective-permute-start | bytes 442376 | tf_op jit(solution)/shard_map/ppermute | solution.py:357
  97.3 2.0 %collective-permute-start.15 = (bf16[144,512]{1,0:T(8,128)(2,1)S(1)}, bf16[144,512]{1,0:T(8,128)(2,1)S(1)}, u32[]{:S(2)}, u32[]{:S(2)}) collective-permute-start(bf16[144,512]{1,0:T(8,128)(2,1)S(1)} %get-tuple-element.38), channel_id=1, source_target_pairs={{0,32},{8,40},{16,48},{24,56},{32,64},{40,72},{48,80},{56,88},{64,... | collective-permute-start | bytes 442376 | tf_op jit(solution)/shard_map/ppermute | solution.py:357
  99.3 6.5 %collective-permute-done.8.rest_5_ = bf16[144,512]{1,0:T(8,128)(2,1)S(1)} collective-permute-done((bf16[144,512]{1,0:T(8,128)(2,1)}, bf16[144,512]{1,0:T(8,128)(2,1)S(1)}, u32[]{:S(2)}, u32[]{:S(2)}) %collective-permute-start.8) | collective-permute-done | bytes 147488 | tf_op jit(solution)/shard_map/ppermute | solution.py:357
  105.8 6.8 %collective-permute-done.13.rest_8_ = bf16[144,512]{1,0:T(8,128)(2,1)S(1)} collective-permute-done((bf16[144,512]{1,0:T(8,128)(2,1)S(1)}, bf16[144,512]{1,0:T(8,128)(2,1)S(1)}, u32[]{:S(2)}, u32[]{:S(2)}) %collective-permute-start.13) | collective-permute-done | bytes 147488 | tf_op jit(solution)/shard_map/ppermute | solution.py:357
  113.4 8.3 %merge_project.1 = bf16[64,4096]{1,0:T(8,128)(2,1)S(1)} custom-call(s32[1]{0:T(128)} %bitcast.me_ref.refs_0_, s32[32,1,128]{2,1,0:T(1,128)S(1)} %all-to-all-done.table_ref.refs_1_, bf16[128,64,256]{2,1,0:T(8,128)(2,1)} %bitcast.28, bf16[1024,4096]{1,0:T(8,128)(2,1)} %weight_ref.1, bf16[64,1024]{1,0:T(8,128)(2,1)S(1)} %copy-done, ...), custom_call_target="tpu_custom_call" | custom-call | flops 536870912 | bytes 8388608 | tf_op jit(solution)/shard_map/merge_project/pallas_call | solution.py:329
  121.9 1.5 %collective-permute-done.16 = bf16[4,8,4096]{2,1,0:T(8,128)(2,1)S(1)} collective-permute-done((bf16[4,8,4096]{2,1,0:T(8,128)(2,1)S(1)}, bf16[4,8,4096]{2,1,0:T(8,128)(2,1)S(1)}, u32[]{:S(2)}, u32[]{:S(2)}) %collective-permute-start.16) | collective-permute-done | bytes 262176 | tf_op jit(solution)/shard_map/ppermute | solution.py:368
  123.4 1.3 collective-permute-start.17
  124.8 2.2 %collective-permute-start.18 = (bf16[8,4096]{1,0:T(8,128)(2,1)S(1)}, bf16[8,4096]{1,0:T(8,128)(2,1)S(1)}, u32[]{:S(2)}, u32[]{:S(2)}) collective-permute-start(bf16[8,4096]{1,0:T(8,128)(2,1)S(1)} %get-tuple-element.41), channel_id=1, source_target_pairs={{0,2},{1,3},{2,4},{3,5},{4,6},{5,7},{6,0},{7,1},{8,10},{9,11},{10,... | collective-permute-start | bytes 196616 | tf_op jit(solution)/shard_map/ppermute | solution.py:364
  126.9 2.5 %collective-permute-done.17 = bf16[8,4096]{1,0:T(8,128)(2,1)S(1)} collective-permute-done((bf16[8,4096]{1,0:T(8,128)(2,1)S(1)}, bf16[8,4096]{1,0:T(8,128)(2,1)S(1)}, u32[]{:S(2)}, u32[]{:S(2)}) %collective-permute-start.17) | collective-permute-done | bytes 65568 | tf_op jit(solution)/shard_map/ppermute | solution.py:364
  129.4 3.0 %collective-permute-done.19 = bf16[8,4096]{1,0:T(8,128)(2,1)S(1)} collective-permute-done((bf16[8,4096]{1,0:T(8,128)(2,1)S(1)}, bf16[8,4096]{1,0:T(8,128)(2,1)S(1)}, u32[]{:S(2)}, u32[]{:S(2)}) %collective-permute-start.19) | collective-permute-done | bytes 65568 | tf_op jit(solution)/shard_map/ppermute | solution.py:364
  (39 shorter events, 8.5 us)
Async XLA Ops:
  6.5 62.1 %copy-start = (bf16[64,1024]{1,0:T(8,128)(2,1)S(1)}, bf16[64,1024]{1,0:T(8,128)(2,1)}, u32[]{:S(2)}) copy-start(bf16[64,1024]{1,0:T(8,128)(2,1)} %query_ref.1) | copy-start | bytes 393220
  6.5 62.1 %copy-start.1 = (bf16[64,1,256]{2,0,1:T(8,128)(2,1)S(1)}, bf16[64,1,256]{2,0,1:T(8,128)(2,1)}, u32[]{:S(2)}) copy-start(bf16[64,1,256]{2,0,1:T(8,128)(2,1)} %param.8) | copy-start | bytes 98308
  6.5 62.1 %all-gather.2.cloned.1.call-start = ((), (), s32[]{:S(2)}) async-start(), calls=%async_computation.1 | async-start | bytes 1179648 | tf_op jit(solution)/shard_map/all_gather | solution.py:389
  10.1 21.1 %all-to-all-start = ((s32[32,1,128]{2,1,0:T(1,128)}), s32[32,1,128]{2,1,0:T(1,128)S(1)}, u32[]{:S(2)}, u32[]{:S(2)}) async-start(s32[32,1,128]{2,1,0:T(1,128)} %wanted_slots.1), calls=%async_computation | async-start | bytes 32768 | tf_op jit(solution)/shard_map/all_to_all | solution.py:387
  33.9 32.2 %collective-permute-start = (bf16[16,64,256]{2,1,0:T(8,128)(2,1)S(1)}, bf16[16,64,256]{2,1,0:T(8,128)(2,1)S(1)}, u32[]{:S(2)}, u32[]{:S(2)}) collective-permute-start(bf16[16,64,256]{2,1,0:T(8,128)(2,1)S(1)} %get-tuple-element.22), channel_id=1, source_target_pairs={{0,8},{8,16},{16,24},{24,0},{32,40},{40,48},{48,56},{56,32},{64,72... | collective-permute-start | bytes 1572872 | tf_op jit(solution)/shard_map/ppermute | solution.py:352
  34.6 34.1 %collective-permute-start.1 = (bf16[16,64,256]{2,1,0:T(8,128)(2,1)S(1)}, bf16[16,64,256]{2,1,0:T(8,128)(2,1)S(1)}, u32[]{:S(2)}, u32[]{:S(2)}) collective-permute-start(bf16[16,64,256]{2,1,0:T(8,128)(2,1)S(1)} %get-tuple-element.23), channel_id=1, source_target_pairs={{0,16},{8,24},{16,0},{24,8},{32,48},{40,56},{48,32},{56,40},{64,80... | collective-permute-start | bytes 1572872 | tf_op jit(solution)/shard_map/ppermute | solution.py:352
  36.8 31.9 %collective-permute-start.2 = (bf16[16,64,256]{2,1,0:T(8,128)(2,1)S(1)}, bf16[16,64,256]{2,1,0:T(8,128)(2,1)S(1)}, u32[]{:S(2)}, u32[]{:S(2)}) collective-permute-start(bf16[16,64,256]{2,1,0:T(8,128)(2,1)S(1)} %get-tuple-element.24), channel_id=1, source_target_pairs={{0,24},{8,0},{16,8},{24,16},{32,56},{40,32},{48,40},{56,48},{64,88... | collective-permute-start | bytes 1572872 | tf_op jit(solution)/shard_map/ppermute | solution.py:352
  63.7 16.2 %collective-permute-start.10 = (bf16[12,64,256]{2,1,0:T(8,128)(2,1)S(1)}, bf16[12,64,256]{2,1,0:T(8,128)(2,1)S(1)}, u32[]{:S(2)}, u32[]{:S(2)}) collective-permute-start(bf16[12,64,256]{2,1,0:T(8,128)(2,1)S(1)} %get-tuple-element.33), channel_id=1, source_target_pairs={{0,8},{8,16},{16,24},{24,0},{32,40},{40,48},{48,56},{56,32},{64,72... | collective-permute-start | bytes 1179656 | tf_op jit(solution)/shard_map/ppermute | solution.py:352
  64.7 18.4 %collective-permute-start.11 = (bf16[12,64,256]{2,1,0:T(8,128)(2,1)}, bf16[12,64,256]{2,1,0:T(8,128)(2,1)S(1)}, u32[]{:S(2)}, u32[]{:S(2)}) collective-permute-start(bf16[12,64,256]{2,1,0:T(8,128)(2,1)} %get-tuple-element.34), channel_id=1, source_target_pairs={{0,16},{8,24},{16,0},{24,8},{32,48},{40,56},{48,32},{56,40},{64,80... | collective-permute-start | bytes 1179656 | tf_op jit(solution)/shard_map/ppermute | solution.py:352
  66.1 19.1 %collective-permute-start.12 = (bf16[12,64,256]{2,1,0:T(8,128)(2,1)}, bf16[12,64,256]{2,1,0:T(8,128)(2,1)S(1)}, u32[]{:S(2)}, u32[]{:S(2)}) collective-permute-start(bf16[12,64,256]{2,1,0:T(8,128)(2,1)} %get-tuple-element.35), channel_id=1, source_target_pairs={{0,24},{8,0},{16,8},{24,16},{32,56},{40,32},{48,40},{56,48},{64,88... | collective-permute-start | bytes 1179656 | tf_op jit(solution)/shard_map/ppermute | solution.py:352
  76.1 21.2 %collective-permute-start.6 = (bf16[144,512]{1,0:T(8,128)(2,1)S(1)}, bf16[144,512]{1,0:T(8,128)(2,1)S(1)}, u32[]{:S(2)}, u32[]{:S(2)}) collective-permute-start(bf16[144,512]{1,0:T(8,128)(2,1)S(1)} %get-tuple-element.28), channel_id=1, source_target_pairs={{0,128},{8,136},{16,144},{24,152},{32,160},{40,168},{48,176},{56,1... | collective-permute-start | bytes 442376 | tf_op jit(solution)/shard_map/ppermute | solution.py:357
  76.6 20.6 %collective-permute-start.7 = (bf16[144,512]{1,0:T(8,128)(2,1)S(1)}, bf16[144,512]{1,0:T(8,128)(2,1)S(1)}, u32[]{:S(2)}, u32[]{:S(2)}) collective-permute-start(bf16[144,512]{1,0:T(8,128)(2,1)S(1)} %get-tuple-element.29), channel_id=1, source_target_pairs={{0,96},{8,104},{16,112},{24,120},{32,128},{40,136},{48,144},{56,15... | collective-permute-start | bytes 442376 | tf_op jit(solution)/shard_map/ppermute | solution.py:357
  79.9 12.7 %collective-permute-start.3 = (bf16[4,64,256]{2,1,0:T(8,128)(2,1)S(1)}, bf16[4,64,256]{2,1,0:T(8,128)(2,1)S(1)}, u32[]{:S(2)}, u32[]{:S(2)}) collective-permute-start(bf16[4,64,256]{2,1,0:T(8,128)(2,1)S(1)} %get-tuple-element.25), channel_id=1, source_target_pairs={{0,8},{8,16},{16,24},{24,0},{32,40},{40,48},{48,56},{56,32},{64,72... | collective-permute-start | bytes 393224 | tf_op jit(solution)/shard_map/ppermute | solution.py:352
  83.1 10.0 %collective-permute-start.4 = (bf16[4,64,256]{2,1,0:T(8,128)(2,1)S(1)}, bf16[4,64,256]{2,1,0:T(8,128)(2,1)S(1)}, u32[]{:S(2)}, u32[]{:S(2)}) collective-permute-start(bf16[4,64,256]{2,1,0:T(8,128)(2,1)S(1)} %get-tuple-element.26), channel_id=1, source_target_pairs={{0,16},{8,24},{16,0},{24,8},{32,48},{40,56},{48,32},{56,40},{64,80... | collective-permute-start | bytes 393224 | tf_op jit(solution)/shard_map/ppermute | solution.py:352
  85.3 10.0 %collective-permute-start.5 = (bf16[4,64,256]{2,1,0:T(8,128)(2,1)S(1)}, bf16[4,64,256]{2,1,0:T(8,128)(2,1)S(1)}, u32[]{:S(2)}, u32[]{:S(2)}) collective-permute-start(bf16[4,64,256]{2,1,0:T(8,128)(2,1)S(1)} %get-tuple-element.27), channel_id=1, source_target_pairs={{0,24},{8,0},{16,8},{24,16},{32,56},{40,32},{48,40},{56,48},{64,88... | collective-permute-start | bytes 393224 | tf_op jit(solution)/shard_map/ppermute | solution.py:352
  92.6 13.2 %collective-permute-start.8 = (bf16[144,512]{1,0:T(8,128)(2,1)}, bf16[144,512]{1,0:T(8,128)(2,1)S(1)}, u32[]{:S(2)}, u32[]{:S(2)}) collective-permute-start(bf16[144,512]{1,0:T(8,128)(2,1)} %get-tuple-element.30), channel_id=1, source_target_pairs={{0,160},{8,168},{16,176},{24,184},{32,192},{40,200},{48,208},{56,2... | collective-permute-start | bytes 442376 | tf_op jit(solution)/shard_map/ppermute | solution.py:357
  93.1 12.7 %collective-permute-start.9 = (bf16[144,512]{1,0:T(8,128)(2,1)}, bf16[144,512]{1,0:T(8,128)(2,1)S(1)}, u32[]{:S(2)}, u32[]{:S(2)}) collective-permute-start(bf16[144,512]{1,0:T(8,128)(2,1)} %get-tuple-element.31), channel_id=1, source_target_pairs={{0,64},{8,72},{16,80},{24,88},{32,96},{40,104},{48,112},{56,120},{... | collective-permute-start | bytes 442376 | tf_op jit(solution)/shard_map/ppermute | solution.py:357
  95.3 17.4 %collective-permute-start.13 = (bf16[144,512]{1,0:T(8,128)(2,1)S(1)}, bf16[144,512]{1,0:T(8,128)(2,1)S(1)}, u32[]{:S(2)}, u32[]{:S(2)}) collective-permute-start(bf16[144,512]{1,0:T(8,128)(2,1)S(1)} %get-tuple-element.36), channel_id=1, source_target_pairs={{0,192},{8,200},{16,208},{24,216},{32,224},{40,232},{48,240},{56,2... | collective-permute-start | bytes 442376 | tf_op jit(solution)/shard_map/ppermute | solution.py:357
  97.2 16.1 %collective-permute-start.14 = (bf16[144,512]{1,0:T(8,128)(2,1)S(1)}, bf16[144,512]{1,0:T(8,128)(2,1)S(1)}, u32[]{:S(2)}, u32[]{:S(2)}) collective-permute-start(bf16[144,512]{1,0:T(8,128)(2,1)S(1)} %get-tuple-element.37), channel_id=1, source_target_pairs={{0,224},{8,232},{16,240},{24,248},{32,0},{40,8},{48,16},{56,24},{6... | collective-permute-start | bytes 442376 | tf_op jit(solution)/shard_map/ppermute | solution.py:357
  97.3 16.1 %collective-permute-start.15 = (bf16[144,512]{1,0:T(8,128)(2,1)S(1)}, bf16[144,512]{1,0:T(8,128)(2,1)S(1)}, u32[]{:S(2)}, u32[]{:S(2)}) collective-permute-start(bf16[144,512]{1,0:T(8,128)(2,1)S(1)} %get-tuple-element.38), channel_id=1, source_target_pairs={{0,32},{8,40},{16,48},{24,56},{32,64},{40,72},{48,80},{56,88},{64,... | collective-permute-start | bytes 442376 | tf_op jit(solution)/shard_map/ppermute | solution.py:357
  121.7 1.6 %collective-permute-start.16 = (bf16[4,8,4096]{2,1,0:T(8,128)(2,1)S(1)}, bf16[4,8,4096]{2,1,0:T(8,128)(2,1)S(1)}, u32[]{:S(2)}, u32[]{:S(2)}) collective-permute-start(bf16[4,8,4096]{2,1,0:T(8,128)(2,1)S(1)} %dynamic-slice_bitcast_fusion), channel_id=1, source_target_pairs={{0,1},{1,0},{2,3},{3,2},{4,5},{5,4},{6,7},{7,6},{8,9},{9,8},{10,11... | collective-permute-start | bytes 786440 | tf_op jit(solution)/shard_map/ppermute | solution.py:368
  123.4 6.0 %collective-permute-start.17 = (bf16[8,4096]{1,0:T(8,128)(2,1)S(1)}, bf16[8,4096]{1,0:T(8,128)(2,1)S(1)}, u32[]{:S(2)}, u32[]{:S(2)}) collective-permute-start(bf16[8,4096]{1,0:T(8,128)(2,1)S(1)} %get-tuple-element.39), channel_id=1, source_target_pairs={{0,4},{1,5},{2,6},{3,7},{4,0},{5,1},{6,2},{7,3},{8,12},{9,13},{10,... | collective-permute-start | bytes 196616 | tf_op jit(solution)/shard_map/ppermute | solution.py:364
  124.8 4.7 %collective-permute-start.18 = (bf16[8,4096]{1,0:T(8,128)(2,1)S(1)}, bf16[8,4096]{1,0:T(8,128)(2,1)S(1)}, u32[]{:S(2)}, u32[]{:S(2)}) collective-permute-start(bf16[8,4096]{1,0:T(8,128)(2,1)S(1)} %get-tuple-element.41), channel_id=1, source_target_pairs={{0,2},{1,3},{2,4},{3,5},{4,6},{5,7},{6,0},{7,1},{8,10},{9,11},{10,... | collective-permute-start | bytes 196616 | tf_op jit(solution)/shard_map/ppermute | solution.py:364
  126.9 5.5 %collective-permute-start.19 = (bf16[8,4096]{1,0:T(8,128)(2,1)S(1)}, bf16[8,4096]{1,0:T(8,128)(2,1)S(1)}, u32[]{:S(2)}, u32[]{:S(2)}) collective-permute-start(bf16[8,4096]{1,0:T(8,128)(2,1)S(1)} %get-tuple-element.40), channel_id=1, source_target_pairs={{0,6},{1,7},{2,0},{3,1},{4,2},{5,3},{6,4},{7,5},{8,14},{9,15},{10,... | collective-permute-start | bytes 196616 | tf_op jit(solution)/shard_map/ppermute | solution.py:364
  (2 other events, 1.3 us)
Sparse Core Ops, SparseCore 0:
  9.1 41.1 all-gather.1

commit v3 on v2

--- a/solution.py
+++ b/solution.py
@@ -25,8 +25,8 @@
 NEG_FILL = -1e30
 FLOOR = -1e9
 TO_LOG2 = math.log2(math.e) / math.sqrt(HD)
-CHUNKS = ((4, 3, 5, 2), (6, 7, 1), (0,))
-AHEAD = 2
+CHUNKS = ((4, 3, 5, 2), (6, 7, 1, 0))
+WIDE_PARTS = 8
 VMEM_LIMIT = 40 * 1024 * 1024
 
 CONTRACT_LAST = (((1,), (1,)), ((), ()))
@@ -96,60 +96,50 @@
 
 def start_picks(shifts, me_ref, table_ref, cache_ref, outs, sems):
     zo, xo = coordinates(me_ref)
-    for k in range(1, NX):
+    for k in range(NX):
         for n, shift in enumerate(shifts):
             home = rem(zo + shift, NZ) * NX + rem(xo + k, NX)
             for c in range(CAP):
                 slot = slot_of(table_ref, home, me_ref[0], c, cache_ref)
                 pltpu.make_async_copy(
                     cache_ref.at[pl.ds(slot, 1)],
-                    outs[k - 1].at[pl.ds(n * CAP + c, 1)],
-                    sems.at[k - 1],
+                    outs[k].at[pl.ds(n * CAP + c, 1)],
+                    sems.at[k],
                 ).start()
 
 
 def wait_picks(shifts, cache_ref, outs, sems):
-    for k in range(1, NX):
+    for k in range(NX):
         pltpu.make_async_copy(
-            cache_ref.at[pl.ds(0, len(shifts) * CAP)], outs[k - 1], sems.at[k - 1]
+            cache_ref.at[pl.ds(0, len(shifts) * CAP)], outs[k], sems.at[k]
         ).wait()
 
 
-def start_own_blocks(shifts, me_ref, table_ref, cache_ref, here_ref, sem):
-    zo, xo = coordinates(me_ref)
-    for n, shift in enumerate(shifts):
-        for c in range(CAP):
-            slot = slot_of(table_ref, rem(zo + shift, NZ) * NX + xo, me_ref[0], c, cache_ref)
-            pltpu.make_async_copy(
-                cache_ref.at[pl.ds(slot, 1)], here_ref.at[pl.ds(n * CAP + c, 1)], sem
-            ).start()
-
-
-def wait_own_blocks(shifts, cache_ref, here_ref, sem):
-    pltpu.make_async_copy(cache_ref.at[pl.ds(0, len(shifts) * CAP)], here_ref, sem).wait()
-
-
 def picked_shapes(shifts, dtype):
-    return [jax.ShapeDtypeStruct((len(shifts) * CAP, BLK, 2 * HD), dtype)] * (NX - 1)
-
-
-def pick_kernel(shifts, me_ref, table_ref, cache_ref, *rest):
+    return [jax.ShapeDtypeStruct((len(shifts) * CAP, BLK, 2 * HD), dtype)] * NX
+
+
+def pick_kernel(groups, me_ref, table_ref, cache_ref, *rest):
     outs, sems = rest[:-1], rest[-1]
-    start_picks(shifts, me_ref, table_ref, cache_ref, outs, sems)
-    wait_picks(shifts, cache_ref, outs, sems)
-
-
-def pick(shifts, me, table, cache):
-    shapes = picked_shapes(shifts, cache.dtype)
-    return pl.pallas_call(
-        functools.partial(pick_kernel, shifts),
+    of_group = lambda g: outs[g * NX : (g + 1) * NX]
+    for g, shifts in enumerate(groups):
+        start_picks(shifts, me_ref, table_ref, cache_ref, of_group(g), sems.at[g])
+    for g, shifts in enumerate(groups):
+        wait_picks(shifts, cache_ref, of_group(g), sems.at[g])
+
+
+def pick(groups, me, table, cache):
+    shapes = [shape for shifts in groups for shape in picked_shapes(shifts, cache.dtype)]
+    outs = pl.pallas_call(
+        functools.partial(pick_kernel, groups),
         out_shape=shapes,
         in_specs=[IN_SMEM, IN_SMEM, IN_HBM],
         out_specs=[IN_HBM] * len(shapes),
-        scratch_shapes=[pltpu.SemaphoreType.DMA((NX - 1,))],
+        scratch_shapes=[pltpu.SemaphoreType.DMA((len(groups), NX))],
         compiler_params=pltpu.CompilerParams(vmem_limit_bytes=VMEM_LIMIT),
         name="pick_blocks",
     )(me, table, cache)
+    return [outs[g * NX : (g + 1) * NX] for g in range(len(groups))]
 
 
 def head_rows(block):
@@ -213,138 +203,95 @@
     return partial_sums([jnp.where(key <= token, scores, NEG_FILL)], [both[:, HD:]])
 
 
-def blocks_here(shifts):
-    return pltpu.VMEM((NX, len(shifts) * CAP, BLK, 2 * HD), jnp.bfloat16)
-
-
-def attend_kernel(shifts, later, with_suffix, *refs):
+def attend_kernel(chunk, shifts, n_after, with_suffix, with_weight, *refs):
     refs = list(refs)
     take = lambda n: [refs.pop(0) for _ in range(n)]
-    me_ref, table_ref, cache_ref, z_query_ref = take(4)
-    arrived = take(NX - 1)
-    own_refs = take(2) if with_suffix else None
+    me_ref, table_ref, z_query_ref = take(3)
+    blocks = take(NX)
+    own_refs = take(2 * with_suffix)
+    take(n_after)
+    weight_ref = take(1)[0] if with_weight else None
     packet_refs = take(len(shifts) + with_suffix)
-    picked = take(NX - 1) if later else []
-    here, query_here, packet_here = take(3)
-    block_sems, query_sems, packet_sems, pick_sems = take(4)
+    wide_ref = take(1)[0] if with_weight else None
+    query_here, query_sems, wide_sems = take(3)
     zo, _ = coordinates(me_ref)
-    start_own_blocks(shifts, me_ref, table_ref, cache_ref, here.at[0], block_sems.at[0])
     fetches = []
     for n, shift in enumerate(shifts):
         start = pl.multiple_of(rem(zo + shift, NZ) * SUF, SUF)
         fetches.append(
             pltpu.make_async_copy(z_query_ref.at[pl.ds(start, SUF), :], query_here.at[n], query_sems.at[n])
         )
-    fetches += [
-        pltpu.make_async_copy(arrived[k - 1], here.at[k], block_sems.at[k]) for k in range(1, NX)
-    ]
-    for fetch in fetches:
-        fetch.start()
-    if later:
-        start_picks(later, me_ref, table_ref, cache_ref, picked, pick_sems)
-    sends = [
-        pltpu.make_async_copy(packet_here.at[n], ref, packet_sems.at[n])
-        for n, ref in enumerate(packet_refs)
-    ]
+        fetches[-1].start()
+    wide = []
+    if with_weight:
+        step = weight_ref.shape[0] // WIDE_PARTS
+        for n in range(WIDE_PARTS):
+            part = pl.ds(n * step, step)
+            wide.append(
+                pltpu.make_async_copy(weight_ref.at[part, :], wide_ref.at[part, :], wide_sems.at[n])
+            )
+            wide[-1].start()
     if with_suffix:
-        last = len(shifts)
         part = suffix_part(head_rows(own_refs[0][...]), own_refs[1][...])
-        write_packet(packet_here.at[last], *part)
-        sends[last].start()
-    for fetch in fetches:
-        fetch.wait()
-    wait_own_blocks(shifts, cache_ref, here.at[0], block_sems.at[0])
+        write_packet(packet_refs[-1], *part)
     for n, shift in enumerate(shifts):
+        fetches[n].wait()
         rows = head_rows(query_here[n])
-        blocks = [here.at[k] for k in range(NX)]
-        write_packet(packet_here.at[n], *cached_part(shift, n, me_ref, table_ref, rows, blocks))
-        sends[n].start()
-    for send in sends:
-        send.wait()
-    if later:
-        wait_picks(later, cache_ref, picked, pick_sems)
-
-
-def attend(shifts, later, me, table, cache, z_queries, arrived, own):
+        part = cached_part(shift, chunk.index(shift), me_ref, table_ref, rows, blocks)
+        write_packet(packet_refs[n], *part)
+    for copy in wide:
+        copy.wait()
+
+
+def attend(chunk, shifts, me, table, z_queries, blocks, own=(), after=(), weight=None):
     keys = len(shifts) * NX * CAP * BLK
-    own = list(own)
-    picked = picked_shapes(later, cache.dtype) if later else []
+    with_weight = weight is not None
     n_packets = len(shifts) + bool(own)
+    extra = list(after) + ([weight] if with_weight else [])
+    wide = [pltpu.VMEM(weight.shape, weight.dtype)] if with_weight else []
     outs = pl.pallas_call(
-        functools.partial(attend_kernel, shifts, later, bool(own)),
-        out_shape=[jax.ShapeDtypeStruct((PACKET, ROWS), jnp.bfloat16)] * n_packets + picked,
-        in_specs=[IN_SMEM] * 2 + [IN_HBM] * (NX + 1) + [IN_VMEM] * len(own),
-        out_specs=[IN_HBM] * (n_packets + len(picked)),
+        functools.partial(attend_kernel, chunk, shifts, len(after), bool(own), with_weight),
+        out_shape=[jax.ShapeDtypeStruct((PACKET, ROWS), jnp.bfloat16)] * n_packets + wide,
+        in_specs=[IN_SMEM] * 2 + [IN_HBM] + [IN_VMEM] * (NX + len(own)) + [IN_HBM] * len(extra),
+        out_specs=[IN_VMEM] * (n_packets + len(wide)),
         scratch_shapes=[
-            blocks_here(shifts),
             pltpu.VMEM((len(shifts), SUF, GROUP * HD), jnp.bfloat16),
-            pltpu.VMEM((n_packets, PACKET, ROWS), jnp.bfloat16),
-            pltpu.SemaphoreType.DMA((NX,)),
             pltpu.SemaphoreType.DMA((len(shifts),)),
-            pltpu.SemaphoreType.DMA((n_packets,)),
-            pltpu.SemaphoreType.DMA((NX - 1,)),
+            pltpu.SemaphoreType.DMA((WIDE_PARTS,)),
         ],
         compiler_params=pltpu.CompilerParams(vmem_limit_bytes=VMEM_LIMIT),
         cost_estimate=pl.CostEstimate(
             flops=4 * keys * ROWS * HD, bytes_accessed=4 * keys * HD, transcendentals=keys * ROWS
         ),
         name="attend_chunk",
-    )(me, table, cache, z_queries, *arrived, *own)
-    return outs[: len(shifts)], outs[len(shifts) : n_packets], outs[n_packets:]
-
-
-def finish_kernel(shifts, me_ref, table_ref, cache_ref, weight_ref, query_ref, *rest):
-    arrived, packet_refs = rest[: NX - 1], rest[NX - 1 : -7]
-    out_ref, here, packet_here, wide, block_sems, packet_sems, wide_sem = rest[-7:]
-    start_own_blocks(shifts, me_ref, table_ref, cache_ref, here.at[0], block_sems.at[0])
-    fetches = [
-        pltpu.make_async_copy(arrived[k - 1], here.at[k], block_sems.at[k]) for k in range(1, NX)
-    ]
-    packets = [
-        pltpu.make_async_copy(ref, packet_here.at[n], packet_sems.at[n])
-        for n, ref in enumerate(packet_refs)
-    ]
-    weight = pltpu.make_async_copy(weight_ref, wide, wide_sem)
-    for copy in fetches + packets + [weight]:
-        copy.start()
-    rows = head_rows(query_ref[...])
-    for fetch in fetches:
-        fetch.wait()
-    wait_own_blocks(shifts, cache_ref, here.at[0], block_sems.at[0])
-    parts = [cached_part(0, 0, me_ref, table_ref, rows, [here.at[k] for k in range(NX)])]
-    for packet in packets:
-        packet.wait()
-    parts += [read_packet(packet_here.at[n]) for n in range(len(packets))]
+    )(me, table, z_queries, *blocks, *own, *extra)
+    return outs[:n_packets], outs[n_packets:]
+
+
+def finish_kernel(wide_ref, *rest):
+    packet_refs, out_ref = rest[:-1], rest[-1]
+    parts = [read_packet(ref) for ref in packet_refs]
     top = functools.reduce(jnp.maximum, [part[0] for part in parts])
     factors = [jnp.exp2(part[0] - top) for part in parts]
     row_sum = sum(f * part[1] for f, part in zip(factors, parts))
     summed = sum(f * part[2] for f, part in zip(factors, parts))
     rows = (summed / row_sum).T.astype(jnp.bfloat16)
     attended = jnp.concatenate([rows[i * SUF : (i + 1) * SUF] for i in range(GROUP)], axis=1)
-    weight.wait()
-    out_ref[...] = jnp.dot(attended, wide[...], preferred_element_type=jnp.float32).astype(jnp.bfloat16)
-
-
-def finish(shifts, me, table, cache, weight, queries, arrived, packets):
+    out_ref[...] = jnp.dot(
+        attended, wide_ref[...], preferred_element_type=jnp.float32
+    ).astype(jnp.bfloat16)
+
+
+def finish(wide, packets):
     return pl.pallas_call(
-        functools.partial(finish_kernel, shifts),
-        out_shape=jax.ShapeDtypeStruct((SUF, weight.shape[1]), jnp.bfloat16),
-        in_specs=[IN_SMEM] * 2 + [IN_HBM] * 2 + [IN_VMEM] + [IN_HBM] * (NX - 1 + len(packets)),
-        out_specs=IN_VMEM,
-        scratch_shapes=[
-            blocks_here(shifts),
-            pltpu.VMEM((len(packets), PACKET, ROWS), jnp.bfloat16),
-            pltpu.VMEM(weight.shape, weight.dtype),
-            pltpu.SemaphoreType.DMA((NX,)),
-            pltpu.SemaphoreType.DMA((len(packets),)),
-            pltpu.SemaphoreType.DMA,
-        ],
+        finish_kernel,
+        out_shape=jax.ShapeDtypeStruct((SUF, wide.shape[1]), jnp.bfloat16),
         compiler_params=pltpu.CompilerParams(vmem_limit_bytes=VMEM_LIMIT),
         cost_estimate=pl.CostEstimate(
-            flops=2 * SUF * weight.size, bytes_accessed=2 * weight.size, transcendentals=0
+            flops=2 * SUF * wide.size, bytes_accessed=2 * wide.size, transcendentals=0
         ),
         name="merge_project",
-    )(me, table, cache, weight, queries, *arrived, *packets)
+    )(wide, *packets)
 
 
 def x_permute(a, step):
@@ -390,17 +337,20 @@
     z_queries = keep_in_hbm(z_queries)
     cache = keep_in_hbm(kv_cache.reshape(kv_cache.shape[0], BLK, 2 * HD))
     suffix = suffix_kv.reshape(SUF, 2 * HD)
-    picked = [pick(shifts, me, table, cache) for shifts in CHUNKS[:AHEAD]]
-    packets = []
-    for g, shifts in enumerate(CHUNKS[:-1]):
-        arrived = [x_permute(a, k) for k, a in enumerate(picked[g], 1)]
-        later = CHUNKS[g + AHEAD] if g + AHEAD < len(CHUNKS) else ()
-        own = () if g else (queries, suffix)
-        mine, own, more = attend(shifts, later, me, table, cache, z_queries, arrived, own)
-        packets += [z_permute(packet, s) for s, packet in zip(shifts, mine)] + list(own)
-        picked.append(more)
-    arrived = [x_permute(a, k) for k, a in enumerate(picked[len(CHUNKS) - 1], 1)]
-    return sum_heads(finish(CHUNKS[-1], me, table, cache, keep_in_hbm(out_weight), queries, arrived, packets))
+    far, near = CHUNKS
+    away = near[:-1]
+    far_picked, near_picked = pick(CHUNKS, me, table, cache)
+    over_x = lambda blocks: [blocks[0]] + [x_permute(blocks[k], k) for k in range(1, NX)]
+    over_z = lambda shifts, parts: [z_permute(part, s) for s, part in zip(shifts, parts)]
+    far_blocks, near_blocks = over_x(far_picked), over_x(near_picked)
+    parts, _ = attend(far, far, me, table, z_queries, far_blocks, own=(queries, suffix))
+    packets = over_z(far, parts) + [parts[-1]]
+    parts, _ = attend(near, away, me, table, z_queries, near_blocks, after=packets[:2])
+    packets += over_z(away, parts)
+    home, (wide,) = attend(
+        near, near[-1:], me, table, z_queries, near_blocks, after=parts[:1], weight=keep_in_hbm(out_weight)
+    )
+    return sum_heads(finish(wide, packets + list(home)))
 
 
 def solution(mesh):

time: 140 us -> 167 us (1.19)
  waiting for transfers between devices: 34.8 us -> 52 us
  local copies, waits for them, and re-layouts: 1.37 us -> 10.4 us
  starting transfers between devices: 37.9 us -> 34.1 us
  Pallas kernels: 50.9 us -> 54.4 us
    ppermute x9 -> x6, waiting for transfers between devices: 3.25 us -> 21.9 us  [x_permute(): return lax.ppermute(a, 'store', pairs)]
    unnamed x8 -> x24, local copies, waits for them, and re-layouts: 1.31 us -> 10.3 us
    ppermute x9 -> x6, starting transfers between devices: 12.5 us -> 6.17 us  [x_permute(): return lax.ppermute(a, 'store', pairs)]
    pallas_call x5, Pallas kernels: 50 us -> 53.5 us  [the longest x1 34.1 us: pick(): pl.pallas_call(functools.partial(pick_kernel, groups), out_shape=shapes,...]
    ppermute x7, starting transfers between devices: 10.5 us -> 13 us  [z_permute(): return lax.ppermute(a, 'store', pairs)]
  transfers between devices with their start and end apart: 22 -> 19, of which waited for: 8 -> 8; matrix products, arithmetic and copies ran while one was open for 0% -> 0% of each run, Pallas kernels for 30% -> 32%
where the time goes in v3:
time: 167 us; the launch traced here: 166 us
  Pallas kernels  54.4 us (33%)
  waiting for transfers between devices  52 us (31%)
  starting transfers between devices  34.1 us (20%)
  between operations  14.2 us (9%)
  local copies, waits for them, and re-layouts  10.4 us (6%)
    pallas_call x1, Pallas kernels, pick(): pl.pallas_call(functools.partial(pick_kernel, groups), out_shape=shapes,...  34.1 us
    ppermute x6, waiting for transfers between devices, x_permute(): return lax.ppermute(a, 'store', pairs)  21.9 us
    pallas_call x3, Pallas kernels, attend(): pl.pallas_call(functools.partial(attend_kernel, chunk, shifts, len(after)...  17.5 us
    ppermute x7, starting transfers between devices, z_permute(): return lax.ppermute(a, 'store', pairs)  13 us
    ppermute x7, waiting for transfers between devices, z_permute(): return lax.ppermute(a, 'store', pairs)  12.6 us
    all_to_all x1, starting transfers between devices, local(): lax.all_to_all(wanted, 'store', split_axis=0, concat_axis=0, tiled=True)  11.3 us
    unnamed x24, local copies, waits for them, and re-layouts  10.3 us
    all_to_all x1, waiting for transfers between devices, local(): lax.all_to_all(wanted, 'store', split_axis=0, concat_axis=0, tiled=True)  9.76 us
  transfers between devices with their start and end apart: 19, of which 8 were waited for; matrix products, arithmetic and copies ran while one was open for 0% of the time, Pallas kernels for 32%

profile of v3, /device:TPU:24, one launch (start us, length us, event | category | flops | bytes accessed | tf_op | source)
XLA Modules:
  0.0 165.8 jit_solution(3705069573717271347)
XLA Ops:
  10.1 11.3 %all-to-all-start = ((s32[32,1,128]{2,1,0:T(1,128)}), s32[32,1,128]{2,1,0:T(1,128)S(1)}, u32[]{:S(2)}, u32[]{:S(2)}) async-start(s32[32,1,128]{2,1,0:T(1,128)} %wanted_slots.1), calls=%async_computation | async-start | bytes 32768 | tf_op jit(solution)/shard_map/all_to_all | solution.py:334
  21.5 9.8 %all-to-all-done.table_ref.refs_1_ = s32[32,1,128]{2,1,0:T(1,128)S(1)} async-done(((s32[32,1,128]{2,1,0:T(1,128)}), s32[32,1,128]{2,1,0:T(1,128)S(1)}, u32[]{:S(2)}, u32[]{:S(2)}) %all-to-all-start) | async-done | bytes 16416 | tf_op jit(solution)/shard_map/all_to_all | solution.py:334
  31.2 34.1 %pick_blocks.1 = (bf16[16,64,256]{2,1,0:T(8,128)(2,1)S(1)}, bf16[16,64,256]{2,1,0:T(8,128)(2,1)S(1)}, bf16[16,64,256]{2,1,0:T(8,128)(2,1)S(1)}, bf16[16,64,256]{...) custom-call(s32[1]{0:T(128)} %bitcast.me_ref.refs_0_, ...), custom_call_target="tpu_custom_call" | custom-call | tf_op jit(solution)/shard_map/pick_blocks/pallas_call | solution.py:133
  66.7 2.2 %collective-permute-start.4 = (bf16[16,64,256]{2,1,0:T(8,128)(2,1)S(1)}, bf16[16,64,256]{2,1,0:T(8,128)(2,1)S(1)}, u32[]{:S(2)}, u32[]{:S(2)}) collective-permute-start(bf16[16,64,256]{2,1,0:T(8,128)(2,1)S(1)} %get-tuple-element.29), channel_id=1, source_target_pairs={{0,16},{8,24},{16,0},{24,8},{32,48},{40,56},{48,32},{56,40},{64,80... | collective-permute-start | bytes 1572872 | tf_op jit(solution)/shard_map/ppermute | solution.py:299
  68.9 1.2 collective-permute-start.5
  70.9 1.4 collective-permute-start.1
  72.3 21.1 %collective-permute-done.3.refs_4_ = bf16[16,64,256]{2,1,0:T(8,128)(2,1)S(1)} collective-permute-done((bf16[16,64,256]{2,1,0:T(8,128)(2,1)S(1)}, bf16[16,64,256]{2,1,0:T(8,128)(2,1)S(1)}, u32[]{:S(2)}, u32[]{:S(2)}) %collective-permute-start.3) | collective-permute-done | bytes 524320 | tf_op jit(solution)/shard_map/ppermute | solution.py:299
  97.8 1.0 copy-done.6
  98.8 1.0 copy-done.8
  101.7 6.7 %attend_chunk.3 = (bf16[144,512]{1,0:T(8,128)(2,1)S(1)}, bf16[144,512]{1,0:T(8,128)(2,1)S(1)}, bf16[144,512]{1,0:T(8,128)(2,1)}, bf16[144,512]{1,0:T(8,128)(2,1)}, bf16[144,512]{1,0:T(8,128)(2,1)S(1)}) custom-call(s32[1]{0:T(128)} %bitcast.me_ref.refs_0_, s32[32,1,128]{2,1,0:T(1,128)S(1)} %all-to-all-done.table_ref.refs_1_, ...), custom_call_target="tpu_custom_call" | custom-call | flops 1073741824 | bytes 2097152 | tf_op jit(solution)/shard_map/attend_chunk/pallas_call | solution.py:252
  109.0 3.4 %collective-permute-start.7 = (bf16[144,512]{1,0:T(8,128)(2,1)S(1)}, bf16[144,512]{1,0:T(8,128)(2,1)S(1)}, u32[]{:S(2)}, u32[]{:S(2)}) collective-permute-start(bf16[144,512]{1,0:T(8,128)(2,1)S(1)} %get-tuple-element.32), channel_id=1, source_target_pairs={{0,96},{8,104},{16,112},{24,120},{32,128},{40,136},{48,144},{56,15... | collective-permute-start | bytes 442376 | tf_op jit(solution)/shard_map/ppermute | solution.py:304
  114.1 2.4 %collective-permute-start.9 = (bf16[144,512]{1,0:T(8,128)(2,1)}, bf16[144,512]{1,0:T(8,128)(2,1)S(1)}, u32[]{:S(2)}, u32[]{:S(2)}) collective-permute-start(bf16[144,512]{1,0:T(8,128)(2,1)} %get-tuple-element.36), channel_id=1, source_target_pairs={{0,64},{8,72},{16,80},{24,88},{32,96},{40,104},{48,112},{56,120},{... | collective-permute-start | bytes 442376 | tf_op jit(solution)/shard_map/ppermute | solution.py:304
  116.5 7.5 %collective-permute-done.6.refs_7_.rest_0_ = bf16[144,512]{1,0:T(8,128)(2,1)S(1)} collective-permute-done((bf16[144,512]{1,0:T(8,128)(2,1)S(1)}, bf16[144,512]{1,0:T(8,128)(2,1)S(1)}, u32[]{:S(2)}, u32[]{:S(2)}) %collective-permute-start.6) | collective-permute-done | bytes 147488 | tf_op jit(solution)/shard_map/ppermute | solution.py:304
  123.9 5.1 %collective-permute-done.7.refs_8_.rest_1_ = bf16[144,512]{1,0:T(8,128)(2,1)S(1)} collective-permute-done((bf16[144,512]{1,0:T(8,128)(2,1)S(1)}, bf16[144,512]{1,0:T(8,128)(2,1)S(1)}, u32[]{:S(2)}, u32[]{:S(2)}) %collective-permute-start.7) | collective-permute-done | bytes 147488 | tf_op jit(solution)/shard_map/ppermute | solution.py:304
  129.1 5.6 %attend_chunk.4 = (bf16[144,512]{1,0:T(8,128)(2,1)S(1)}, bf16[144,512]{1,0:T(8,128)(2,1)}, bf16[144,512]{1,0:T(8,128)(2,1)}) custom-call(s32[1]{0:T(128)} %bitcast.me_ref.refs_0_, s32[32,1,128]{2,1,0:T(1,128)S(1)} %all-to-all-done.table_ref.refs_1_, bf16[512,1024]{1,0:T(8,128)(2,1)} %all-gather.2.cloned.1.call-done.refs_2_, ...), custom_call_target="tpu_custom_call" | custom-call | flops 805306368 | bytes 1572864 | tf_op jit(solution)/shard_map/attend_chunk/pallas_call | solution.py:252
  134.6 3.7 %collective-permute-start.10 = (bf16[144,512]{1,0:T(8,128)(2,1)S(1)}, bf16[144,512]{1,0:T(8,128)(2,1)S(1)}, u32[]{:S(2)}, u32[]{:S(2)}) collective-permute-start(bf16[144,512]{1,0:T(8,128)(2,1)S(1)} %get-tuple-element.33.refs_7_), channel_id=1, source_target_pairs={{0,192},{8,200},{16,208},{24,216},{32,224},{40,232},{48,240},{56,2... | collective-permute-start | bytes 442376 | tf_op jit(solution)/shard_map/ppermute | solution.py:304
  138.3 2.0 %collective-permute-start.12 = (bf16[144,512]{1,0:T(8,128)(2,1)}, bf16[144,512]{1,0:T(8,128)(2,1)S(1)}, u32[]{:S(2)}, u32[]{:S(2)}) collective-permute-start(bf16[144,512]{1,0:T(8,128)(2,1)} %get-tuple-element.39), channel_id=1, source_target_pairs={{0,32},{8,40},{16,48},{24,56},{32,64},{40,72},{48,80},{56,88},{64,... | collective-permute-start | bytes 442376 | tf_op jit(solution)/shard_map/ppermute | solution.py:304
  140.3 5.3 %attend_chunk.5 = (bf16[144,512]{1,0:T(8,128)(2,1)S(1)}, bf16[1024,4096]{1,0:T(8,128)(2,1)S(1)}) custom-call(s32[1]{0:T(128)} %bitcast.me_ref.refs_0_, s32[32,1,128]{2,1,0:T(1,128)S(1)} %all-to-all-done.table_ref.refs_1_, bf16[512,1024]{1,0:T(8,128)(2,1)} %all-gather.2.cloned.1.call-done.refs_2_, bf16[16,64,256]{2,1,0:T(8,128)(2,1)S(1)} %get-tuple-element.23.refs_3_, ...), custom_call_target="tpu_custom_call" | custom-call | flops 268435456 | bytes 524288 | tf_op jit(solution)/shard_map/attend_chunk/pallas_call | solution.py:252
  145.7 1.9 %merge_project.1 = bf16[64,4096]{1,0:T(8,128)(2,1)S(1)} custom-call(bf16[1024,4096]{1,0:T(8,128)(2,1)S(1)} %get-tuple-element.34.wide_ref, bf16[144,512]{1,0:T(8,128)(2,1)S(1)} %collective-permute-done.6.refs_7_.rest_0_, bf16[144,512]{1,0:T(8,128)(2,1)S(1)} %collective-permute-done.7.refs_8_.rest_1_, bf16[144,512]{1,0:T(8,128)(2,1)S(1)} %collective-permute-done.8.rest_2_, ...), custom_call_target="tpu_custom_call" | custom-call | flops 536870912 | bytes 8388608 | tf_op jit(solution)/shard_map/merge_project/pallas_call | solution.py:286
  147.7 1.5 collective-permute-done.13
  149.3 1.2 collective-permute-start.14
  150.5 2.3 %collective-permute-start.15 = (bf16[8,4096]{1,0:T(8,128)(2,1)S(1)}, bf16[8,4096]{1,0:T(8,128)(2,1)S(1)}, u32[]{:S(2)}, u32[]{:S(2)}) collective-permute-start(bf16[8,4096]{1,0:T(8,128)(2,1)S(1)} %get-tuple-element.43), channel_id=1, source_target_pairs={{0,2},{1,3},{2,4},{3,5},{4,6},{5,7},{6,0},{7,1},{8,10},{9,11},{10,... | collective-permute-start | bytes 196616 | tf_op jit(solution)/shard_map/ppermute | solution.py:311
  152.8 2.5 %collective-permute-done.14 = bf16[8,4096]{1,0:T(8,128)(2,1)S(1)} collective-permute-done((bf16[8,4096]{1,0:T(8,128)(2,1)S(1)}, bf16[8,4096]{1,0:T(8,128)(2,1)S(1)}, u32[]{:S(2)}, u32[]{:S(2)}) %collective-permute-start.14) | collective-permute-done | bytes 65568 | tf_op jit(solution)/shard_map/ppermute | solution.py:311
  155.3 3.0 %collective-permute-done.16 = bf16[8,4096]{1,0:T(8,128)(2,1)S(1)} collective-permute-done((bf16[8,4096]{1,0:T(8,128)(2,1)S(1)}, bf16[8,4096]{1,0:T(8,128)(2,1)S(1)}, u32[]{:S(2)}, u32[]{:S(2)}) %collective-permute-start.16) | collective-permute-done | bytes 65568 | tf_op jit(solution)/shard_map/ppermute | solution.py:311
  (49 shorter events, 14.5 us)
Async XLA Ops:
  6.5 89.3 %all-gather.2.cloned.1.call-start = ((), (), s32[]{:S(2)}) async-start(), calls=%async_computation.1 | async-start | bytes 1179648 | tf_op jit(solution)/shard_map/all_gather | solution.py:336
  10.1 21.1 %all-to-all-start = ((s32[32,1,128]{2,1,0:T(1,128)}), s32[32,1,128]{2,1,0:T(1,128)S(1)}, u32[]{:S(2)}, u32[]{:S(2)}) async-start(s32[32,1,128]{2,1,0:T(1,128)} %wanted_slots.1), calls=%async_computation | async-start | bytes 32768 | tf_op jit(solution)/shard_map/all_to_all | solution.py:334
  66.1 27.3 %collective-permute-start.3 = (bf16[16,64,256]{2,1,0:T(8,128)(2,1)S(1)}, bf16[16,64,256]{2,1,0:T(8,128)(2,1)S(1)}, u32[]{:S(2)}, u32[]{:S(2)}) collective-permute-start(bf16[16,64,256]{2,1,0:T(8,128)(2,1)S(1)} %get-tuple-element.28), channel_id=1, source_target_pairs={{0,8},{8,16},{16,24},{24,0},{32,40},{40,48},{48,56},{56,32},{64,72... | collective-permute-start | bytes 1572872 | tf_op jit(solution)/shard_map/ppermute | solution.py:299
  66.7 27.5 %collective-permute-start.4 = (bf16[16,64,256]{2,1,0:T(8,128)(2,1)S(1)}, bf16[16,64,256]{2,1,0:T(8,128)(2,1)S(1)}, u32[]{:S(2)}, u32[]{:S(2)}) collective-permute-start(bf16[16,64,256]{2,1,0:T(8,128)(2,1)S(1)} %get-tuple-element.29), channel_id=1, source_target_pairs={{0,16},{8,24},{16,0},{24,8},{32,48},{40,56},{48,32},{56,40},{64,80... | collective-permute-start | bytes 1572872 | tf_op jit(solution)/shard_map/ppermute | solution.py:299
  68.9 26.2 %collective-permute-start.5 = (bf16[16,64,256]{2,1,0:T(8,128)(2,1)S(1)}, bf16[16,64,256]{2,1,0:T(8,128)(2,1)S(1)}, u32[]{:S(2)}, u32[]{:S(2)}) collective-permute-start(bf16[16,64,256]{2,1,0:T(8,128)(2,1)S(1)} %get-tuple-element.30), channel_id=1, source_target_pairs={{0,24},{8,0},{16,8},{24,16},{32,56},{40,32},{48,40},{56,48},{64,88... | collective-permute-start | bytes 1572872 | tf_op jit(solution)/shard_map/ppermute | solution.py:299
  70.1 43.1 %collective-permute-start = (bf16[16,64,256]{2,1,0:T(8,128)(2,1)}, bf16[16,64,256]{2,1,0:T(8,128)(2,1)S(1)}, u32[]{:S(2)}, u32[]{:S(2)}) collective-permute-start(bf16[16,64,256]{2,1,0:T(8,128)(2,1)} %get-tuple-element.24), channel_id=1, source_target_pairs={{0,8},{8,16},{16,24},{24,0},{32,40},{40,48},{48,56},{56,32},{64,72... | collective-permute-start | bytes 1572872 | tf_op jit(solution)/shard_map/ppermute | solution.py:299
  70.9 43.1 %collective-permute-start.1 = (bf16[16,64,256]{2,1,0:T(8,128)(2,1)}, bf16[16,64,256]{2,1,0:T(8,128)(2,1)S(1)}, u32[]{:S(2)}, u32[]{:S(2)}) collective-permute-start(bf16[16,64,256]{2,1,0:T(8,128)(2,1)} %get-tuple-element.25), channel_id=1, source_target_pairs={{0,16},{8,24},{16,0},{24,8},{32,48},{40,56},{48,32},{56,40},{64,80... | collective-permute-start | bytes 1572872 | tf_op jit(solution)/shard_map/ppermute | solution.py:299
  94.2 22.2 %collective-permute-start.2 = (bf16[16,64,256]{2,1,0:T(8,128)(2,1)S(1)}, bf16[16,64,256]{2,1,0:T(8,128)(2,1)S(1)}, u32[]{:S(2)}, u32[]{:S(2)}) collective-permute-start(bf16[16,64,256]{2,1,0:T(8,128)(2,1)S(1)} %get-tuple-element.26), channel_id=1, source_target_pairs={{0,24},{8,0},{16,8},{24,16},{32,56},{40,32},{48,40},{56,48},{64,88... | collective-permute-start | bytes 1572872 | tf_op jit(solution)/shard_map/ppermute | solution.py:299
  95.8 0.9 copy-start
  96.7 1.0 copy-start.4
  97.8 1.0 copy-start.6
  98.8 1.0 copy-start.8
  99.9 1.0 copy-start.10
  108.3 15.6 %collective-permute-start.6 = (bf16[144,512]{1,0:T(8,128)(2,1)S(1)}, bf16[144,512]{1,0:T(8,128)(2,1)S(1)}, u32[]{:S(2)}, u32[]{:S(2)}) collective-permute-start(bf16[144,512]{1,0:T(8,128)(2,1)S(1)} %get-tuple-element.31), channel_id=1, source_target_pairs={{0,128},{8,136},{16,144},{24,152},{32,160},{40,168},{48,176},{56,1... | collective-permute-start | bytes 442376 | tf_op jit(solution)/shard_map/ppermute | solution.py:304
  109.0 20.0 %collective-permute-start.7 = (bf16[144,512]{1,0:T(8,128)(2,1)S(1)}, bf16[144,512]{1,0:T(8,128)(2,1)S(1)}, u32[]{:S(2)}, u32[]{:S(2)}) collective-permute-start(bf16[144,512]{1,0:T(8,128)(2,1)S(1)} %get-tuple-element.32), channel_id=1, source_target_pairs={{0,96},{8,104},{16,112},{24,120},{32,128},{40,136},{48,144},{56,15... | collective-permute-start | bytes 442376 | tf_op jit(solution)/shard_map/ppermute | solution.py:304
  113.2 32.5 %collective-permute-start.8 = (bf16[144,512]{1,0:T(8,128)(2,1)}, bf16[144,512]{1,0:T(8,128)(2,1)S(1)}, u32[]{:S(2)}, u32[]{:S(2)}) collective-permute-start(bf16[144,512]{1,0:T(8,128)(2,1)} %get-tuple-element.35), channel_id=1, source_target_pairs={{0,160},{8,168},{16,176},{24,184},{32,192},{40,200},{48,208},{56,2... | collective-permute-start | bytes 442376 | tf_op jit(solution)/shard_map/ppermute | solution.py:304
  114.1 31.6 %collective-permute-start.9 = (bf16[144,512]{1,0:T(8,128)(2,1)}, bf16[144,512]{1,0:T(8,128)(2,1)S(1)}, u32[]{:S(2)}, u32[]{:S(2)}) collective-permute-start(bf16[144,512]{1,0:T(8,128)(2,1)} %get-tuple-element.36), channel_id=1, source_target_pairs={{0,64},{8,72},{16,80},{24,88},{32,96},{40,104},{48,112},{56,120},{... | collective-permute-start | bytes 442376 | tf_op jit(solution)/shard_map/ppermute | solution.py:304
  134.6 11.0 %collective-permute-start.10 = (bf16[144,512]{1,0:T(8,128)(2,1)S(1)}, bf16[144,512]{1,0:T(8,128)(2,1)S(1)}, u32[]{:S(2)}, u32[]{:S(2)}) collective-permute-start(bf16[144,512]{1,0:T(8,128)(2,1)S(1)} %get-tuple-element.33.refs_7_), channel_id=1, source_target_pairs={{0,192},{8,200},{16,208},{24,216},{32,224},{40,232},{48,240},{56,2... | collective-permute-start | bytes 442376 | tf_op jit(solution)/shard_map/ppermute | solution.py:304
  138.3 7.4 %collective-permute-start.11 = (bf16[144,512]{1,0:T(8,128)(2,1)}, bf16[144,512]{1,0:T(8,128)(2,1)S(1)}, u32[]{:S(2)}, u32[]{:S(2)}) collective-permute-start(bf16[144,512]{1,0:T(8,128)(2,1)} %get-tuple-element.38), channel_id=1, source_target_pairs={{0,224},{8,232},{16,240},{24,248},{32,0},{40,8},{48,16},{56,24},{6... | collective-permute-start | bytes 442376 | tf_op jit(solution)/shard_map/ppermute | solution.py:304
  138.3 7.4 %collective-permute-start.12 = (bf16[144,512]{1,0:T(8,128)(2,1)}, bf16[144,512]{1,0:T(8,128)(2,1)S(1)}, u32[]{:S(2)}, u32[]{:S(2)}) collective-permute-start(bf16[144,512]{1,0:T(8,128)(2,1)} %get-tuple-element.39), channel_id=1, source_target_pairs={{0,32},{8,40},{16,48},{24,56},{32,64},{40,72},{48,80},{56,88},{64,... | collective-permute-start | bytes 442376 | tf_op jit(solution)/shard_map/ppermute | solution.py:304
  147.6 1.6 collective-permute-start.13
  149.3 6.0 %collective-permute-start.14 = (bf16[8,4096]{1,0:T(8,128)(2,1)S(1)}, bf16[8,4096]{1,0:T(8,128)(2,1)S(1)}, u32[]{:S(2)}, u32[]{:S(2)}) collective-permute-start(bf16[8,4096]{1,0:T(8,128)(2,1)S(1)} %get-tuple-element.41), channel_id=1, source_target_pairs={{0,4},{1,5},{2,6},{3,7},{4,0},{5,1},{6,2},{7,3},{8,12},{9,13},{10,... | collective-permute-start | bytes 196616 | tf_op jit(solution)/shard_map/ppermute | solution.py:311
  150.5 4.8 %collective-permute-start.15 = (bf16[8,4096]{1,0:T(8,128)(2,1)S(1)}, bf16[8,4096]{1,0:T(8,128)(2,1)S(1)}, u32[]{:S(2)}, u32[]{:S(2)}) collective-permute-start(bf16[8,4096]{1,0:T(8,128)(2,1)S(1)} %get-tuple-element.43), channel_id=1, source_target_pairs={{0,2},{1,3},{2,4},{3,5},{4,6},{5,7},{6,0},{7,1},{8,10},{9,11},{10,... | collective-permute-start | bytes 196616 | tf_op jit(solution)/shard_map/ppermute | solution.py:311
  152.8 5.5 %collective-permute-start.16 = (bf16[8,4096]{1,0:T(8,128)(2,1)S(1)}, bf16[8,4096]{1,0:T(8,128)(2,1)S(1)}, u32[]{:S(2)}, u32[]{:S(2)}) collective-permute-start(bf16[8,4096]{1,0:T(8,128)(2,1)S(1)} %get-tuple-element.42), channel_id=1, source_target_pairs={{0,6},{1,7},{2,0},{3,1},{4,2},{5,3},{6,4},{7,5},{8,14},{9,15},{10,... | collective-permute-start | bytes 196616 | tf_op jit(solution)/shard_map/ppermute | solution.py:311
  (7 other events, 5.3 us)
Sparse Core Ops, SparseCore 0:
  9.1 41.1 all-gather.1

commit v4 on v3

--- a/solution.py
+++ b/solution.py
@@ -27,7 +27,7 @@
 TO_LOG2 = math.log2(math.e) / math.sqrt(HD)
 CHUNKS = ((4, 3, 5, 2), (6, 7, 1, 0))
 WIDE_PARTS = 8
-VMEM_LIMIT = 40 * 1024 * 1024
+VMEM_LIMIT = 24 * 1024 * 1024
 
 CONTRACT_LAST = (((1,), (1,)), ((), ()))
 CONTRACT_FIRST = (((0,), (0,)), ((), ()))
@@ -94,52 +94,37 @@
     return jnp.clip(table_ref[home, 0, owner * CAP + c], 0, cache_ref.shape[0] - 1)
 
 
-def start_picks(shifts, me_ref, table_ref, cache_ref, outs, sems):
+def pick_kernel(wanted, me_ref, table_ref, cache_ref, *rest):
+    outs, sems = rest[:-1], rest[-1]
     zo, xo = coordinates(me_ref)
-    for k in range(NX):
+    for m, (shifts, k) in enumerate(wanted):
         for n, shift in enumerate(shifts):
             home = rem(zo + shift, NZ) * NX + rem(xo + k, NX)
             for c in range(CAP):
                 slot = slot_of(table_ref, home, me_ref[0], c, cache_ref)
                 pltpu.make_async_copy(
                     cache_ref.at[pl.ds(slot, 1)],
-                    outs[k].at[pl.ds(n * CAP + c, 1)],
-                    sems.at[k],
+                    outs[m].at[pl.ds(n * CAP + c, 1)],
+                    sems.at[m],
                 ).start()
-
-
-def wait_picks(shifts, cache_ref, outs, sems):
-    for k in range(NX):
+    for m, (shifts, k) in enumerate(wanted):
         pltpu.make_async_copy(
-            cache_ref.at[pl.ds(0, len(shifts) * CAP)], outs[k], sems.at[k]
+            cache_ref.at[pl.ds(0, len(shifts) * CAP)], outs[m], sems.at[m]
         ).wait()
 
 
-def picked_shapes(shifts, dtype):
-    return [jax.ShapeDtypeStruct((len(shifts) * CAP, BLK, 2 * HD), dtype)] * NX
-
-
-def pick_kernel(groups, me_ref, table_ref, cache_ref, *rest):
-    outs, sems = rest[:-1], rest[-1]
-    of_group = lambda g: outs[g * NX : (g + 1) * NX]
-    for g, shifts in enumerate(groups):
-        start_picks(shifts, me_ref, table_ref, cache_ref, of_group(g), sems.at[g])
-    for g, shifts in enumerate(groups):
-        wait_picks(shifts, cache_ref, of_group(g), sems.at[g])
-
-
-def pick(groups, me, table, cache):
-    shapes = [shape for shifts in groups for shape in picked_shapes(shifts, cache.dtype)]
-    outs = pl.pallas_call(
-        functools.partial(pick_kernel, groups),
-        out_shape=shapes,
+def pick(wanted, me, table, cache):
+    return pl.pallas_call(
+        functools.partial(pick_kernel, wanted),
+        out_shape=[
+            pltpu.VMEM((len(shifts) * CAP, BLK, 2 * HD), cache.dtype) for shifts, k in wanted
+        ],
         in_specs=[IN_SMEM, IN_SMEM, IN_HBM],
-        out_specs=[IN_HBM] * len(shapes),
-        scratch_shapes=[pltpu.SemaphoreType.DMA((len(groups), NX))],
+        out_specs=[IN_VMEM] * len(wanted),
+        scratch_shapes=[pltpu.SemaphoreType.DMA((len(wanted),))],
         compiler_params=pltpu.CompilerParams(vmem_limit_bytes=VMEM_LIMIT),
         name="pick_blocks",
     )(me, table, cache)
-    return [outs[g * NX : (g + 1) * NX] for g in range(len(groups))]
 
 
 def head_rows(block):
@@ -339,13 +324,17 @@
     suffix = suffix_kv.reshape(SUF, 2 * HD)
     far, near = CHUNKS
     away = near[:-1]
-    far_picked, near_picked = pick(CHUNKS, me, table, cache)
-    over_x = lambda blocks: [blocks[0]] + [x_permute(blocks[k], k) for k in range(1, NX)]
+    steps = range(1, NX)
+    far_sent = pick([(far, k) for k in steps], me, table, cache)
+    *near_sent, far_here, near_here = pick(
+        [(near, k) for k in steps] + [(far, 0), (near, 0)], me, table, cache
+    )
+    over_x = lambda blocks: [x_permute(block, k) for k, block in zip(steps, blocks)]
     over_z = lambda shifts, parts: [z_permute(part, s) for s, part in zip(shifts, parts)]
-    far_blocks, near_blocks = over_x(far_picked), over_x(near_picked)
+    far_blocks, near_blocks = [far_here] + over_x(far_sent), [near_here] + over_x(near_sent)
     parts, _ = attend(far, far, me, table, z_queries, far_blocks, own=(queries, suffix))
     packets = over_z(far, parts) + [parts[-1]]
-    parts, _ = attend(near, away, me, table, z_queries, near_blocks, after=packets[:2])
+    parts, _ = attend(near, away, me, table, z_queries, near_blocks, after=packets[:1])
     packets += over_z(away, parts)
     home, (wide,) = attend(
         near, near[-1:], me, table, z_queries, near_blocks, after=parts[:1], weight=keep_in_hbm(out_weight)

time: 167 us -> 126 us (0.75)
  Pallas kernels: 54.4 us -> 27.3 us
  waiting for transfers between devices: 52 us -> 41.6 us
  starting transfers between devices: 34.1 us -> 30.7 us
  local copies, waits for them, and re-layouts: 10.4 us -> 8.7 us
    pallas_call x1 -> x2, Pallas kernels: 34.1 us -> 7.01 us  [pick(): pl.pallas_call(functools.partial(pick_kernel, wanted), out_shape=[pltpu.V...]
    ppermute x7, waiting for transfers between devices: 12.6 us -> 6.01 us  [z_permute(): return lax.ppermute(a, 'store', pairs)]
    ppermute x6, waiting for transfers between devices: 21.9 us -> 18.2 us  [x_permute(): return lax.ppermute(a, 'store', pairs)]
    ppermute x7, starting transfers between devices: 13 us -> 9.88 us  [z_permute(): return lax.ppermute(a, 'store', pairs)]
    unnamed x24, local copies, waits for them, and re-layouts: 10.3 us -> 8.64 us
  transfers between devices with their start and end apart: 19 -> 19, of which waited for: 8 -> 7; matrix products, arithmetic and copies ran while one was open for 0% -> 0% of each run, Pallas kernels for 32% -> 21%
where the time goes in v4:
time: 126 us; the launch traced here: 123 us
  waiting for transfers between devices  41.6 us (33%)
  starting transfers between devices  30.7 us (24%)
  Pallas kernels  27.3 us (22%)
  between operations  14.3 us (11%)
  local copies, waits for them, and re-layouts  8.7 us (7%)
    ppermute x6, waiting for transfers between devices, x_permute(): return lax.ppermute(a, 'store', pairs)  18.2 us
    pallas_call x3, Pallas kernels, attend(): pl.pallas_call(functools.partial(attend_kernel, chunk, shifts, len(after)...  17.5 us
    all_to_all x1, starting transfers between devices, local(): lax.all_to_all(wanted, 'store', split_axis=0, concat_axis=0, tiled=True)  11.3 us
    ppermute x7, starting transfers between devices, z_permute(): return lax.ppermute(a, 'store', pairs)  9.88 us
    all_to_all x1, waiting for transfers between devices, local(): lax.all_to_all(wanted, 'store', split_axis=0, concat_axis=0, tiled=True)  9.76 us
    unnamed x24, local copies, waits for them, and re-layouts  8.64 us
    pallas_call x2, Pallas kernels, pick(): pl.pallas_call(functools.partial(pick_kernel, wanted), out_shape=[pltpu.V...  7.01 us
    ppermute x6, starting transfers between devices, x_permute(): return lax.ppermute(a, 'store', pairs)  6.19 us
  transfers between devices with their start and end apart: 19, of which 7 were waited for; matrix products, arithmetic and copies ran while one was open for 0% of the time, Pallas kernels for 21%

profile of v4, /device:TPU:24, one launch (start us, length us, event | category | flops | bytes accessed | tf_op | source)
XLA Modules:
  0.0 123.3 jit_solution(11939956585338597885)
XLA Ops:
  10.1 11.3 %all-to-all-start = ((s32[32,1,128]{2,1,0:T(1,128)}), s32[32,1,128]{2,1,0:T(1,128)S(1)}, u32[]{:S(2)}, u32[]{:S(2)}) async-start(s32[32,1,128]{2,1,0:T(1,128)} %wanted_slots.1), calls=%async_computation | async-start | bytes 32768 | tf_op jit(solution)/shard_map/all_to_all | solution.py:319
  21.5 9.8 %all-to-all-done.table_ref.refs_1_ = s32[32,1,128]{2,1,0:T(1,128)S(1)} async-done(((s32[32,1,128]{2,1,0:T(1,128)}), s32[32,1,128]{2,1,0:T(1,128)S(1)}, u32[]{:S(2)}, u32[]{:S(2)}) %all-to-all-start) | async-done | bytes 16416 | tf_op jit(solution)/shard_map/all_to_all | solution.py:319
  31.2 2.5 %pick_blocks.3 = (bf16[16,64,256]{2,1,0:T(8,128)(2,1)S(1)}, bf16[16,64,256]{2,1,0:T(8,128)(2,1)S(1)}, bf16[16,64,256]{2,1,0:T(8,128)(2,1)S(1)}) custom-call(s32[1]{0:T(128)} %bitcast.me_ref.refs_0_, s32[32,1,128]{2,1,0:T(1,128)S(1)} %all-to-all-done.table_ref.refs_1_, bf16[128,64,256]{2,1,0:T(8,128)(2,1)} %bitcast.24), custom_call_target="tpu_custom_call" | custom-call | tf_op jit(solution)/shard_map/pick_blocks/pallas_call | solution.py:117
  34.5 2.3 %collective-permute-start.4 = (bf16[16,64,256]{2,1,0:T(8,128)(2,1)S(1)}, bf16[16,64,256]{2,1,0:T(8,128)(2,1)S(1)}, u32[]{:S(2)}, u32[]{:S(2)}) collective-permute-start(bf16[16,64,256]{2,1,0:T(8,128)(2,1)S(1)} %get-tuple-element.29), channel_id=1, source_target_pairs={{0,16},{8,24},{16,0},{24,8},{32,48},{40,56},{48,32},{56,40},{64,80... | collective-permute-start | bytes 1572872 | tf_op jit(solution)/shard_map/ppermute | solution.py:284
  36.8 1.1 collective-permute-start.5
  37.9 4.5 %pick_blocks.2 = (bf16[16,64,256]{2,1,0:T(8,128)(2,1)}, bf16[16,64,256]{2,1,0:T(8,128)(2,1)}, bf16[16,64,256]{2,1,0:T(8,128)(2,1)S(1)}, bf16[16,64,256]{2,1,0:T(8,128)(2,1)S(1)}, bf16[16,64,256]{2,1,0:T(8,128)(2,1)S(1)}) custom-call(s32[1]{0:T(128)} %bitcast.me_ref.refs_0_, s32[32,1,128]{2,1,0:T(1,128)S(1)} %all-to-all-done.table_ref.refs_1_, ...), custom_call_target="tpu_custom_call" | custom-call | tf_op jit(solution)/shard_map/pick_blocks/pallas_call | solution.py:117
  44.1 1.1 collective-permute-start.1
  45.2 15.8 %collective-permute-done.3.refs_4_ = bf16[16,64,256]{2,1,0:T(8,128)(2,1)S(1)} collective-permute-done((bf16[16,64,256]{2,1,0:T(8,128)(2,1)S(1)}, bf16[16,64,256]{2,1,0:T(8,128)(2,1)S(1)}, u32[]{:S(2)}, u32[]{:S(2)}) %collective-permute-start.3) | collective-permute-done | bytes 524320 | tf_op jit(solution)/shard_map/ppermute | solution.py:284
  64.5 1.0 copy-done.6
  65.6 1.0 copy-done.8
  66.6 1.0 copy-done.10
  67.6 6.7 %attend_chunk.3 = (bf16[144,512]{1,0:T(8,128)(2,1)S(1)}, bf16[144,512]{1,0:T(8,128)(2,1)S(1)}, bf16[144,512]{1,0:T(8,128)(2,1)}, bf16[144,512]{1,0:T(8,128)(2,1)}, bf16[144,512]{1,0:T(8,128)(2,1)S(1)}) custom-call(s32[1]{0:T(128)} %bitcast.me_ref.refs_0_, s32[32,1,128]{2,1,0:T(1,128)S(1)} %all-to-all-done.table_ref.refs_1_, ...), custom_call_target="tpu_custom_call" | custom-call | flops 1073741824 | bytes 2097152 | tf_op jit(solution)/shard_map/attend_chunk/pallas_call | solution.py:237
  75.2 3.2 %collective-permute-start.7 = (bf16[144,512]{1,0:T(8,128)(2,1)S(1)}, bf16[144,512]{1,0:T(8,128)(2,1)S(1)}, u32[]{:S(2)}, u32[]{:S(2)}) collective-permute-start(bf16[144,512]{1,0:T(8,128)(2,1)S(1)} %get-tuple-element.34), channel_id=1, source_target_pairs={{0,96},{8,104},{16,112},{24,120},{32,128},{40,136},{48,144},{56,15... | collective-permute-start | bytes 442376 | tf_op jit(solution)/shard_map/ppermute | solution.py:289
  78.5 2.4 %collective-permute-done.refs_4_ = bf16[16,64,256]{2,1,0:T(8,128)(2,1)S(1)} collective-permute-done((bf16[16,64,256]{2,1,0:T(8,128)(2,1)}, bf16[16,64,256]{2,1,0:T(8,128)(2,1)S(1)}, u32[]{:S(2)}, u32[]{:S(2)}) %collective-permute-start) | collective-permute-done | bytes 524320 | tf_op jit(solution)/shard_map/ppermute | solution.py:284
  81.6 2.3 %collective-permute-start.9 = (bf16[144,512]{1,0:T(8,128)(2,1)}, bf16[144,512]{1,0:T(8,128)(2,1)S(1)}, u32[]{:S(2)}, u32[]{:S(2)}) collective-permute-start(bf16[144,512]{1,0:T(8,128)(2,1)} %get-tuple-element.36), channel_id=1, source_target_pairs={{0,64},{8,72},{16,80},{24,88},{32,96},{40,104},{48,112},{56,120},{... | collective-permute-start | bytes 442376 | tf_op jit(solution)/shard_map/ppermute | solution.py:289
  83.9 6.0 %collective-permute-done.6.refs_7_.rest_0_ = bf16[144,512]{1,0:T(8,128)(2,1)S(1)} collective-permute-done((bf16[144,512]{1,0:T(8,128)(2,1)S(1)}, bf16[144,512]{1,0:T(8,128)(2,1)S(1)}, u32[]{:S(2)}, u32[]{:S(2)}) %collective-permute-start.6) | collective-permute-done | bytes 147488 | tf_op jit(solution)/shard_map/ppermute | solution.py:289
  89.9 5.5 %attend_chunk.4 = (bf16[144,512]{1,0:T(8,128)(2,1)S(1)}, bf16[144,512]{1,0:T(8,128)(2,1)}, bf16[144,512]{1,0:T(8,128)(2,1)}) custom-call(s32[1]{0:T(128)} %bitcast.me_ref.refs_0_, s32[32,1,128]{2,1,0:T(1,128)S(1)} %all-to-all-done.table_ref.refs_1_, bf16[512,1024]{1,0:T(8,128)(2,1)} %all-gather.2.cloned.1.call-done.refs_2_, ...), custom_call_target="tpu_custom_call" | custom-call | flops 805306368 | bytes 1572864 | tf_op jit(solution)/shard_map/attend_chunk/pallas_call | solution.py:237
  96.1 2.0 %collective-permute-start.12 = (bf16[144,512]{1,0:T(8,128)(2,1)}, bf16[144,512]{1,0:T(8,128)(2,1)S(1)}, u32[]{:S(2)}, u32[]{:S(2)}) collective-permute-start(bf16[144,512]{1,0:T(8,128)(2,1)} %get-tuple-element.39), channel_id=1, source_target_pairs={{0,32},{8,40},{16,48},{24,56},{32,64},{40,72},{48,80},{56,88},{64,... | collective-permute-start | bytes 442376 | tf_op jit(solution)/shard_map/ppermute | solution.py:289
  98.1 5.3 %attend_chunk.5 = (bf16[144,512]{1,0:T(8,128)(2,1)S(1)}, bf16[1024,4096]{1,0:T(8,128)(2,1)S(1)}) custom-call(s32[1]{0:T(128)} %bitcast.me_ref.refs_0_, s32[32,1,128]{2,1,0:T(1,128)S(1)} %all-to-all-done.table_ref.refs_1_, bf16[512,1024]{1,0:T(8,128)(2,1)} %all-gather.2.cloned.1.call-done.refs_2_, bf16[16,64,256]{2,1,0:T(8,128)(2,1)S(1)} %get-tuple-element.23.refs_3_, ...), custom_call_target="tpu_custom_call" | custom-call | flops 268435456 | bytes 524288 | tf_op jit(solution)/shard_map/attend_chunk/pallas_call | solution.py:237
  103.5 1.9 %merge_project.1 = bf16[64,4096]{1,0:T(8,128)(2,1)S(1)} custom-call(bf16[1024,4096]{1,0:T(8,128)(2,1)S(1)} %get-tuple-element.33.wide_ref, bf16[144,512]{1,0:T(8,128)(2,1)S(1)} %collective-permute-done.6.refs_7_.rest_0_, bf16[144,512]{1,0:T(8,128)(2,1)S(1)} %collective-permute-done.7.rest_1_, bf16[144,512]{1,0:T(8,128)(2,1)S(1)} %collective-permute-done.8.rest_2_, ...), custom_call_target="tpu_custom_call" | custom-call | flops 536870912 | bytes 8388608 | tf_op jit(solution)/shard_map/merge_project/pallas_call | solution.py:271
  105.5 1.5 %collective-permute-done.13 = bf16[4,8,4096]{2,1,0:T(8,128)(2,1)S(1)} collective-permute-done((bf16[4,8,4096]{2,1,0:T(8,128)(2,1)S(1)}, bf16[4,8,4096]{2,1,0:T(8,128)(2,1)S(1)}, u32[]{:S(2)}, u32[]{:S(2)}) %collective-permute-start.13) | collective-permute-done | bytes 262176 | tf_op jit(solution)/shard_map/ppermute | solution.py:300
  108.1 2.2 %collective-permute-start.15 = (bf16[8,4096]{1,0:T(8,128)(2,1)S(1)}, bf16[8,4096]{1,0:T(8,128)(2,1)S(1)}, u32[]{:S(2)}, u32[]{:S(2)}) collective-permute-start(bf16[8,4096]{1,0:T(8,128)(2,1)S(1)} %get-tuple-element.43), channel_id=1, source_target_pairs={{0,2},{1,3},{2,4},{3,5},{4,6},{5,7},{6,0},{7,1},{8,10},{9,11},{10,... | collective-permute-start | bytes 196616 | tf_op jit(solution)/shard_map/ppermute | solution.py:296
  110.3 2.7 %collective-permute-done.14 = bf16[8,4096]{1,0:T(8,128)(2,1)S(1)} collective-permute-done((bf16[8,4096]{1,0:T(8,128)(2,1)S(1)}, bf16[8,4096]{1,0:T(8,128)(2,1)S(1)}, u32[]{:S(2)}, u32[]{:S(2)}) %collective-permute-start.14) | collective-permute-done | bytes 65568 | tf_op jit(solution)/shard_map/ppermute | solution.py:296
  113.1 2.7 %collective-permute-done.16 = bf16[8,4096]{1,0:T(8,128)(2,1)S(1)} collective-permute-done((bf16[8,4096]{1,0:T(8,128)(2,1)S(1)}, bf16[8,4096]{1,0:T(8,128)(2,1)S(1)}, u32[]{:S(2)}, u32[]{:S(2)}) %collective-permute-start.16) | collective-permute-done | bytes 65568 | tf_op jit(solution)/shard_map/ppermute | solution.py:296
  (50 shorter events, 13.1 us)
Async XLA Ops:
  6.5 56.9 %copy-start = (bf16[64,1024]{1,0:T(8,128)(2,1)S(1)}, bf16[64,1024]{1,0:T(8,128)(2,1)}, u32[]{:S(2)}) copy-start(bf16[64,1024]{1,0:T(8,128)(2,1)} %refs_7_.1) | copy-start | bytes 393220
  6.5 56.9 %all-gather.2.cloned.1.call-start = ((), (), s32[]{:S(2)}) async-start(), calls=%async_computation.1 | async-start | bytes 1179648 | tf_op jit(solution)/shard_map/all_gather | solution.py:321
  9.2 54.3 %copy-start.11 = (bf16[64,1,256]{2,0,1:T(8,128)(2,1)S(1)}, bf16[64,1,256]{2,0,1:T(8,128)(2,1)}, u32[]{:S(2)}) copy-start(bf16[64,1,256]{2,0,1:T(8,128)(2,1)} %param.8) | copy-start | bytes 98308
  10.1 21.1 %all-to-all-start = ((s32[32,1,128]{2,1,0:T(1,128)}), s32[32,1,128]{2,1,0:T(1,128)S(1)}, u32[]{:S(2)}, u32[]{:S(2)}) async-start(s32[32,1,128]{2,1,0:T(1,128)} %wanted_slots.1), calls=%async_computation | async-start | bytes 32768 | tf_op jit(solution)/shard_map/all_to_all | solution.py:319
  33.7 27.4 %collective-permute-start.3 = (bf16[16,64,256]{2,1,0:T(8,128)(2,1)S(1)}, bf16[16,64,256]{2,1,0:T(8,128)(2,1)S(1)}, u32[]{:S(2)}, u32[]{:S(2)}) collective-permute-start(bf16[16,64,256]{2,1,0:T(8,128)(2,1)S(1)} %get-tuple-element.28), channel_id=1, source_target_pairs={{0,8},{8,16},{16,24},{24,0},{32,40},{40,48},{48,56},{56,32},{64,72... | collective-permute-start | bytes 1572872 | tf_op jit(solution)/shard_map/ppermute | solution.py:284
  34.5 27.4 %collective-permute-start.4 = (bf16[16,64,256]{2,1,0:T(8,128)(2,1)S(1)}, bf16[16,64,256]{2,1,0:T(8,128)(2,1)S(1)}, u32[]{:S(2)}, u32[]{:S(2)}) collective-permute-start(bf16[16,64,256]{2,1,0:T(8,128)(2,1)S(1)} %get-tuple-element.29), channel_id=1, source_target_pairs={{0,16},{8,24},{16,0},{24,8},{32,48},{40,56},{48,32},{56,40},{64,80... | collective-permute-start | bytes 1572872 | tf_op jit(solution)/shard_map/ppermute | solution.py:284
  36.8 25.9 %collective-permute-start.5 = (bf16[16,64,256]{2,1,0:T(8,128)(2,1)S(1)}, bf16[16,64,256]{2,1,0:T(8,128)(2,1)S(1)}, u32[]{:S(2)}, u32[]{:S(2)}) collective-permute-start(bf16[16,64,256]{2,1,0:T(8,128)(2,1)S(1)} %get-tuple-element.30), channel_id=1, source_target_pairs={{0,24},{8,0},{16,8},{24,16},{32,56},{40,32},{48,40},{56,48},{64,88... | collective-permute-start | bytes 1572872 | tf_op jit(solution)/shard_map/ppermute | solution.py:284
  43.2 37.6 %collective-permute-start = (bf16[16,64,256]{2,1,0:T(8,128)(2,1)}, bf16[16,64,256]{2,1,0:T(8,128)(2,1)S(1)}, u32[]{:S(2)}, u32[]{:S(2)}) collective-permute-start(bf16[16,64,256]{2,1,0:T(8,128)(2,1)} %get-tuple-element.24), channel_id=1, source_target_pairs={{0,8},{8,16},{16,24},{24,0},{32,40},{40,48},{48,56},{56,32},{64,72... | collective-permute-start | bytes 1572872 | tf_op jit(solution)/shard_map/ppermute | solution.py:284
  44.1 37.5 %collective-permute-start.1 = (bf16[16,64,256]{2,1,0:T(8,128)(2,1)}, bf16[16,64,256]{2,1,0:T(8,128)(2,1)S(1)}, u32[]{:S(2)}, u32[]{:S(2)}) collective-permute-start(bf16[16,64,256]{2,1,0:T(8,128)(2,1)} %get-tuple-element.25), channel_id=1, source_target_pairs={{0,16},{8,24},{16,0},{24,8},{32,48},{40,56},{48,32},{56,40},{64,80... | collective-permute-start | bytes 1572872 | tf_op jit(solution)/shard_map/ppermute | solution.py:284
  61.9 22.0 %collective-permute-start.2 = (bf16[16,64,256]{2,1,0:T(8,128)(2,1)S(1)}, bf16[16,64,256]{2,1,0:T(8,128)(2,1)S(1)}, u32[]{:S(2)}, u32[]{:S(2)}) collective-permute-start(bf16[16,64,256]{2,1,0:T(8,128)(2,1)S(1)} %get-tuple-element.26), channel_id=1, source_target_pairs={{0,24},{8,0},{16,8},{24,16},{32,56},{40,32},{48,40},{56,48},{64,88... | collective-permute-start | bytes 1572872 | tf_op jit(solution)/shard_map/ppermute | solution.py:284
  63.5 1.0 copy-start.4
  64.5 1.0 copy-start.6
  65.6 1.0 copy-start.8
  74.3 15.6 %collective-permute-start.6 = (bf16[144,512]{1,0:T(8,128)(2,1)S(1)}, bf16[144,512]{1,0:T(8,128)(2,1)S(1)}, u32[]{:S(2)}, u32[]{:S(2)}) collective-permute-start(bf16[144,512]{1,0:T(8,128)(2,1)S(1)} %get-tuple-element.31), channel_id=1, source_target_pairs={{0,128},{8,136},{16,144},{24,152},{32,160},{40,168},{48,176},{56,1... | collective-permute-start | bytes 442376 | tf_op jit(solution)/shard_map/ppermute | solution.py:289
  75.2 20.8 %collective-permute-start.7 = (bf16[144,512]{1,0:T(8,128)(2,1)S(1)}, bf16[144,512]{1,0:T(8,128)(2,1)S(1)}, u32[]{:S(2)}, u32[]{:S(2)}) collective-permute-start(bf16[144,512]{1,0:T(8,128)(2,1)S(1)} %get-tuple-element.34), channel_id=1, source_target_pairs={{0,96},{8,104},{16,112},{24,120},{32,128},{40,136},{48,144},{56,15... | collective-permute-start | bytes 442376 | tf_op jit(solution)/shard_map/ppermute | solution.py:289
  80.8 22.6 %collective-permute-start.8 = (bf16[144,512]{1,0:T(8,128)(2,1)}, bf16[144,512]{1,0:T(8,128)(2,1)S(1)}, u32[]{:S(2)}, u32[]{:S(2)}) collective-permute-start(bf16[144,512]{1,0:T(8,128)(2,1)} %get-tuple-element.35), channel_id=1, source_target_pairs={{0,160},{8,168},{16,176},{24,184},{32,192},{40,200},{48,208},{56,2... | collective-permute-start | bytes 442376 | tf_op jit(solution)/shard_map/ppermute | solution.py:289
  81.6 21.8 %collective-permute-start.9 = (bf16[144,512]{1,0:T(8,128)(2,1)}, bf16[144,512]{1,0:T(8,128)(2,1)S(1)}, u32[]{:S(2)}, u32[]{:S(2)}) collective-permute-start(bf16[144,512]{1,0:T(8,128)(2,1)} %get-tuple-element.36), channel_id=1, source_target_pairs={{0,64},{8,72},{16,80},{24,88},{32,96},{40,104},{48,112},{56,120},{... | collective-permute-start | bytes 442376 | tf_op jit(solution)/shard_map/ppermute | solution.py:289
  95.5 8.0 %collective-permute-start.10 = (bf16[144,512]{1,0:T(8,128)(2,1)S(1)}, bf16[144,512]{1,0:T(8,128)(2,1)S(1)}, u32[]{:S(2)}, u32[]{:S(2)}) collective-permute-start(bf16[144,512]{1,0:T(8,128)(2,1)S(1)} %get-tuple-element.32.refs_7_), channel_id=1, source_target_pairs={{0,192},{8,200},{16,208},{24,216},{32,224},{40,232},{48,240},{56,2... | collective-permute-start | bytes 442376 | tf_op jit(solution)/shard_map/ppermute | solution.py:289
  96.1 7.4 %collective-permute-start.11 = (bf16[144,512]{1,0:T(8,128)(2,1)}, bf16[144,512]{1,0:T(8,128)(2,1)S(1)}, u32[]{:S(2)}, u32[]{:S(2)}) collective-permute-start(bf16[144,512]{1,0:T(8,128)(2,1)} %get-tuple-element.38), channel_id=1, source_target_pairs={{0,224},{8,232},{16,240},{24,248},{32,0},{40,8},{48,16},{56,24},{6... | collective-permute-start | bytes 442376 | tf_op jit(solution)/shard_map/ppermute | solution.py:289
  96.1 7.4 %collective-permute-start.12 = (bf16[144,512]{1,0:T(8,128)(2,1)}, bf16[144,512]{1,0:T(8,128)(2,1)S(1)}, u32[]{:S(2)}, u32[]{:S(2)}) collective-permute-start(bf16[144,512]{1,0:T(8,128)(2,1)} %get-tuple-element.39), channel_id=1, source_target_pairs={{0,32},{8,40},{16,48},{24,56},{32,64},{40,72},{48,80},{56,88},{64,... | collective-permute-start | bytes 442376 | tf_op jit(solution)/shard_map/ppermute | solution.py:289
  105.4 1.6 %collective-permute-start.13 = (bf16[4,8,4096]{2,1,0:T(8,128)(2,1)S(1)}, bf16[4,8,4096]{2,1,0:T(8,128)(2,1)S(1)}, u32[]{:S(2)}, u32[]{:S(2)}) collective-permute-start(bf16[4,8,4096]{2,1,0:T(8,128)(2,1)S(1)} %dynamic-slice_bitcast_fusion), channel_id=1, source_target_pairs={{0,1},{1,0},{2,3},{3,2},{4,5},{5,4},{6,7},{7,6},{8,9},{9,8},{10,11... | collective-permute-start | bytes 786440 | tf_op jit(solution)/shard_map/ppermute | solution.py:300
  107.1 6.0 %collective-permute-start.14 = (bf16[8,4096]{1,0:T(8,128)(2,1)S(1)}, bf16[8,4096]{1,0:T(8,128)(2,1)S(1)}, u32[]{:S(2)}, u32[]{:S(2)}) collective-permute-start(bf16[8,4096]{1,0:T(8,128)(2,1)S(1)} %get-tuple-element.41), channel_id=1, source_target_pairs={{0,4},{1,5},{2,6},{3,7},{4,0},{5,1},{6,2},{7,3},{8,12},{9,13},{10,... | collective-permute-start | bytes 196616 | tf_op jit(solution)/shard_map/ppermute | solution.py:296
  108.1 5.0 %collective-permute-start.15 = (bf16[8,4096]{1,0:T(8,128)(2,1)S(1)}, bf16[8,4096]{1,0:T(8,128)(2,1)S(1)}, u32[]{:S(2)}, u32[]{:S(2)}) collective-permute-start(bf16[8,4096]{1,0:T(8,128)(2,1)S(1)} %get-tuple-element.43), channel_id=1, source_target_pairs={{0,2},{1,3},{2,4},{3,5},{4,6},{5,7},{6,0},{7,1},{8,10},{9,11},{10,... | collective-permute-start | bytes 196616 | tf_op jit(solution)/shard_map/ppermute | solution.py:296
  110.3 5.5 %collective-permute-start.16 = (bf16[8,4096]{1,0:T(8,128)(2,1)S(1)}, bf16[8,4096]{1,0:T(8,128)(2,1)S(1)}, u32[]{:S(2)}, u32[]{:S(2)}) collective-permute-start(bf16[8,4096]{1,0:T(8,128)(2,1)S(1)} %get-tuple-element.42), channel_id=1, source_target_pairs={{0,6},{1,7},{2,0},{3,1},{4,2},{5,3},{6,4},{7,5},{8,14},{9,15},{10,... | collective-permute-start | bytes 196616 | tf_op jit(solution)/shard_map/ppermute | solution.py:296
  (7 other events, 5.5 us)
Sparse Core Ops, SparseCore 0:
  9.1 41.1 all-gather.1

commit v5 on v4

--- a/solution.py
+++ b/solution.py
@@ -94,36 +94,85 @@
     return jnp.clip(table_ref[home, 0, owner * CAP + c], 0, cache_ref.shape[0] - 1)
 
 
-def pick_kernel(wanted, me_ref, table_ref, cache_ref, *rest):
-    outs, sems = rest[:-1], rest[-1]
+def start_picks(shifts, k, me_ref, table_ref, cache_ref, out, sem):
     zo, xo = coordinates(me_ref)
-    for m, (shifts, k) in enumerate(wanted):
-        for n, shift in enumerate(shifts):
-            home = rem(zo + shift, NZ) * NX + rem(xo + k, NX)
-            for c in range(CAP):
-                slot = slot_of(table_ref, home, me_ref[0], c, cache_ref)
-                pltpu.make_async_copy(
-                    cache_ref.at[pl.ds(slot, 1)],
-                    outs[m].at[pl.ds(n * CAP + c, 1)],
-                    sems.at[m],
-                ).start()
-    for m, (shifts, k) in enumerate(wanted):
-        pltpu.make_async_copy(
-            cache_ref.at[pl.ds(0, len(shifts) * CAP)], outs[m], sems.at[m]
-        ).wait()
-
-
-def pick(wanted, me, table, cache):
+    for n, shift in enumerate(shifts):
+        home = rem(zo + shift, NZ) * NX + rem(xo + k, NX)
+        for c in range(CAP):
+            slot = slot_of(table_ref, home, me_ref[0], c, cache_ref)
+            pltpu.make_async_copy(
+                cache_ref.at[pl.ds(slot, 1)], out.at[pl.ds(n * CAP + c, 1)], sem
+            ).start()
+
+
+def wait_picks(shifts, cache_ref, out, sem):
+    pltpu.make_async_copy(cache_ref.at[pl.ds(0, len(shifts) * CAP)], out, sem).wait()
+
+
+def pick_far_kernel(shifts, me_ref, table_ref, cache_ref, query_ref, *refs):
+    outs, (copies_ref, query_here, sems, query_sem, copy_sems) = refs[: NX - 1], refs[NX - 1 :]
+    fetch = pltpu.make_async_copy(query_ref, query_here, query_sem)
+    fetch.start()
+    for k, out in enumerate(outs, 1):
+        start_picks(shifts, k, me_ref, table_ref, cache_ref, out, sems.at[k - 1])
+    copies = [
+        pltpu.make_async_copy(query_here, copies_ref.at[z], copy_sems.at[z]) for z in range(NZ)
+    ]
+    fetch.wait()
+    for copy in copies:
+        copy.start()
+    for k, out in enumerate(outs, 1):
+        wait_picks(shifts, cache_ref, out, sems.at[k - 1])
+    for copy in copies:
+        copy.wait()
+
+
+def pick_far(shifts, me, table, cache, queries):
+    block = (len(shifts) * CAP, BLK, 2 * HD)
+    *sent, copies = pl.pallas_call(
+        functools.partial(pick_far_kernel, shifts),
+        out_shape=[pltpu.VMEM(block, cache.dtype)] * (NX - 1)
+        + [jax.ShapeDtypeStruct((NZ,) + queries.shape, queries.dtype)],
+        in_specs=[IN_SMEM, IN_SMEM, IN_HBM, IN_HBM],
+        out_specs=[IN_VMEM] * (NX - 1) + [IN_HBM],
+        scratch_shapes=[
+            pltpu.VMEM(queries.shape, queries.dtype),
+            pltpu.SemaphoreType.DMA((NX - 1,)),
+            pltpu.SemaphoreType.DMA,
+            pltpu.SemaphoreType.DMA((NZ,)),
+        ],
+        compiler_params=pltpu.CompilerParams(vmem_limit_bytes=VMEM_LIMIT),
+        name="pick_far",
+    )(me, table, cache, keep_in_hbm(queries))
+    return sent, copies
+
+
+def pick_near_kernel(shifts, me_ref, table_ref, cache_ref, *refs):
+    outs, here, sems = refs[: NX - 1], refs[-2], refs[-1]
+    for k in range(1, NX):
+        start_picks(shifts, k, me_ref, table_ref, cache_ref, here.at[k - 1], sems.at[k - 1])
+    moves = []
+    for k, out in enumerate(outs, 1):
+        wait_picks(shifts, cache_ref, here.at[k - 1], sems.at[k - 1])
+        moves.append(pltpu.make_async_copy(here.at[k - 1], out, sems.at[k - 1]))
+        moves[-1].start()
+    for move in moves:
+        move.wait()
+
+
+def pick_near(shifts, me, table, cache):
+    block = (len(shifts) * CAP, BLK, 2 * HD)
     return pl.pallas_call(
-        functools.partial(pick_kernel, wanted),
-        out_shape=[
-            pltpu.VMEM((len(shifts) * CAP, BLK, 2 * HD), cache.dtype) for shifts, k in wanted
+        functools.partial(pick_near_kernel, shifts),
+        out_shape=[jax.ShapeDtypeStruct(block, cache.dtype)] * (NX - 1),
+        in_specs=[IN_SMEM, IN_SMEM, IN_HBM],
+        out_specs=[IN_HBM] * (NX - 1),
+        scratch_shapes=[
+            pltpu.VMEM((NX - 1,) + block, cache.dtype),
+            pltpu.SemaphoreType.DMA((NX - 1,)),
         ],
-        in_specs=[IN_SMEM, IN_SMEM, IN_HBM],
-        out_specs=[IN_VMEM] * len(wanted),
-        scratch_shapes=[pltpu.SemaphoreType.DMA((len(wanted),))],
         compiler_params=pltpu.CompilerParams(vmem_limit_bytes=VMEM_LIMIT),
-        name="pick_blocks",
+        name="pick_near",
     )(me, table, cache)
 
 
@@ -191,22 +240,31 @@
 def attend_kernel(chunk, shifts, n_after, with_suffix, with_weight, *refs):
     refs = list(refs)
     take = lambda n: [refs.pop(0) for _ in range(n)]
-    me_ref, table_ref, z_query_ref = take(3)
-    blocks = take(NX)
+    me_ref, table_ref, cache_ref, z_query_ref = take(4)
+    arrived = take(NX - 1)
     own_refs = take(2 * with_suffix)
     take(n_after)
     weight_ref = take(1)[0] if with_weight else None
     packet_refs = take(len(shifts) + with_suffix)
     wide_ref = take(1)[0] if with_weight else None
-    query_here, query_sems, wide_sems = take(3)
+    here, query_here, block_sems, query_sems, wide_sems = take(5)
     zo, _ = coordinates(me_ref)
-    fetches = []
+    first = chunk.index(shifts[0]) * CAP
+    fetches = [
+        pltpu.make_async_copy(
+            arrived[k - 1].at[pl.ds(first, len(shifts) * CAP)], here.at[k], block_sems.at[k]
+        )
+        for k in range(1, NX)
+    ]
     for n, shift in enumerate(shifts):
-        start = pl.multiple_of(rem(zo + shift, NZ) * SUF, SUF)
         fetches.append(
-            pltpu.make_async_copy(z_query_ref.at[pl.ds(start, SUF), :], query_here.at[n], query_sems.at[n])
+            pltpu.make_async_copy(
+                z_query_ref.at[rem(zo + shift, NZ)], query_here.at[n], query_sems.at[n]
+            )
         )
-        fetches[-1].start()
+    for fetch in fetches:
+        fetch.start()
+    start_picks(shifts, 0, me_ref, table_ref, cache_ref, here.at[0], block_sems.at[0])
     wide = []
     if with_weight:
         step = weight_ref.shape[0] // WIDE_PARTS
@@ -219,16 +277,18 @@
     if with_suffix:
         part = suffix_part(head_rows(own_refs[0][...]), own_refs[1][...])
         write_packet(packet_refs[-1], *part)
+    for fetch in fetches:
+        fetch.wait()
+    wait_picks(shifts, cache_ref, here.at[0], block_sems.at[0])
     for n, shift in enumerate(shifts):
-        fetches[n].wait()
         rows = head_rows(query_here[n])
-        part = cached_part(shift, chunk.index(shift), me_ref, table_ref, rows, blocks)
+        part = cached_part(shift, n, me_ref, table_ref, rows, [here.at[k] for k in range(NX)])
         write_packet(packet_refs[n], *part)
     for copy in wide:
         copy.wait()
 
 
-def attend(chunk, shifts, me, table, z_queries, blocks, own=(), after=(), weight=None):
+def attend(chunk, shifts, me, table, cache, z_queries, arrived, own=(), after=(), weight=None):
     keys = len(shifts) * NX * CAP * BLK
     with_weight = weight is not None
     n_packets = len(shifts) + bool(own)
@@ -237,10 +297,12 @@
     outs = pl.pallas_call(
         functools.partial(attend_kernel, chunk, shifts, len(after), bool(own), with_weight),
         out_shape=[jax.ShapeDtypeStruct((PACKET, ROWS), jnp.bfloat16)] * n_packets + wide,
-        in_specs=[IN_SMEM] * 2 + [IN_HBM] + [IN_VMEM] * (NX + len(own)) + [IN_HBM] * len(extra),
+        in_specs=[IN_SMEM] * 2 + [IN_HBM] * (NX + 1) + [IN_VMEM] * len(own) + [IN_HBM] * len(extra),
         out_specs=[IN_VMEM] * (n_packets + len(wide)),
         scratch_shapes=[
+            pltpu.VMEM((NX, len(shifts) * CAP, BLK, 2 * HD), cache.dtype),
             pltpu.VMEM((len(shifts), SUF, GROUP * HD), jnp.bfloat16),
+            pltpu.SemaphoreType.DMA((NX,)),
             pltpu.SemaphoreType.DMA((len(shifts),)),
             pltpu.SemaphoreType.DMA((WIDE_PARTS,)),
         ],
@@ -249,7 +311,7 @@
             flops=4 * keys * ROWS * HD, bytes_accessed=4 * keys * HD, transcendentals=keys * ROWS
         ),
         name="attend_chunk",
-    )(me, table, z_queries, *blocks, *own, *extra)
+    )(me, table, cache, z_queries, *arrived, *own, *extra)
     return outs[:n_packets], outs[n_packets:]
 
 
@@ -317,27 +379,28 @@
     me = lax.axis_index("store").astype(jnp.int32).reshape(1)
     wanted = wanted_slots(prefix_blocks, block_owner, block_slot, store_count)
     table = lax.all_to_all(wanted, "store", split_axis=0, concat_axis=0, tiled=True)
-    z_groups = [[z * NX + x for z in range(NZ)] for x in range(NX)]
-    z_queries = lax.all_gather(queries, "store", axis=0, tiled=True, axis_index_groups=z_groups)
-    z_queries = keep_in_hbm(z_queries)
     cache = keep_in_hbm(kv_cache.reshape(kv_cache.shape[0], BLK, 2 * HD))
     suffix = suffix_kv.reshape(SUF, 2 * HD)
     far, near = CHUNKS
     away = near[:-1]
-    steps = range(1, NX)
-    far_sent = pick([(far, k) for k in steps], me, table, cache)
-    *near_sent, far_here, near_here = pick(
-        [(near, k) for k in steps] + [(far, 0), (near, 0)], me, table, cache
-    )
-    over_x = lambda blocks: [x_permute(block, k) for k, block in zip(steps, blocks)]
+    over_x = lambda blocks: [x_permute(block, k) for k, block in enumerate(blocks, 1)]
     over_z = lambda shifts, parts: [z_permute(part, s) for s, part in zip(shifts, parts)]
-    far_blocks, near_blocks = [far_here] + over_x(far_sent), [near_here] + over_x(near_sent)
-    parts, _ = attend(far, far, me, table, z_queries, far_blocks, own=(queries, suffix))
+    far_sent, copies = pick_far(far, me, table, cache, queries)
+    far_blocks = over_x(far_sent)
+    near_blocks = over_x(pick_near(near, me, table, cache))
+    z_groups = [[z * NX + x for z in range(NZ)] for x in range(NX)]
+    z_queries = keep_in_hbm(
+        lax.all_to_all(
+            copies, "store", split_axis=0, concat_axis=0, tiled=True, axis_index_groups=z_groups
+        )
+    )
+    common = (me, table, cache, z_queries)
+    parts, _ = attend(far, far, *common, far_blocks, own=(queries, suffix))
     packets = over_z(far, parts) + [parts[-1]]
-    parts, _ = attend(near, away, me, table, z_queries, near_blocks, after=packets[:1])
+    parts, _ = attend(near, away, *common, near_blocks, after=packets[:1])
     packets += over_z(away, parts)
     home, (wide,) = attend(
-        near, near[-1:], me, table, z_queries, near_blocks, after=parts[:1], weight=keep_in_hbm(out_weight)
+        near, near[-1:], *common, near_blocks, after=parts[:1], weight=keep_in_hbm(out_weight)
     )
     return sum_heads(finish(wide, packets + list(home)))
 

time: 126 us -> 116 us (0.921); the launches traced: 123 us -> 115 us
  between operations: 14.3 us -> 0.9 us
  starting transfers between devices: 30.7 us -> 43 us
  local copies, waits for them, and re-layouts: 8.7 us -> 1.37 us
  Pallas kernels: 27.3 us -> 29 us
    ppermute x7, starting transfers between devices: 9.88 us -> 17.2 us  [z_permute(): return lax.ppermute(a, 'store', pairs)]
    unnamed x24 -> x8, local copies, waits for them, and re-layouts: 8.64 us -> 1.31 us
    ppermute x7, waiting for transfers between devices: 6.01 us -> 0.02 us  [z_permute(): return lax.ppermute(a, 'store', pairs)]
    ppermute x6, waiting for transfers between devices: 18.2 us -> 23.9 us  [x_permute(): return lax.ppermute(a, 'store', pairs)]
    all_to_all x0 -> x1, starting transfers between devices: none -> 4.25 us  [local(): lax.all_to_all(copies, 'store', split_axis=0, concat_axis=0, tiled=True,...]
    pallas_call x2, Pallas kernels: 7.01 us -> 8.36 us  [the longest x1 4.71 us: pick_far(): pl.pallas_call(functools.partial(pick_far_kernel, shifts), out_shape=[plt...]
  transfers between devices with their start and end apart: 19 -> 19, of which waited for: 7 -> 7; matrix products, arithmetic and copies ran while one was open for 0% -> 0% of each run, Pallas kernels for 21% -> 19%
where the time goes in v5:
time: 116 us; the launch traced here: 115 us
  starting transfers between devices  43 us (37%)
  waiting for transfers between devices  40.5 us (35%)
  Pallas kernels  29 us (25%)
  local copies, waits for them, and re-layouts  1.37 us (1%)
    ppermute x6, waiting for transfers between devices, x_permute(): return lax.ppermute(a, 'store', pairs)  23.9 us
    pallas_call x3, Pallas kernels, attend(): pl.pallas_call(functools.partial(attend_kernel, chunk, shifts, len(after)...  17.9 us
    ppermute x7, starting transfers between devices, z_permute(): return lax.ppermute(a, 'store', pairs)  17.2 us
    all_to_all x1, starting transfers between devices, local(): lax.all_to_all(wanted, 'store', split_axis=0, concat_axis=0, tiled=True)  11.3 us
    all_to_all x1, waiting for transfers between devices, local(): lax.all_to_all(wanted, 'store', split_axis=0, concat_axis=0, tiled=True)  9.65 us
    ppermute x6, starting transfers between devices, x_permute(): return lax.ppermute(a, 'store', pairs)  6.62 us
    ppermute x3, waiting for transfers between devices, y_permute(): return lax.ppermute(a, 'head', pairs)  5.47 us
    pallas_call x1, Pallas kernels, pick_far(): pl.pallas_call(functools.partial(pick_far_kernel, shifts), out_shape=[plt...  4.71 us
  transfers between devices with their start and end apart: 19, of which 7 were waited for; matrix products, arithmetic and copies ran while one was open for 0% of the time, Pallas kernels for 19%

profile of v5, /device:TPU:24, one launch (start us, length us, event | category | flops | bytes accessed | tf_op | source)
XLA Modules:
  0.0 115.5 jit_solution(16465445984526528847)
XLA Ops:
  2.9 11.3 %all-to-all-start = ((s32[32,1,128]{2,1,0:T(1,128)}), s32[32,1,128]{2,1,0:T(1,128)S(1)}, u32[]{:S(2)}, u32[]{:S(2)}) async-start(s32[32,1,128]{2,1,0:T(1,128)} %wanted_slots.1), calls=%async_computation | async-start | bytes 32768 | tf_op jit(solution)/shard_map/all_to_all | solution.py:381
  14.2 9.7 %all-to-all-done.table_ref.refs_1_ = s32[32,1,128]{2,1,0:T(1,128)S(1)} async-done(((s32[32,1,128]{2,1,0:T(1,128)}), s32[32,1,128]{2,1,0:T(1,128)S(1)}, u32[]{:S(2)}, u32[]{:S(2)}) %all-to-all-start) | async-done | bytes 16416 | tf_op jit(solution)/shard_map/all_to_all | solution.py:381
  23.9 4.7 %pick_far.1 = (bf16[16,64,256]{2,1,0:T(8,128)(2,1)S(1)}, bf16[16,64,256]{2,1,0:T(8,128)(2,1)}, bf16[16,64,256]{2,1,0:T(8,128)(2,1)}, bf16[8,64,1024]{2,1,0:T(8,128)(2,1)}) custom-call(s32[1]{0:T(128)} %bitcast.me_ref.refs_0_, s32[32,1,128]{2,1,0:T(1,128)S(1)} %all-to-all-done.table_ref.refs_1_, bf16[128,64,256]{2,1,0:T(8,128)(2,1)} %bitcast.24, ...), custom_call_target="tpu_custom_call" | custom-call | tf_op jit(solution)/shard_map/pick_far/pallas_call | solution.py:132
  28.6 4.3 %all-to-all-start.1 = ((bf16[8,64,1024]{2,1,0:T(8,128)(2,1)}), bf16[8,64,1024]{2,1,0:T(8,128)(2,1)}, u32[]{:S(2)}, u32[]{:S(2)}) async-start(bf16[8,64,1024]{2,1,0:T(8,128)(2,1)} %get-tuple-element.22), calls=%async_computation.1 | async-start | bytes 2097152 | tf_op jit(solution)/shard_map/all_to_all | solution.py:393
  33.5 2.0 %collective-permute-start.4 = (bf16[16,64,256]{2,1,0:T(8,128)(2,1)}, bf16[16,64,256]{2,1,0:T(8,128)(2,1)S(1)}, u32[]{:S(2)}, u32[]{:S(2)}) collective-permute-start(bf16[16,64,256]{2,1,0:T(8,128)(2,1)} %get-tuple-element.27), channel_id=1, source_target_pairs={{0,16},{8,24},{16,0},{24,8},{32,48},{40,56},{48,32},{56,40},{64,80... | collective-permute-start | bytes 1572872 | tf_op jit(solution)/shard_map/ppermute | solution.py:346
  35.4 1.3 %collective-permute-start.5 = (bf16[16,64,256]{2,1,0:T(8,128)(2,1)}, bf16[16,64,256]{2,1,0:T(8,128)(2,1)S(1)}, u32[]{:S(2)}, u32[]{:S(2)}) collective-permute-start(bf16[16,64,256]{2,1,0:T(8,128)(2,1)} %get-tuple-element.28), channel_id=1, source_target_pairs={{0,24},{8,0},{16,8},{24,16},{32,56},{40,32},{48,40},{56,48},{64,88... | collective-permute-start | bytes 1572872 | tf_op jit(solution)/shard_map/ppermute | solution.py:346
  36.7 3.7 %pick_near.1 = (bf16[16,64,256]{2,1,0:T(8,128)(2,1)}, bf16[16,64,256]{2,1,0:T(8,128)(2,1)}, bf16[16,64,256]{2,1,0:T(8,128)(2,1)}) custom-call(s32[1]{0:T(128)} %bitcast.me_ref.refs_0_, s32[32,1,128]{2,1,0:T(1,128)S(1)} %all-to-all-done.table_ref.refs_1_, bf16[128,64,256]{2,1,0:T(8,128)(2,1)} %bitcast.25), custom_call_target="tpu_custom_call" | custom-call | tf_op jit(solution)/shard_map/pick_near/pallas_call | solution.py:165
  41.4 1.8 %collective-permute-start.1 = (bf16[16,64,256]{2,1,0:T(8,128)(2,1)}, bf16[16,64,256]{2,1,0:T(8,128)(2,1)S(1)}, u32[]{:S(2)}, u32[]{:S(2)}) collective-permute-start(bf16[16,64,256]{2,1,0:T(8,128)(2,1)} %get-tuple-element.24), channel_id=1, source_target_pairs={{0,16},{8,24},{16,0},{24,8},{32,48},{40,56},{48,32},{56,40},{64,80... | collective-permute-start | bytes 1572872 | tf_op jit(solution)/shard_map/ppermute | solution.py:346
  43.2 17.1 %collective-permute-done.3.refs_4_ = bf16[16,64,256]{2,1,0:T(8,128)(2,1)S(1)} collective-permute-done((bf16[16,64,256]{2,1,0:T(8,128)(2,1)S(1)}, bf16[16,64,256]{2,1,0:T(8,128)(2,1)S(1)}, u32[]{:S(2)}, u32[]{:S(2)}) %collective-permute-start.3) | collective-permute-done | bytes 524320 | tf_op jit(solution)/shard_map/ppermute | solution.py:346
  60.3 1.1 collective-permute-done.5.refs_6_
  61.3 6.6 %attend_chunk.3 = (bf16[144,512]{1,0:T(8,128)(2,1)S(1)}, bf16[144,512]{1,0:T(8,128)(2,1)S(1)}, bf16[144,512]{1,0:T(8,128)(2,1)}, bf16[144,512]{1,0:T(8,128)(2,1)}, bf16[144,512]{1,0:T(8,128)(2,1)S(1)}) custom-call(s32[1]{0:T(128)} %bitcast.me_ref.refs_0_, s32[32,1,128]{2,1,0:T(1,128)S(1)} %all-to-all-done.table_ref.refs_1_, bf16[128,64,256]{2,1,0:T(8,128)(2,1)} %bitcast.26, ...), custom_call_target="tpu_custom_call" | custom-call | flops 1073741824 | bytes 2097152 | tf_op jit(solution)/shard_map/attend_chunk/pallas_call | solution.py:297
  68.0 5.8 %collective-permute-start.6 = (bf16[144,512]{1,0:T(8,128)(2,1)S(1)}, bf16[144,512]{1,0:T(8,128)(2,1)S(1)}, u32[]{:S(2)}, u32[]{:S(2)}) collective-permute-start(bf16[144,512]{1,0:T(8,128)(2,1)S(1)} %get-tuple-element.29), channel_id=1, source_target_pairs={{0,128},{8,136},{16,144},{24,152},{32,160},{40,168},{48,176},{56,1... | collective-permute-start | bytes 442376 | tf_op jit(solution)/shard_map/ppermute | solution.py:351
  74.4 5.7 %collective-permute-done.refs_4_ = bf16[16,64,256]{2,1,0:T(8,128)(2,1)S(1)} collective-permute-done((bf16[16,64,256]{2,1,0:T(8,128)(2,1)}, bf16[16,64,256]{2,1,0:T(8,128)(2,1)S(1)}, u32[]{:S(2)}, u32[]{:S(2)}) %collective-permute-start) | collective-permute-done | bytes 524320 | tf_op jit(solution)/shard_map/ppermute | solution.py:346
  80.1 4.6 %collective-permute-start.8 = (bf16[144,512]{1,0:T(8,128)(2,1)}, bf16[144,512]{1,0:T(8,128)(2,1)S(1)}, u32[]{:S(2)}, u32[]{:S(2)}) collective-permute-start(bf16[144,512]{1,0:T(8,128)(2,1)} %get-tuple-element.33), channel_id=1, source_target_pairs={{0,160},{8,168},{16,176},{24,184},{32,192},{40,200},{48,208},{56,2... | collective-permute-start | bytes 442376 | tf_op jit(solution)/shard_map/ppermute | solution.py:351
  85.3 5.4 %attend_chunk.4 = (bf16[144,512]{1,0:T(8,128)(2,1)S(1)}, bf16[144,512]{1,0:T(8,128)(2,1)S(1)}, bf16[144,512]{1,0:T(8,128)(2,1)S(1)}) custom-call(s32[1]{0:T(128)} %bitcast.me_ref.refs_0_, s32[32,1,128]{2,1,0:T(1,128)S(1)} %all-to-all-done.table_ref.refs_1_, bf16[128,64,256]{2,1,0:T(8,128)(2,1)} %bitcast.27, bf16[8,64,1024]{2,1,0:T(8,128)(2,1)} %all-to-all-done.1.refs_3_, ...), custom_call_target="tpu_custom_call" | custom-call | flops 805306368 | bytes 1572864 | tf_op jit(solution)/shard_map/attend_chunk/pallas_call | solution.py:297
  90.7 3.6 %collective-permute-start.10 = (bf16[144,512]{1,0:T(8,128)(2,1)S(1)}, bf16[144,512]{1,0:T(8,128)(2,1)S(1)}, u32[]{:S(2)}, u32[]{:S(2)}) collective-permute-start(bf16[144,512]{1,0:T(8,128)(2,1)S(1)} %get-tuple-element.30.refs_7_), channel_id=1, source_target_pairs={{0,192},{8,200},{16,208},{24,216},{32,224},{40,232},{48,240},{56,2... | collective-permute-start | bytes 442376 | tf_op jit(solution)/shard_map/ppermute | solution.py:351
  94.6 1.8 %collective-permute-start.12 = (bf16[144,512]{1,0:T(8,128)(2,1)S(1)}, bf16[144,512]{1,0:T(8,128)(2,1)S(1)}, u32[]{:S(2)}, u32[]{:S(2)}) collective-permute-start(bf16[144,512]{1,0:T(8,128)(2,1)S(1)} %get-tuple-element.37), channel_id=1, source_target_pairs={{0,32},{8,40},{16,48},{24,56},{32,64},{40,72},{48,80},{56,88},{64,... | collective-permute-start | bytes 442376 | tf_op jit(solution)/shard_map/ppermute | solution.py:351
  96.4 5.8 %attend_chunk.5 = (bf16[144,512]{1,0:T(8,128)(2,1)S(1)}, bf16[1024,4096]{1,0:T(8,128)(2,1)S(1)}) custom-call(s32[1]{0:T(128)} %bitcast.me_ref.refs_0_, s32[32,1,128]{2,1,0:T(1,128)S(1)} %all-to-all-done.table_ref.refs_1_, bf16[128,64,256]{2,1,0:T(8,128)(2,1)} %bitcast.28, bf16[8,64,1024]{2,1,0:T(8,128)(2,1)} %all-to-all-done.1.refs_3_, ...), custom_call_target="tpu_custom_call" | custom-call | flops 268435456 | bytes 524288 | tf_op jit(solution)/shard_map/attend_chunk/pallas_call | solution.py:297
  102.2 1.9 %merge_project.1 = bf16[64,4096]{1,0:T(8,128)(2,1)S(1)} custom-call(bf16[1024,4096]{1,0:T(8,128)(2,1)S(1)} %get-tuple-element.31.wide_ref, bf16[144,512]{1,0:T(8,128)(2,1)S(1)} %collective-permute-done.6.refs_7_.rest_0_, bf16[144,512]{1,0:T(8,128)(2,1)S(1)} %collective-permute-done.7.rest_1_, bf16[144,512]{1,0:T(8,128)(2,1)S(1)} %collective-permute-done.8.rest_2_, ...), custom_call_target="tpu_custom_call" | custom-call | flops 536870912 | bytes 8388608 | tf_op jit(solution)/shard_map/merge_project/pallas_call | solution.py:333
  104.3 1.5 %collective-permute-done.13 = bf16[4,8,4096]{2,1,0:T(8,128)(2,1)S(1)} collective-permute-done((bf16[4,8,4096]{2,1,0:T(8,128)(2,1)S(1)}, bf16[4,8,4096]{2,1,0:T(8,128)(2,1)S(1)}, u32[]{:S(2)}, u32[]{:S(2)}) %collective-permute-start.13) | collective-permute-done | bytes 262176 | tf_op jit(solution)/shard_map/ppermute | solution.py:362
  105.9 1.3 %collective-permute-start.14 = (bf16[8,4096]{1,0:T(8,128)(2,1)S(1)}, bf16[8,4096]{1,0:T(8,128)(2,1)S(1)}, u32[]{:S(2)}, u32[]{:S(2)}) collective-permute-start(bf16[8,4096]{1,0:T(8,128)(2,1)S(1)} %get-tuple-element.39), channel_id=1, source_target_pairs={{0,4},{1,5},{2,6},{3,7},{4,0},{5,1},{6,2},{7,3},{8,12},{9,13},{10,... | collective-permute-start | bytes 196616 | tf_op jit(solution)/shard_map/ppermute | solution.py:358
  107.2 2.2 %collective-permute-start.15 = (bf16[8,4096]{1,0:T(8,128)(2,1)S(1)}, bf16[8,4096]{1,0:T(8,128)(2,1)S(1)}, u32[]{:S(2)}, u32[]{:S(2)}) collective-permute-start(bf16[8,4096]{1,0:T(8,128)(2,1)S(1)} %get-tuple-element.41), channel_id=1, source_target_pairs={{0,2},{1,3},{2,4},{3,5},{4,6},{5,7},{6,0},{7,1},{8,10},{9,11},{10,... | collective-permute-start | bytes 196616 | tf_op jit(solution)/shard_map/ppermute | solution.py:358
  109.4 2.5 %collective-permute-done.14 = bf16[8,4096]{1,0:T(8,128)(2,1)S(1)} collective-permute-done((bf16[8,4096]{1,0:T(8,128)(2,1)S(1)}, bf16[8,4096]{1,0:T(8,128)(2,1)S(1)}, u32[]{:S(2)}, u32[]{:S(2)}) %collective-permute-start.14) | collective-permute-done | bytes 65568 | tf_op jit(solution)/shard_map/ppermute | solution.py:358
  111.8 3.0 %collective-permute-done.16 = bf16[8,4096]{1,0:T(8,128)(2,1)S(1)} collective-permute-done((bf16[8,4096]{1,0:T(8,128)(2,1)S(1)}, bf16[8,4096]{1,0:T(8,128)(2,1)S(1)}, u32[]{:S(2)}, u32[]{:S(2)}) %collective-permute-start.16) | collective-permute-done | bytes 65568 | tf_op jit(solution)/shard_map/ppermute | solution.py:358
  (33 shorter events, 6.1 us)
Async XLA Ops:
  0.0 61.3 %copy-start = (bf16[64,1024]{1,0:T(8,128)(2,1)S(1)}, bf16[64,1024]{1,0:T(8,128)(2,1)}, u32[]{:S(2)}) copy-start(bf16[64,1024]{1,0:T(8,128)(2,1)} %refs_7_.1) | copy-start | bytes 393220
  0.0 61.3 %copy-start.1 = (bf16[64,1,256]{2,0,1:T(8,128)(2,1)S(1)}, bf16[64,1,256]{2,0,1:T(8,128)(2,1)}, u32[]{:S(2)}) copy-start(bf16[64,1,256]{2,0,1:T(8,128)(2,1)} %param.8) | copy-start | bytes 98308
  0.7 0.7 copy-start.2
  1.3 0.7 copy-start.3
  2.9 21.0 %all-to-all-start = ((s32[32,1,128]{2,1,0:T(1,128)}), s32[32,1,128]{2,1,0:T(1,128)S(1)}, u32[]{:S(2)}, u32[]{:S(2)}) async-start(s32[32,1,128]{2,1,0:T(1,128)} %wanted_slots.1), calls=%async_computation | async-start | bytes 32768 | tf_op jit(solution)/shard_map/all_to_all | solution.py:381
  28.6 32.7 %all-to-all-start.1 = ((bf16[8,64,1024]{2,1,0:T(8,128)(2,1)}), bf16[8,64,1024]{2,1,0:T(8,128)(2,1)}, u32[]{:S(2)}, u32[]{:S(2)}) async-start(bf16[8,64,1024]{2,1,0:T(8,128)(2,1)} %get-tuple-element.22), calls=%async_computation.1 | async-start | bytes 2097152 | tf_op jit(solution)/shard_map/all_to_all | solution.py:393
  32.9 27.4 %collective-permute-start.3 = (bf16[16,64,256]{2,1,0:T(8,128)(2,1)S(1)}, bf16[16,64,256]{2,1,0:T(8,128)(2,1)S(1)}, u32[]{:S(2)}, u32[]{:S(2)}) collective-permute-start(bf16[16,64,256]{2,1,0:T(8,128)(2,1)S(1)} %get-tuple-element.26), channel_id=1, source_target_pairs={{0,8},{8,16},{16,24},{24,0},{32,40},{40,48},{48,56},{56,32},{64,72... | collective-permute-start | bytes 1572872 | tf_op jit(solution)/shard_map/ppermute | solution.py:346
  33.5 26.8 %collective-permute-start.4 = (bf16[16,64,256]{2,1,0:T(8,128)(2,1)}, bf16[16,64,256]{2,1,0:T(8,128)(2,1)S(1)}, u32[]{:S(2)}, u32[]{:S(2)}) collective-permute-start(bf16[16,64,256]{2,1,0:T(8,128)(2,1)} %get-tuple-element.27), channel_id=1, source_target_pairs={{0,16},{8,24},{16,0},{24,8},{32,48},{40,56},{48,32},{56,40},{64,80... | collective-permute-start | bytes 1572872 | tf_op jit(solution)/shard_map/ppermute | solution.py:346
  35.4 25.9 %collective-permute-start.5 = (bf16[16,64,256]{2,1,0:T(8,128)(2,1)}, bf16[16,64,256]{2,1,0:T(8,128)(2,1)S(1)}, u32[]{:S(2)}, u32[]{:S(2)}) collective-permute-start(bf16[16,64,256]{2,1,0:T(8,128)(2,1)} %get-tuple-element.28), channel_id=1, source_target_pairs={{0,24},{8,0},{16,8},{24,16},{32,56},{40,32},{48,40},{56,48},{64,88... | collective-permute-start | bytes 1572872 | tf_op jit(solution)/shard_map/ppermute | solution.py:346
  40.4 39.7 %collective-permute-start = (bf16[16,64,256]{2,1,0:T(8,128)(2,1)}, bf16[16,64,256]{2,1,0:T(8,128)(2,1)S(1)}, u32[]{:S(2)}, u32[]{:S(2)}) collective-permute-start(bf16[16,64,256]{2,1,0:T(8,128)(2,1)} %get-tuple-element.23), channel_id=1, source_target_pairs={{0,8},{8,16},{16,24},{24,0},{32,40},{40,48},{48,56},{56,32},{64,72... | collective-permute-start | bytes 1572872 | tf_op jit(solution)/shard_map/ppermute | solution.py:346
  41.4 43.3 %collective-permute-start.1 = (bf16[16,64,256]{2,1,0:T(8,128)(2,1)}, bf16[16,64,256]{2,1,0:T(8,128)(2,1)S(1)}, u32[]{:S(2)}, u32[]{:S(2)}) collective-permute-start(bf16[16,64,256]{2,1,0:T(8,128)(2,1)} %get-tuple-element.24), channel_id=1, source_target_pairs={{0,16},{8,24},{16,0},{24,8},{32,48},{40,56},{48,32},{56,40},{64,80... | collective-permute-start | bytes 1572872 | tf_op jit(solution)/shard_map/ppermute | solution.py:346
  60.3 25.0 %collective-permute-start.2 = (bf16[16,64,256]{2,1,0:T(8,128)(2,1)}, bf16[16,64,256]{2,1,0:T(8,128)(2,1)S(1)}, u32[]{:S(2)}, u32[]{:S(2)}) collective-permute-start(bf16[16,64,256]{2,1,0:T(8,128)(2,1)} %get-tuple-element.25), channel_id=1, source_target_pairs={{0,24},{8,0},{16,8},{24,16},{32,56},{40,32},{48,40},{56,48},{64,88... | collective-permute-start | bytes 1572872 | tf_op jit(solution)/shard_map/ppermute | solution.py:346
  68.0 17.3 %collective-permute-start.6 = (bf16[144,512]{1,0:T(8,128)(2,1)S(1)}, bf16[144,512]{1,0:T(8,128)(2,1)S(1)}, u32[]{:S(2)}, u32[]{:S(2)}) collective-permute-start(bf16[144,512]{1,0:T(8,128)(2,1)S(1)} %get-tuple-element.29), channel_id=1, source_target_pairs={{0,128},{8,136},{16,144},{24,152},{32,160},{40,168},{48,176},{56,1... | collective-permute-start | bytes 442376 | tf_op jit(solution)/shard_map/ppermute | solution.py:351
  73.8 20.8 %collective-permute-start.7 = (bf16[144,512]{1,0:T(8,128)(2,1)S(1)}, bf16[144,512]{1,0:T(8,128)(2,1)S(1)}, u32[]{:S(2)}, u32[]{:S(2)}) collective-permute-start(bf16[144,512]{1,0:T(8,128)(2,1)S(1)} %get-tuple-element.32), channel_id=1, source_target_pairs={{0,96},{8,104},{16,112},{24,120},{32,128},{40,136},{48,144},{56,15... | collective-permute-start | bytes 442376 | tf_op jit(solution)/shard_map/ppermute | solution.py:351
  80.1 22.1 %collective-permute-start.8 = (bf16[144,512]{1,0:T(8,128)(2,1)}, bf16[144,512]{1,0:T(8,128)(2,1)S(1)}, u32[]{:S(2)}, u32[]{:S(2)}) collective-permute-start(bf16[144,512]{1,0:T(8,128)(2,1)} %get-tuple-element.33), channel_id=1, source_target_pairs={{0,160},{8,168},{16,176},{24,184},{32,192},{40,200},{48,208},{56,2... | collective-permute-start | bytes 442376 | tf_op jit(solution)/shard_map/ppermute | solution.py:351
  84.7 17.5 %collective-permute-start.9 = (bf16[144,512]{1,0:T(8,128)(2,1)}, bf16[144,512]{1,0:T(8,128)(2,1)S(1)}, u32[]{:S(2)}, u32[]{:S(2)}) collective-permute-start(bf16[144,512]{1,0:T(8,128)(2,1)} %get-tuple-element.34), channel_id=1, source_target_pairs={{0,64},{8,72},{16,80},{24,88},{32,96},{40,104},{48,112},{56,120},{... | collective-permute-start | bytes 442376 | tf_op jit(solution)/shard_map/ppermute | solution.py:351
  90.7 11.5 %collective-permute-start.10 = (bf16[144,512]{1,0:T(8,128)(2,1)S(1)}, bf16[144,512]{1,0:T(8,128)(2,1)S(1)}, u32[]{:S(2)}, u32[]{:S(2)}) collective-permute-start(bf16[144,512]{1,0:T(8,128)(2,1)S(1)} %get-tuple-element.30.refs_7_), channel_id=1, source_target_pairs={{0,192},{8,200},{16,208},{24,216},{32,224},{40,232},{48,240},{56,2... | collective-permute-start | bytes 442376 | tf_op jit(solution)/shard_map/ppermute | solution.py:351
  94.4 7.9 %collective-permute-start.11 = (bf16[144,512]{1,0:T(8,128)(2,1)S(1)}, bf16[144,512]{1,0:T(8,128)(2,1)S(1)}, u32[]{:S(2)}, u32[]{:S(2)}) collective-permute-start(bf16[144,512]{1,0:T(8,128)(2,1)S(1)} %get-tuple-element.36), channel_id=1, source_target_pairs={{0,224},{8,232},{16,240},{24,248},{32,0},{40,8},{48,16},{56,24},{6... | collective-permute-start | bytes 442376 | tf_op jit(solution)/shard_map/ppermute | solution.py:351
  94.6 7.6 %collective-permute-start.12 = (bf16[144,512]{1,0:T(8,128)(2,1)S(1)}, bf16[144,512]{1,0:T(8,128)(2,1)S(1)}, u32[]{:S(2)}, u32[]{:S(2)}) collective-permute-start(bf16[144,512]{1,0:T(8,128)(2,1)S(1)} %get-tuple-element.37), channel_id=1, source_target_pairs={{0,32},{8,40},{16,48},{24,56},{32,64},{40,72},{48,80},{56,88},{64,... | collective-permute-start | bytes 442376 | tf_op jit(solution)/shard_map/ppermute | solution.py:351
  104.1 1.6 %collective-permute-start.13 = (bf16[4,8,4096]{2,1,0:T(8,128)(2,1)S(1)}, bf16[4,8,4096]{2,1,0:T(8,128)(2,1)S(1)}, u32[]{:S(2)}, u32[]{:S(2)}) collective-permute-start(bf16[4,8,4096]{2,1,0:T(8,128)(2,1)S(1)} %dynamic-slice_bitcast_fusion), channel_id=1, source_target_pairs={{0,1},{1,0},{2,3},{3,2},{4,5},{5,4},{6,7},{7,6},{8,9},{9,8},{10,11... | collective-permute-start | bytes 786440 | tf_op jit(solution)/shard_map/ppermute | solution.py:362
  105.9 6.0 %collective-permute-start.14 = (bf16[8,4096]{1,0:T(8,128)(2,1)S(1)}, bf16[8,4096]{1,0:T(8,128)(2,1)S(1)}, u32[]{:S(2)}, u32[]{:S(2)}) collective-permute-start(bf16[8,4096]{1,0:T(8,128)(2,1)S(1)} %get-tuple-element.39), channel_id=1, source_target_pairs={{0,4},{1,5},{2,6},{3,7},{4,0},{5,1},{6,2},{7,3},{8,12},{9,13},{10,... | collective-permute-start | bytes 196616 | tf_op jit(solution)/shard_map/ppermute | solution.py:358
  107.2 4.7 %collective-permute-start.15 = (bf16[8,4096]{1,0:T(8,128)(2,1)S(1)}, bf16[8,4096]{1,0:T(8,128)(2,1)S(1)}, u32[]{:S(2)}, u32[]{:S(2)}) collective-permute-start(bf16[8,4096]{1,0:T(8,128)(2,1)S(1)} %get-tuple-element.41), channel_id=1, source_target_pairs={{0,2},{1,3},{2,4},{3,5},{4,6},{5,7},{6,0},{7,1},{8,10},{9,11},{10,... | collective-permute-start | bytes 196616 | tf_op jit(solution)/shard_map/ppermute | solution.py:358
  109.4 5.5 %collective-permute-start.16 = (bf16[8,4096]{1,0:T(8,128)(2,1)S(1)}, bf16[8,4096]{1,0:T(8,128)(2,1)S(1)}, u32[]{:S(2)}, u32[]{:S(2)}) collective-permute-start(bf16[8,4096]{1,0:T(8,128)(2,1)S(1)} %get-tuple-element.40), channel_id=1, source_target_pairs={{0,6},{1,7},{2,0},{3,1},{4,2},{5,3},{6,4},{7,5},{8,14},{9,15},{10,... | collective-permute-start | bytes 196616 | tf_op jit(solution)/shard_map/ppermute | solution.py:358

commit v6 on v5

--- a/solution.py
+++ b/solution.py
@@ -49,7 +49,20 @@
     return lax.div(me_ref[0], NX), lax.rem(me_ref[0], NX)
 
 
-def wanted_kernel(length_ref, owner_ref, slot_ref, out_ref):
+def wanted_kernel(length_ref, owner_hbm, slot_hbm, query_hbm, out_ref, copies_ref, *scratch):
+    owner_ref, slot_ref, query_ref, sems, copy_sems = scratch
+    fetches = [
+        pltpu.make_async_copy(owner_hbm, owner_ref, sems.at[0]),
+        pltpu.make_async_copy(slot_hbm, slot_ref, sems.at[1]),
+        pltpu.make_async_copy(query_hbm, query_ref, sems.at[2]),
+    ]
+    for fetch in fetches:
+        fetch.start()
+    copies = [
+        pltpu.make_async_copy(query_ref, copies_ref.at[z], copy_sems.at[z]) for z in range(NZ)
+    ]
+    fetches[0].wait()
+    fetches[1].wait()
     count = owner_ref.shape[1]
     owners = count // CAP
     entry = lax.broadcasted_iota(jnp.int32, (1, count), 1)
@@ -77,17 +90,32 @@
     out_ref[...] = jnp.broadcast_to(
         (row[0:1].astype(jnp.int32) - 1).reshape(1, 1, count), out_ref.shape
     )
-
-
-def wanted_slots(prefix_blocks, block_owner, block_slot, store_count):
+    fetches[2].wait()
+    for copy in copies:
+        copy.start()
+    for copy in copies:
+        copy.wait()
+
+
+def wanted_slots(prefix_blocks, block_owner, block_slot, queries, store_count):
     return pl.pallas_call(
         wanted_kernel,
-        out_shape=jax.ShapeDtypeStruct((store_count, 1, block_owner.shape[1]), jnp.int32),
-        in_specs=[IN_SMEM, IN_VMEM, IN_VMEM],
-        out_specs=IN_VMEM,
+        out_shape=[
+            jax.ShapeDtypeStruct((store_count, 1, block_owner.shape[1]), jnp.int32),
+            jax.ShapeDtypeStruct((NZ,) + queries.shape, queries.dtype),
+        ],
+        in_specs=[IN_SMEM, IN_HBM, IN_HBM, IN_HBM],
+        out_specs=[IN_VMEM, IN_HBM],
+        scratch_shapes=[
+            pltpu.VMEM(block_owner.shape, block_owner.dtype),
+            pltpu.VMEM(block_slot.shape, block_slot.dtype),
+            pltpu.VMEM(queries.shape, queries.dtype),
+            pltpu.SemaphoreType.DMA((3,)),
+            pltpu.SemaphoreType.DMA((NZ,)),
+        ],
         compiler_params=pltpu.CompilerParams(vmem_limit_bytes=VMEM_LIMIT),
         name="wanted_slots",
-    )(prefix_blocks, block_owner, block_slot)
+    )(prefix_blocks, keep_in_hbm(block_owner), keep_in_hbm(block_slot), keep_in_hbm(queries))
 
 
 def slot_of(table_ref, home, owner, c, cache_ref):
@@ -109,42 +137,25 @@
     pltpu.make_async_copy(cache_ref.at[pl.ds(0, len(shifts) * CAP)], out, sem).wait()
 
 
-def pick_far_kernel(shifts, me_ref, table_ref, cache_ref, query_ref, *refs):
-    outs, (copies_ref, query_here, sems, query_sem, copy_sems) = refs[: NX - 1], refs[NX - 1 :]
-    fetch = pltpu.make_async_copy(query_ref, query_here, query_sem)
-    fetch.start()
+def pick_far_kernel(shifts, me_ref, table_ref, cache_ref, *refs):
+    outs, sems = refs[:-1], refs[-1]
     for k, out in enumerate(outs, 1):
         start_picks(shifts, k, me_ref, table_ref, cache_ref, out, sems.at[k - 1])
-    copies = [
-        pltpu.make_async_copy(query_here, copies_ref.at[z], copy_sems.at[z]) for z in range(NZ)
-    ]
-    fetch.wait()
-    for copy in copies:
-        copy.start()
     for k, out in enumerate(outs, 1):
         wait_picks(shifts, cache_ref, out, sems.at[k - 1])
-    for copy in copies:
-        copy.wait()
-
-
-def pick_far(shifts, me, table, cache, queries):
+
+
+def pick_far(shifts, me, table, cache):
     block = (len(shifts) * CAP, BLK, 2 * HD)
-    *sent, copies = pl.pallas_call(
+    return pl.pallas_call(
         functools.partial(pick_far_kernel, shifts),
-        out_shape=[pltpu.VMEM(block, cache.dtype)] * (NX - 1)
-        + [jax.ShapeDtypeStruct((NZ,) + queries.shape, queries.dtype)],
-        in_specs=[IN_SMEM, IN_SMEM, IN_HBM, IN_HBM],
-        out_specs=[IN_VMEM] * (NX - 1) + [IN_HBM],
-        scratch_shapes=[
-            pltpu.VMEM(queries.shape, queries.dtype),
-            pltpu.SemaphoreType.DMA((NX - 1,)),
-            pltpu.SemaphoreType.DMA,
-            pltpu.SemaphoreType.DMA((NZ,)),
-        ],
+        out_shape=[pltpu.VMEM(block, cache.dtype)] * (NX - 1),
+        in_specs=[IN_SMEM, IN_SMEM, IN_HBM],
+        out_specs=[IN_VMEM] * (NX - 1),
+        scratch_shapes=[pltpu.SemaphoreType.DMA((NX - 1,))],
         compiler_params=pltpu.CompilerParams(vmem_limit_bytes=VMEM_LIMIT),
         name="pick_far",
-    )(me, table, cache, keep_in_hbm(queries))
-    return sent, copies
+    )(me, table, cache)
 
 
 def pick_near_kernel(shifts, me_ref, table_ref, cache_ref, *refs):
@@ -377,7 +388,7 @@
 def local(queries, suffix_kv, kv_cache, block_owner, block_slot, prefix_blocks, out_weight):
     store_count = lax.axis_size("store")
     me = lax.axis_index("store").astype(jnp.int32).reshape(1)
-    wanted = wanted_slots(prefix_blocks, block_owner, block_slot, store_count)
+    wanted, copies = wanted_slots(prefix_blocks, block_owner, block_slot, queries, store_count)
     table = lax.all_to_all(wanted, "store", split_axis=0, concat_axis=0, tiled=True)
     cache = keep_in_hbm(kv_cache.reshape(kv_cache.shape[0], BLK, 2 * HD))
     suffix = suffix_kv.reshape(SUF, 2 * HD)
@@ -385,7 +396,7 @@
     away = near[:-1]
     over_x = lambda blocks: [x_permute(block, k) for k, block in enumerate(blocks, 1)]
     over_z = lambda shifts, parts: [z_permute(part, s) for s, part in zip(shifts, parts)]
-    far_sent, copies = pick_far(far, me, table, cache, queries)
+    far_sent = pick_far(far, me, table, cache)
     far_blocks = over_x(far_sent)
     near_blocks = over_x(pick_near(near, me, table, cache))
     z_groups = [[z * NX + x for z in range(NZ)] for x in range(NX)]

time: 116 us -> 114 us (0.983)
  blocking collectives: 0 us -> 20.8 us
  starting transfers between devices: 43 us -> 31.5 us
  waiting for transfers between devices: 40.5 us -> 31 us
  local copies, waits for them, and re-layouts: 1.37 us -> 0.07 us
    all_to_all x0 -> x1, blocking collectives: none -> 20.8 us  [local(): lax.all_to_all(wanted, 'store', split_axis=0, concat_axis=0, tiled=True)]
    all_to_all x1 -> x0, starting transfers between devices: 11.3 us -> none  [local(): lax.all_to_all(wanted, 'store', split_axis=0, concat_axis=0, tiled=True)]
    all_to_all x1 -> x0, waiting for transfers between devices: 9.65 us -> none  [local(): lax.all_to_all(wanted, 'store', split_axis=0, concat_axis=0, tiled=True)]
    pallas_call x1, Pallas kernels: 4.71 us -> 2.67 us  [pick_far(): pl.pallas_call(functools.partial(pick_far_kernel, shifts), out_shape=[plt...]
    unnamed x8 -> x4, local copies, waits for them, and re-layouts: 1.31 us -> 0.01 us
  transfers between devices with their start and end apart: 19 -> 18, of which waited for: 7 -> 6; matrix products, arithmetic and copies ran while one was open for 0% -> 0% of each run, Pallas kernels for 19% -> 21%
where the time goes in v6:
time: 114 us; the launch traced here: 113 us
  starting transfers between devices  31.5 us (28%)
  waiting for transfers between devices  31 us (27%)
  Pallas kernels  28.1 us (25%)
  blocking collectives  20.8 us (18%)
    ppermute x6, waiting for transfers between devices, x_permute(): return lax.ppermute(a, 'store', pairs)  24.1 us
    all_to_all x1, blocking collectives, local(): lax.all_to_all(wanted, 'store', split_axis=0, concat_axis=0, tiled=True)  20.8 us
    pallas_call x3, Pallas kernels, attend(): pl.pallas_call(functools.partial(attend_kernel, chunk, shifts, len(after)...  17.9 us
    ppermute x7, starting transfers between devices, z_permute(): return lax.ppermute(a, 'store', pairs)  17.2 us
    ppermute x6, starting transfers between devices, x_permute(): return lax.ppermute(a, 'store', pairs)  6.46 us
    ppermute x3, waiting for transfers between devices, y_permute(): return lax.ppermute(a, 'head', pairs)  5.47 us
    all_to_all x1, starting transfers between devices, local(): lax.all_to_all(copies, 'store', split_axis=0, concat_axis=0, tiled=True,...  4.24 us
    pallas_call x1, Pallas kernels, pick_near(): pl.pallas_call(functools.partial(pick_near_kernel, shifts), out_shape=[ja...  3.67 us
  transfers between devices with their start and end apart: 18, of which 6 were waited for; matrix products, arithmetic and copies ran while one was open for 0% of the time, Pallas kernels for 21%

profile of v6, /device:TPU:24, one launch (start us, length us, event | category | flops | bytes accessed | tf_op | source)
XLA Modules:
  0.0 113.1 jit_solution(1242704927630175156)
XLA Ops:
  0.7 2.0 %wanted_slots.1 = (s32[32,1,128]{2,1,0:T(1,128)S(1)}, bf16[8,64,1024]{2,1,0:T(8,128)(2,1)}) custom-call(s32[1]{0:T(128)S(6)} %copy.10.length_ref, s32[1,128]{1,0:T(1,128)} %owner_hbm.1, s32[1,128]{1,0:T(1,128)} %slot_hbm.1, bf16[64,1024]{1,0:T(8,128)(2,1)} %refs_7_.1), custom_call_target="tpu_custom_call" | custom-call | tf_op jit(solution)/shard_map/wanted_slots/pallas_call | solution.py:101
  2.7 20.8 %all_to_all.10.table_ref.refs_1_ = s32[32,1,128]{2,1,0:T(1,128)S(1)} all-to-all(s32[32,1,128]{2,1,0:T(1,128)S(1)} %get-tuple-element.23), channel_id=1, replica_groups=mesh['store'=32,'head'=8] {'store'}, dimensions={0} | all-to-all | bytes 32768 | tf_op jit(solution)/shard_map/all_to_all | solution.py:392
  23.6 4.2 %all-to-all-start.1 = ((bf16[8,64,1024]{2,1,0:T(8,128)(2,1)}), bf16[8,64,1024]{2,1,0:T(8,128)(2,1)}, u32[]{:S(2)}, u32[]{:S(2)}) async-start(bf16[8,64,1024]{2,1,0:T(8,128)(2,1)} %get-tuple-element.24), calls=%async_computation.1 | async-start | bytes 2097152 | tf_op jit(solution)/shard_map/all_to_all | solution.py:404
  27.8 2.7 %pick_far.1 = (bf16[16,64,256]{2,1,0:T(8,128)(2,1)S(1)}, bf16[16,64,256]{2,1,0:T(8,128)(2,1)S(1)}, bf16[16,64,256]{2,1,0:T(8,128)(2,1)S(1)}) custom-call(s32[1]{0:T(128)} %bitcast.me_ref.refs_0_, s32[32,1,128]{2,1,0:T(1,128)S(1)} %all_to_all.10.table_ref.refs_1_, bf16[128,64,256]{2,1,0:T(8,128)(2,1)} %bitcast.24), custom_call_target="tpu_custom_call" | custom-call | tf_op jit(solution)/shard_map/pick_far/pallas_call | solution.py:150
  31.1 2.2 %collective-permute-start.4 = (bf16[16,64,256]{2,1,0:T(8,128)(2,1)S(1)}, bf16[16,64,256]{2,1,0:T(8,128)(2,1)S(1)}, u32[]{:S(2)}, u32[]{:S(2)}) collective-permute-start(bf16[16,64,256]{2,1,0:T(8,128)(2,1)S(1)} %get-tuple-element.29), channel_id=1, source_target_pairs={{0,16},{8,24},{16,0},{24,8},{32,48},{40,56},{48,32},{56,40},{64,80... | collective-permute-start | bytes 1572872 | tf_op jit(solution)/shard_map/ppermute | solution.py:357
  33.3 1.4 %collective-permute-start.5 = (bf16[16,64,256]{2,1,0:T(8,128)(2,1)S(1)}, bf16[16,64,256]{2,1,0:T(8,128)(2,1)S(1)}, u32[]{:S(2)}, u32[]{:S(2)}) collective-permute-start(bf16[16,64,256]{2,1,0:T(8,128)(2,1)S(1)} %get-tuple-element.30), channel_id=1, source_target_pairs={{0,24},{8,0},{16,8},{24,16},{32,56},{40,32},{48,40},{56,48},{64,88... | collective-permute-start | bytes 1572872 | tf_op jit(solution)/shard_map/ppermute | solution.py:357
  34.7 3.7 %pick_near.1 = (bf16[16,64,256]{2,1,0:T(8,128)(2,1)}, bf16[16,64,256]{2,1,0:T(8,128)(2,1)}, bf16[16,64,256]{2,1,0:T(8,128)(2,1)}) custom-call(s32[1]{0:T(128)} %bitcast.me_ref.refs_0_, s32[32,1,128]{2,1,0:T(1,128)S(1)} %all_to_all.10.table_ref.refs_1_, bf16[128,64,256]{2,1,0:T(8,128)(2,1)} %bitcast.25), custom_call_target="tpu_custom_call" | custom-call | tf_op jit(solution)/shard_map/pick_near/pallas_call | solution.py:176
  39.2 1.4 %collective-permute-start.1 = (bf16[16,64,256]{2,1,0:T(8,128)(2,1)}, bf16[16,64,256]{2,1,0:T(8,128)(2,1)S(1)}, u32[]{:S(2)}, u32[]{:S(2)}) collective-permute-start(bf16[16,64,256]{2,1,0:T(8,128)(2,1)} %get-tuple-element.26), channel_id=1, source_target_pairs={{0,16},{8,24},{16,0},{24,8},{32,48},{40,56},{48,32},{56,40},{64,80... | collective-permute-start | bytes 1572872 | tf_op jit(solution)/shard_map/ppermute | solution.py:357
  40.7 17.2 %collective-permute-done.3.refs_4_ = bf16[16,64,256]{2,1,0:T(8,128)(2,1)S(1)} collective-permute-done((bf16[16,64,256]{2,1,0:T(8,128)(2,1)S(1)}, bf16[16,64,256]{2,1,0:T(8,128)(2,1)S(1)}, u32[]{:S(2)}, u32[]{:S(2)}) %collective-permute-start.3) | collective-permute-done | bytes 524320 | tf_op jit(solution)/shard_map/ppermute | solution.py:357
  57.9 0.8 collective-permute-done.5.refs_6_
  58.8 6.6 %attend_chunk.3 = (bf16[144,512]{1,0:T(8,128)(2,1)S(1)}, bf16[144,512]{1,0:T(8,128)(2,1)S(1)}, bf16[144,512]{1,0:T(8,128)(2,1)}, bf16[144,512]{1,0:T(8,128)(2,1)}, bf16[144,512]{1,0:T(8,128)(2,1)S(1)}) custom-call(s32[1]{0:T(128)} %bitcast.me_ref.refs_0_, s32[32,1,128]{2,1,0:T(1,128)S(1)} %all_to_all.10.table_ref.refs_1_, bf16[128,64,256]{2,1,0:T(8,128)(2,1)} %bitcast.26, ...), custom_call_target="tpu_custom_call" | custom-call | flops 1073741824 | bytes 2097152 | tf_op jit(solution)/shard_map/attend_chunk/pallas_call | solution.py:308
  65.4 5.9 %collective-permute-start.6 = (bf16[144,512]{1,0:T(8,128)(2,1)S(1)}, bf16[144,512]{1,0:T(8,128)(2,1)S(1)}, u32[]{:S(2)}, u32[]{:S(2)}) collective-permute-start(bf16[144,512]{1,0:T(8,128)(2,1)S(1)} %get-tuple-element.31), channel_id=1, source_target_pairs={{0,128},{8,136},{16,144},{24,152},{32,160},{40,168},{48,176},{56,1... | collective-permute-start | bytes 442376 | tf_op jit(solution)/shard_map/ppermute | solution.py:362
  71.8 6.0 %collective-permute-done.refs_4_ = bf16[16,64,256]{2,1,0:T(8,128)(2,1)S(1)} collective-permute-done((bf16[16,64,256]{2,1,0:T(8,128)(2,1)}, bf16[16,64,256]{2,1,0:T(8,128)(2,1)S(1)}, u32[]{:S(2)}, u32[]{:S(2)}) %collective-permute-start) | collective-permute-done | bytes 524320 | tf_op jit(solution)/shard_map/ppermute | solution.py:357
  77.7 4.6 %collective-permute-start.8 = (bf16[144,512]{1,0:T(8,128)(2,1)}, bf16[144,512]{1,0:T(8,128)(2,1)S(1)}, u32[]{:S(2)}, u32[]{:S(2)}) collective-permute-start(bf16[144,512]{1,0:T(8,128)(2,1)} %get-tuple-element.35), channel_id=1, source_target_pairs={{0,160},{8,168},{16,176},{24,184},{32,192},{40,200},{48,208},{56,2... | collective-permute-start | bytes 442376 | tf_op jit(solution)/shard_map/ppermute | solution.py:362
  82.9 5.4 %attend_chunk.4 = (bf16[144,512]{1,0:T(8,128)(2,1)S(1)}, bf16[144,512]{1,0:T(8,128)(2,1)S(1)}, bf16[144,512]{1,0:T(8,128)(2,1)S(1)}) custom-call(s32[1]{0:T(128)} %bitcast.me_ref.refs_0_, s32[32,1,128]{2,1,0:T(1,128)S(1)} %all_to_all.10.table_ref.refs_1_, bf16[128,64,256]{2,1,0:T(8,128)(2,1)} %bitcast.27, bf16[8,64,1024]{2,1,0:T(8,128)(2,1)} %all-to-all-done.1.refs_3_, ...), custom_call_target="tpu_custom_call" | custom-call | flops 805306368 | bytes 1572864 | tf_op jit(solution)/shard_map/attend_chunk/pallas_call | solution.py:308
  88.3 3.7 %collective-permute-start.10 = (bf16[144,512]{1,0:T(8,128)(2,1)S(1)}, bf16[144,512]{1,0:T(8,128)(2,1)S(1)}, u32[]{:S(2)}, u32[]{:S(2)}) collective-permute-start(bf16[144,512]{1,0:T(8,128)(2,1)S(1)} %get-tuple-element.32.refs_7_), channel_id=1, source_target_pairs={{0,192},{8,200},{16,208},{24,216},{32,224},{40,232},{48,240},{56,2... | collective-permute-start | bytes 442376 | tf_op jit(solution)/shard_map/ppermute | solution.py:362
  92.2 1.8 %collective-permute-start.12 = (bf16[144,512]{1,0:T(8,128)(2,1)S(1)}, bf16[144,512]{1,0:T(8,128)(2,1)S(1)}, u32[]{:S(2)}, u32[]{:S(2)}) collective-permute-start(bf16[144,512]{1,0:T(8,128)(2,1)S(1)} %get-tuple-element.39), channel_id=1, source_target_pairs={{0,32},{8,40},{16,48},{24,56},{32,64},{40,72},{48,80},{56,88},{64,... | collective-permute-start | bytes 442376 | tf_op jit(solution)/shard_map/ppermute | solution.py:362
  94.0 5.8 %attend_chunk.5 = (bf16[144,512]{1,0:T(8,128)(2,1)S(1)}, bf16[1024,4096]{1,0:T(8,128)(2,1)S(1)}) custom-call(s32[1]{0:T(128)} %bitcast.me_ref.refs_0_, s32[32,1,128]{2,1,0:T(1,128)S(1)} %all_to_all.10.table_ref.refs_1_, bf16[128,64,256]{2,1,0:T(8,128)(2,1)} %bitcast.28, bf16[8,64,1024]{2,1,0:T(8,128)(2,1)} %all-to-all-done.1.refs_3_, ...), custom_call_target="tpu_custom_call" | custom-call | flops 268435456 | bytes 524288 | tf_op jit(solution)/shard_map/attend_chunk/pallas_call | solution.py:308
  99.9 1.9 %merge_project.1 = bf16[64,4096]{1,0:T(8,128)(2,1)S(1)} custom-call(bf16[1024,4096]{1,0:T(8,128)(2,1)S(1)} %get-tuple-element.33.wide_ref, bf16[144,512]{1,0:T(8,128)(2,1)S(1)} %collective-permute-done.6.refs_7_.rest_0_, bf16[144,512]{1,0:T(8,128)(2,1)S(1)} %collective-permute-done.7.rest_1_, bf16[144,512]{1,0:T(8,128)(2,1)S(1)} %collective-permute-done.8.rest_2_, ...), custom_call_target="tpu_custom_call" | custom-call | flops 536870912 | bytes 8388608 | tf_op jit(solution)/shard_map/merge_project/pallas_call | solution.py:344
  101.9 1.5 %collective-permute-done.13 = bf16[4,8,4096]{2,1,0:T(8,128)(2,1)S(1)} collective-permute-done((bf16[4,8,4096]{2,1,0:T(8,128)(2,1)S(1)}, bf16[4,8,4096]{2,1,0:T(8,128)(2,1)S(1)}, u32[]{:S(2)}, u32[]{:S(2)}) %collective-permute-start.13) | collective-permute-done | bytes 262176 | tf_op jit(solution)/shard_map/ppermute | solution.py:373
  103.5 1.3 %collective-permute-start.14 = (bf16[8,4096]{1,0:T(8,128)(2,1)S(1)}, bf16[8,4096]{1,0:T(8,128)(2,1)S(1)}, u32[]{:S(2)}, u32[]{:S(2)}) collective-permute-start(bf16[8,4096]{1,0:T(8,128)(2,1)S(1)} %get-tuple-element.41), channel_id=1, source_target_pairs={{0,4},{1,5},{2,6},{3,7},{4,0},{5,1},{6,2},{7,3},{8,12},{9,13},{10,... | collective-permute-start | bytes 196616 | tf_op jit(solution)/shard_map/ppermute | solution.py:369
  104.8 2.2 %collective-permute-start.15 = (bf16[8,4096]{1,0:T(8,128)(2,1)S(1)}, bf16[8,4096]{1,0:T(8,128)(2,1)S(1)}, u32[]{:S(2)}, u32[]{:S(2)}) collective-permute-start(bf16[8,4096]{1,0:T(8,128)(2,1)S(1)} %get-tuple-element.43), channel_id=1, source_target_pairs={{0,2},{1,3},{2,4},{3,5},{4,6},{5,7},{6,0},{7,1},{8,10},{9,11},{10,... | collective-permute-start | bytes 196616 | tf_op jit(solution)/shard_map/ppermute | solution.py:369
  107.0 2.5 %collective-permute-done.14 = bf16[8,4096]{1,0:T(8,128)(2,1)S(1)} collective-permute-done((bf16[8,4096]{1,0:T(8,128)(2,1)S(1)}, bf16[8,4096]{1,0:T(8,128)(2,1)S(1)}, u32[]{:S(2)}, u32[]{:S(2)}) %collective-permute-start.14) | collective-permute-done | bytes 65568 | tf_op jit(solution)/shard_map/ppermute | solution.py:369
  109.4 3.0 %collective-permute-done.16 = bf16[8,4096]{1,0:T(8,128)(2,1)S(1)} collective-permute-done((bf16[8,4096]{1,0:T(8,128)(2,1)S(1)}, bf16[8,4096]{1,0:T(8,128)(2,1)S(1)}, u32[]{:S(2)}, u32[]{:S(2)}) %collective-permute-start.16) | collective-permute-done | bytes 65568 | tf_op jit(solution)/shard_map/ppermute | solution.py:369
  (28 shorter events, 3.6 us)
Async XLA Ops:
  0.0 58.8 %copy-start = (bf16[64,1024]{1,0:T(8,128)(2,1)S(1)}, bf16[64,1024]{1,0:T(8,128)(2,1)}, u32[]{:S(2)}) copy-start(bf16[64,1024]{1,0:T(8,128)(2,1)} %refs_7_.1) | copy-start | bytes 393220
  0.0 58.8 %copy-start.1 = (bf16[64,1,256]{2,0,1:T(8,128)(2,1)S(1)}, bf16[64,1,256]{2,0,1:T(8,128)(2,1)}, u32[]{:S(2)}) copy-start(bf16[64,1,256]{2,0,1:T(8,128)(2,1)} %param.8) | copy-start | bytes 98308
  23.6 35.2 %all-to-all-start.1 = ((bf16[8,64,1024]{2,1,0:T(8,128)(2,1)}), bf16[8,64,1024]{2,1,0:T(8,128)(2,1)}, u32[]{:S(2)}, u32[]{:S(2)}) async-start(bf16[8,64,1024]{2,1,0:T(8,128)(2,1)} %get-tuple-element.24), calls=%async_computation.1 | async-start | bytes 2097152 | tf_op jit(solution)/shard_map/all_to_all | solution.py:404
  30.5 27.4 %collective-permute-start.3 = (bf16[16,64,256]{2,1,0:T(8,128)(2,1)S(1)}, bf16[16,64,256]{2,1,0:T(8,128)(2,1)S(1)}, u32[]{:S(2)}, u32[]{:S(2)}) collective-permute-start(bf16[16,64,256]{2,1,0:T(8,128)(2,1)S(1)} %get-tuple-element.28), channel_id=1, source_target_pairs={{0,8},{8,16},{16,24},{24,0},{32,40},{40,48},{48,56},{56,32},{64,72... | collective-permute-start | bytes 1572872 | tf_op jit(solution)/shard_map/ppermute | solution.py:357
  31.1 26.8 %collective-permute-start.4 = (bf16[16,64,256]{2,1,0:T(8,128)(2,1)S(1)}, bf16[16,64,256]{2,1,0:T(8,128)(2,1)S(1)}, u32[]{:S(2)}, u32[]{:S(2)}) collective-permute-start(bf16[16,64,256]{2,1,0:T(8,128)(2,1)S(1)} %get-tuple-element.29), channel_id=1, source_target_pairs={{0,16},{8,24},{16,0},{24,8},{32,48},{40,56},{48,32},{56,40},{64,80... | collective-permute-start | bytes 1572872 | tf_op jit(solution)/shard_map/ppermute | solution.py:357
  33.3 25.5 %collective-permute-start.5 = (bf16[16,64,256]{2,1,0:T(8,128)(2,1)S(1)}, bf16[16,64,256]{2,1,0:T(8,128)(2,1)S(1)}, u32[]{:S(2)}, u32[]{:S(2)}) collective-permute-start(bf16[16,64,256]{2,1,0:T(8,128)(2,1)S(1)} %get-tuple-element.30), channel_id=1, source_target_pairs={{0,24},{8,0},{16,8},{24,16},{32,56},{40,32},{48,40},{56,48},{64,88... | collective-permute-start | bytes 1572872 | tf_op jit(solution)/shard_map/ppermute | solution.py:357
  38.4 39.4 %collective-permute-start = (bf16[16,64,256]{2,1,0:T(8,128)(2,1)}, bf16[16,64,256]{2,1,0:T(8,128)(2,1)S(1)}, u32[]{:S(2)}, u32[]{:S(2)}) collective-permute-start(bf16[16,64,256]{2,1,0:T(8,128)(2,1)} %get-tuple-element.25), channel_id=1, source_target_pairs={{0,8},{8,16},{16,24},{24,0},{32,40},{40,48},{48,56},{56,32},{64,72... | collective-permute-start | bytes 1572872 | tf_op jit(solution)/shard_map/ppermute | solution.py:357
  39.2 43.1 %collective-permute-start.1 = (bf16[16,64,256]{2,1,0:T(8,128)(2,1)}, bf16[16,64,256]{2,1,0:T(8,128)(2,1)S(1)}, u32[]{:S(2)}, u32[]{:S(2)}) collective-permute-start(bf16[16,64,256]{2,1,0:T(8,128)(2,1)} %get-tuple-element.26), channel_id=1, source_target_pairs={{0,16},{8,24},{16,0},{24,8},{32,48},{40,56},{48,32},{56,40},{64,80... | collective-permute-start | bytes 1572872 | tf_op jit(solution)/shard_map/ppermute | solution.py:357
  57.9 25.0 %collective-permute-start.2 = (bf16[16,64,256]{2,1,0:T(8,128)(2,1)}, bf16[16,64,256]{2,1,0:T(8,128)(2,1)S(1)}, u32[]{:S(2)}, u32[]{:S(2)}) collective-permute-start(bf16[16,64,256]{2,1,0:T(8,128)(2,1)} %get-tuple-element.27), channel_id=1, source_target_pairs={{0,24},{8,0},{16,8},{24,16},{32,56},{40,32},{48,40},{56,48},{64,88... | collective-permute-start | bytes 1572872 | tf_op jit(solution)/shard_map/ppermute | solution.py:357
  65.4 17.5 %collective-permute-start.6 = (bf16[144,512]{1,0:T(8,128)(2,1)S(1)}, bf16[144,512]{1,0:T(8,128)(2,1)S(1)}, u32[]{:S(2)}, u32[]{:S(2)}) collective-permute-start(bf16[144,512]{1,0:T(8,128)(2,1)S(1)} %get-tuple-element.31), channel_id=1, source_target_pairs={{0,128},{8,136},{16,144},{24,152},{32,160},{40,168},{48,176},{56,1... | collective-permute-start | bytes 442376 | tf_op jit(solution)/shard_map/ppermute | solution.py:362
  71.3 21.0 %collective-permute-start.7 = (bf16[144,512]{1,0:T(8,128)(2,1)S(1)}, bf16[144,512]{1,0:T(8,128)(2,1)S(1)}, u32[]{:S(2)}, u32[]{:S(2)}) collective-permute-start(bf16[144,512]{1,0:T(8,128)(2,1)S(1)} %get-tuple-element.34), channel_id=1, source_target_pairs={{0,96},{8,104},{16,112},{24,120},{32,128},{40,136},{48,144},{56,15... | collective-permute-start | bytes 442376 | tf_op jit(solution)/shard_map/ppermute | solution.py:362
  77.7 22.1 %collective-permute-start.8 = (bf16[144,512]{1,0:T(8,128)(2,1)}, bf16[144,512]{1,0:T(8,128)(2,1)S(1)}, u32[]{:S(2)}, u32[]{:S(2)}) collective-permute-start(bf16[144,512]{1,0:T(8,128)(2,1)} %get-tuple-element.35), channel_id=1, source_target_pairs={{0,160},{8,168},{16,176},{24,184},{32,192},{40,200},{48,208},{56,2... | collective-permute-start | bytes 442376 | tf_op jit(solution)/shard_map/ppermute | solution.py:362
  82.3 17.5 %collective-permute-start.9 = (bf16[144,512]{1,0:T(8,128)(2,1)}, bf16[144,512]{1,0:T(8,128)(2,1)S(1)}, u32[]{:S(2)}, u32[]{:S(2)}) collective-permute-start(bf16[144,512]{1,0:T(8,128)(2,1)} %get-tuple-element.36), channel_id=1, source_target_pairs={{0,64},{8,72},{16,80},{24,88},{32,96},{40,104},{48,112},{56,120},{... | collective-permute-start | bytes 442376 | tf_op jit(solution)/shard_map/ppermute | solution.py:362
  88.3 11.5 %collective-permute-start.10 = (bf16[144,512]{1,0:T(8,128)(2,1)S(1)}, bf16[144,512]{1,0:T(8,128)(2,1)S(1)}, u32[]{:S(2)}, u32[]{:S(2)}) collective-permute-start(bf16[144,512]{1,0:T(8,128)(2,1)S(1)} %get-tuple-element.32.refs_7_), channel_id=1, source_target_pairs={{0,192},{8,200},{16,208},{24,216},{32,224},{40,232},{48,240},{56,2... | collective-permute-start | bytes 442376 | tf_op jit(solution)/shard_map/ppermute | solution.py:362
  92.0 7.9 %collective-permute-start.11 = (bf16[144,512]{1,0:T(8,128)(2,1)S(1)}, bf16[144,512]{1,0:T(8,128)(2,1)S(1)}, u32[]{:S(2)}, u32[]{:S(2)}) collective-permute-start(bf16[144,512]{1,0:T(8,128)(2,1)S(1)} %get-tuple-element.38), channel_id=1, source_target_pairs={{0,224},{8,232},{16,240},{24,248},{32,0},{40,8},{48,16},{56,24},{6... | collective-permute-start | bytes 442376 | tf_op jit(solution)/shard_map/ppermute | solution.py:362
  92.2 7.6 %collective-permute-start.12 = (bf16[144,512]{1,0:T(8,128)(2,1)S(1)}, bf16[144,512]{1,0:T(8,128)(2,1)S(1)}, u32[]{:S(2)}, u32[]{:S(2)}) collective-permute-start(bf16[144,512]{1,0:T(8,128)(2,1)S(1)} %get-tuple-element.39), channel_id=1, source_target_pairs={{0,32},{8,40},{16,48},{24,56},{32,64},{40,72},{48,80},{56,88},{64,... | collective-permute-start | bytes 442376 | tf_op jit(solution)/shard_map/ppermute | solution.py:362
  101.7 1.6 %collective-permute-start.13 = (bf16[4,8,4096]{2,1,0:T(8,128)(2,1)S(1)}, bf16[4,8,4096]{2,1,0:T(8,128)(2,1)S(1)}, u32[]{:S(2)}, u32[]{:S(2)}) collective-permute-start(bf16[4,8,4096]{2,1,0:T(8,128)(2,1)S(1)} %dynamic-slice_bitcast_fusion), channel_id=1, source_target_pairs={{0,1},{1,0},{2,3},{3,2},{4,5},{5,4},{6,7},{7,6},{8,9},{9,8},{10,11... | collective-permute-start | bytes 786440 | tf_op jit(solution)/shard_map/ppermute | solution.py:373
  103.5 6.0 %collective-permute-start.14 = (bf16[8,4096]{1,0:T(8,128)(2,1)S(1)}, bf16[8,4096]{1,0:T(8,128)(2,1)S(1)}, u32[]{:S(2)}, u32[]{:S(2)}) collective-permute-start(bf16[8,4096]{1,0:T(8,128)(2,1)S(1)} %get-tuple-element.41), channel_id=1, source_target_pairs={{0,4},{1,5},{2,6},{3,7},{4,0},{5,1},{6,2},{7,3},{8,12},{9,13},{10,... | collective-permute-start | bytes 196616 | tf_op jit(solution)/shard_map/ppermute | solution.py:369
  104.8 4.7 %collective-permute-start.15 = (bf16[8,4096]{1,0:T(8,128)(2,1)S(1)}, bf16[8,4096]{1,0:T(8,128)(2,1)S(1)}, u32[]{:S(2)}, u32[]{:S(2)}) collective-permute-start(bf16[8,4096]{1,0:T(8,128)(2,1)S(1)} %get-tuple-element.43), channel_id=1, source_target_pairs={{0,2},{1,3},{2,4},{3,5},{4,6},{5,7},{6,0},{7,1},{8,10},{9,11},{10,... | collective-permute-start | bytes 196616 | tf_op jit(solution)/shard_map/ppermute | solution.py:369
  107.0 5.5 %collective-permute-start.16 = (bf16[8,4096]{1,0:T(8,128)(2,1)S(1)}, bf16[8,4096]{1,0:T(8,128)(2,1)S(1)}, u32[]{:S(2)}, u32[]{:S(2)}) collective-permute-start(bf16[8,4096]{1,0:T(8,128)(2,1)S(1)} %get-tuple-element.42), channel_id=1, source_target_pairs={{0,6},{1,7},{2,0},{3,1},{4,2},{5,3},{6,4},{7,5},{8,14},{9,15},{10,... | collective-permute-start | bytes 196616 | tf_op jit(solution)/shard_map/ppermute | solution.py:369

commit v7 on v6

--- a/solution.py
+++ b/solution.py
@@ -25,7 +25,8 @@
 NEG_FILL = -1e30
 FLOOR = -1e9
 TO_LOG2 = math.log2(math.e) / math.sqrt(HD)
-CHUNKS = ((4, 3, 5, 2), (6, 7, 1, 0))
+CHUNKS = ((4, 3, 5), (2, 6, 7, 1, 0))
+RELAY = 2
 WIDE_PARTS = 8
 VMEM_LIMIT = 24 * 1024 * 1024
 
@@ -61,8 +62,10 @@
     copies = [
         pltpu.make_async_copy(query_ref, copies_ref.at[z], copy_sems.at[z]) for z in range(NZ)
     ]
-    fetches[0].wait()
-    fetches[1].wait()
+    for fetch in fetches:
+        fetch.wait()
+    for copy in copies:
+        copy.start()
     count = owner_ref.shape[1]
     owners = count // CAP
     entry = lax.broadcasted_iota(jnp.int32, (1, count), 1)
@@ -90,9 +93,6 @@
     out_ref[...] = jnp.broadcast_to(
         (row[0:1].astype(jnp.int32) - 1).reshape(1, 1, count), out_ref.shape
     )
-    fetches[2].wait()
-    for copy in copies:
-        copy.start()
     for copy in copies:
         copy.wait()
 
@@ -191,18 +191,31 @@
     return jnp.concatenate([block[:, i * HD : (i + 1) * HD] for i in range(GROUP)], axis=0)
 
 
-def partial_sums(score_parts, value_parts):
-    peak = functools.reduce(
-        jnp.maximum, [jnp.max(part, axis=0, keepdims=True) for part in score_parts]
-    )
+def partial_sums(scores, lives, values):
+    pieces = []
+    for part, live in zip(scores, lives):
+        size = part.shape[0] // len(live)
+        pieces.append([part[c * size : (c + 1) * size] for c in range(len(live))])
+    peaks = [
+        jnp.where(alive, jnp.max(piece, axis=0, keepdims=True), NEG_FILL)
+        for row, live in zip(pieces, lives)
+        for piece, alive in zip(row, live)
+    ]
+    peak = functools.reduce(jnp.maximum, peaks)
     shift = jnp.maximum(peak * TO_LOG2, FLOOR).astype(jnp.bfloat16).astype(jnp.float32)
     total = jnp.zeros((1, ROWS), jnp.float32)
     acc = jnp.zeros((HD, ROWS), jnp.float32)
-    for part, values in zip(score_parts, value_parts):
-        expo = jnp.exp2(part * TO_LOG2 - shift)
+    for row, live, value in zip(pieces, lives, values):
+        expo = jnp.concatenate(
+            [
+                jnp.exp2(piece * TO_LOG2 - jnp.where(alive, shift, -NEG_FILL))
+                for piece, alive in zip(row, live)
+            ],
+            axis=0,
+        )
         total += jnp.sum(expo, axis=0, keepdims=True)
         acc += lax.dot_general(
-            values, expo.astype(jnp.bfloat16), CONTRACT_FIRST, preferred_element_type=jnp.float32
+            value, expo.astype(jnp.bfloat16), CONTRACT_FIRST, preferred_element_type=jnp.float32
         )
     return shift, total, acc
 
@@ -215,51 +228,62 @@
     out_ref[HD:, :] = stats.astype(jnp.bfloat16)
 
 
+def merge_parts(parts):
+    top = functools.reduce(jnp.maximum, [part[0] for part in parts])
+    factors = [jnp.exp2(part[0] - top) for part in parts]
+    total = sum(f * part[1] for f, part in zip(factors, parts))
+    return top, total, sum(f * part[2] for f, part in zip(factors, parts))
+
+
 def read_packet(ref):
     stats = ref[HD:, :].astype(jnp.float32)
     return stats[0:1], stats[1:2] + stats[2:3], ref[:HD, :].astype(jnp.float32)
 
 
-def cached_part(shift, n, me_ref, table_ref, rows, blocks):
+def cached_scores(shift, n, me_ref, table_ref, rows, blocks):
     zo, xr = coordinates(me_ref)
     home = rem(zo + shift, NZ) * NX + xr
-    score_parts, value_parts = [], []
+    scores, lives, values = [], [], []
     for k in (1, 2, 3, 0):
         owner = zo * NX + rem(xr - k, NX)
         both = blocks[k][n * CAP : (n + 1) * CAP].reshape(CAP * BLK, 2 * HD)
-        scores = lax.dot_general(both[:, :HD], rows, CONTRACT_LAST, preferred_element_type=jnp.float32)
-        live = [
-            jnp.where(
-                table_ref[home, 0, owner * CAP + c] >= 0,
-                scores[c * BLK : (c + 1) * BLK],
-                NEG_FILL,
-            )
-            for c in range(CAP)
-        ]
-        score_parts.append(jnp.concatenate(live, axis=0))
-        value_parts.append(both[:, HD:])
-    return partial_sums(score_parts, value_parts)
+        scores.append(
+            lax.dot_general(both[:, :HD], rows, CONTRACT_LAST, preferred_element_type=jnp.float32)
+        )
+        lives.append([table_ref[home, 0, owner * CAP + c] >= 0 for c in range(CAP)])
+        values.append(both[:, HD:])
+    return scores, lives, values
 
 
 def suffix_part(rows, both):
     scores = lax.dot_general(both[:, :HD], rows, CONTRACT_LAST, preferred_element_type=jnp.float32)
     key = lax.broadcasted_iota(jnp.int32, (SUF, ROWS), 0)
     token = lax.rem(lax.broadcasted_iota(jnp.int32, (SUF, ROWS), 1), SUF)
-    return partial_sums([jnp.where(key <= token, scores, NEG_FILL)], [both[:, HD:]])
-
-
-def attend_kernel(chunk, shifts, n_after, with_suffix, with_weight, *refs):
+    return partial_sums([jnp.where(key <= token, scores, NEG_FILL)], [[True]], [both[:, HD:]])
+
+
+def attend_kernel(chunk, shifts, has, *refs):
     refs = list(refs)
     take = lambda n: [refs.pop(0) for _ in range(n)]
     me_ref, table_ref, cache_ref, z_query_ref = take(4)
     arrived = take(NX - 1)
-    own_refs = take(2 * with_suffix)
-    take(n_after)
-    weight_ref = take(1)[0] if with_weight else None
-    packet_refs = take(len(shifts) + with_suffix)
-    wide_ref = take(1)[0] if with_weight else None
+    own_refs = take(2 * has["suffix"])
+    relayed = take(2 * has["relayed"])
+    weight_ref = take(2)[0] if has["weight"] else None
+    packet_refs = take(2 if has["relay"] else len(shifts))
+    own_packet = take(1)[0] if has["suffix"] else None
+    wide_ref = take(1)[0] if has["weight"] else None
     here, query_here, block_sems, query_sems, wide_sems = take(5)
     zo, _ = coordinates(me_ref)
+    wide = []
+    if has["weight"]:
+        step = weight_ref.shape[0] // WIDE_PARTS
+        for n in range(WIDE_PARTS):
+            part = pl.ds(n * step, step)
+            wide.append(
+                pltpu.make_async_copy(weight_ref.at[part, :], wide_ref.at[part, :], wide_sems.at[n])
+            )
+            wide[-1].start()
     first = chunk.index(shifts[0]) * CAP
     fetches = [
         pltpu.make_async_copy(
@@ -276,40 +300,49 @@
     for fetch in fetches:
         fetch.start()
     start_picks(shifts, 0, me_ref, table_ref, cache_ref, here.at[0], block_sems.at[0])
-    wide = []
-    if with_weight:
-        step = weight_ref.shape[0] // WIDE_PARTS
-        for n in range(WIDE_PARTS):
-            part = pl.ds(n * step, step)
-            wide.append(
-                pltpu.make_async_copy(weight_ref.at[part, :], wide_ref.at[part, :], wide_sems.at[n])
-            )
-            wide[-1].start()
-    if with_suffix:
+    if has["suffix"]:
         part = suffix_part(head_rows(own_refs[0][...]), own_refs[1][...])
-        write_packet(packet_refs[-1], *part)
+        write_packet(own_packet, *part)
     for fetch in fetches:
         fetch.wait()
     wait_picks(shifts, cache_ref, here.at[0], block_sems.at[0])
+    def scores_of(n):
+        blocks = [here.at[k] for k in range(NX)]
+        return cached_scores(shifts[n], n, me_ref, table_ref, head_rows(query_here[n]), blocks)
+
+    following = scores_of(0)
     for n, shift in enumerate(shifts):
-        rows = head_rows(query_here[n])
-        part = cached_part(shift, n, me_ref, table_ref, rows, [here.at[k] for k in range(NX)])
-        write_packet(packet_refs[n], *part)
+        current = following
+        if n + 1 < len(shifts):
+            following = scores_of(n + 1)
+        part = partial_sums(*current)
+        if has["relay"]:
+            out = {4: packet_refs[0].at[0], 3: packet_refs[0].at[1], 5: packet_refs[1]}[shift]
+        else:
+            out = packet_refs[n]
+        if has["relayed"] and shift in (2, 1, 7):
+            other = {2: relayed[0].at[0], 1: relayed[0].at[1], 7: relayed[1]}[shift]
+            part = merge_parts([part, read_packet(other)])
+        write_packet(out, *part)
     for copy in wide:
         copy.wait()
 
 
-def attend(chunk, shifts, me, table, cache, z_queries, arrived, own=(), after=(), weight=None):
+def attend(chunk, shifts, me, table, cache, z_queries, arrived, own=(), relay=False, relayed=(), weight=()):
     keys = len(shifts) * NX * CAP * BLK
-    with_weight = weight is not None
-    n_packets = len(shifts) + bool(own)
-    extra = list(after) + ([weight] if with_weight else [])
-    wide = [pltpu.VMEM(weight.shape, weight.dtype)] if with_weight else []
+    has = dict(suffix=bool(own), relay=relay, relayed=bool(relayed), weight=bool(weight))
+    packet = jax.ShapeDtypeStruct((PACKET, ROWS), jnp.bfloat16)
+    pair = jax.ShapeDtypeStruct((2, PACKET, ROWS), jnp.bfloat16)
+    packets = ([pair, packet] if relay else [packet] * len(shifts)) + [packet] * bool(own)
+    wide = [pltpu.VMEM(weight[0].shape, weight[0].dtype)] if weight else []
     outs = pl.pallas_call(
-        functools.partial(attend_kernel, chunk, shifts, len(after), bool(own), with_weight),
-        out_shape=[jax.ShapeDtypeStruct((PACKET, ROWS), jnp.bfloat16)] * n_packets + wide,
-        in_specs=[IN_SMEM] * 2 + [IN_HBM] * (NX + 1) + [IN_VMEM] * len(own) + [IN_HBM] * len(extra),
-        out_specs=[IN_VMEM] * (n_packets + len(wide)),
+        functools.partial(attend_kernel, chunk, shifts, has),
+        out_shape=packets + wide,
+        in_specs=[IN_SMEM] * 2
+        + [IN_HBM] * (NX + 1)
+        + [IN_VMEM] * (len(own) + len(relayed))
+        + [IN_HBM] * len(weight),
+        out_specs=[IN_VMEM] * len(packets + wide),
         scratch_shapes=[
             pltpu.VMEM((NX, len(shifts) * CAP, BLK, 2 * HD), cache.dtype),
             pltpu.VMEM((len(shifts), SUF, GROUP * HD), jnp.bfloat16),
@@ -322,17 +355,13 @@
             flops=4 * keys * ROWS * HD, bytes_accessed=4 * keys * HD, transcendentals=keys * ROWS
         ),
         name="attend_chunk",
-    )(me, table, cache, z_queries, *arrived, *own, *extra)
-    return outs[:n_packets], outs[n_packets:]
+    )(me, table, cache, z_queries, *arrived, *own, *relayed, *weight)
+    return outs
 
 
 def finish_kernel(wide_ref, *rest):
     packet_refs, out_ref = rest[:-1], rest[-1]
-    parts = [read_packet(ref) for ref in packet_refs]
-    top = functools.reduce(jnp.maximum, [part[0] for part in parts])
-    factors = [jnp.exp2(part[0] - top) for part in parts]
-    row_sum = sum(f * part[1] for f, part in zip(factors, parts))
-    summed = sum(f * part[2] for f, part in zip(factors, parts))
+    _, row_sum, summed = merge_parts([read_packet(ref) for ref in packet_refs])
     rows = (summed / row_sum).T.astype(jnp.bfloat16)
     attended = jnp.concatenate([rows[i * SUF : (i + 1) * SUF] for i in range(GROUP)], axis=1)
     out_ref[...] = jnp.dot(
@@ -406,14 +435,14 @@
         )
     )
     common = (me, table, cache, z_queries)
-    parts, _ = attend(far, far, *common, far_blocks, own=(queries, suffix))
-    packets = over_z(far, parts) + [parts[-1]]
-    parts, _ = attend(near, away, *common, near_blocks, after=packets[:1])
-    packets += over_z(away, parts)
-    home, (wide,) = attend(
-        near, near[-1:], *common, near_blocks, after=parts[:1], weight=keep_in_hbm(out_weight)
-    )
-    return sum_heads(finish(wide, packets + list(home)))
+    plus, minus, own = attend(far, far, *common, far_blocks, own=(queries, suffix), relay=True)
+    relayed = (z_permute(plus, RELAY), z_permute(minus, -RELAY))
+    parts = attend(near, away, *common, near_blocks, relayed=relayed)
+    packets = over_z(away, parts) + [own]
+    home, wide = attend(
+        near, near[-1:], *common, near_blocks, weight=(keep_in_hbm(out_weight), parts[0])
+    )
+    return sum_heads(finish(wide, packets + [home]))
 
 
 def solution(mesh):

time: 114 us -> 113 us (level); the launches traced: 113 us -> 111 us
  starting transfers between devices: 31.5 us -> 25.6 us
  waiting for transfers between devices: 31 us -> 36 us
  Pallas kernels: 28.1 us -> 26.6 us
    ppermute x7 -> x6, starting transfers between devices: 17.2 us -> 11.3 us  [z_permute(): return lax.ppermute(a, 'store', pairs)]
    all_to_all x1, waiting for transfers between devices: 0.01 us -> 2.53 us  [local(): lax.all_to_all(copies, 'store', split_axis=0, concat_axis=0, tiled=True,...]
    ppermute x6, waiting for transfers between devices: 24.1 us -> 25.6 us  [x_permute(): return lax.ppermute(a, 'store', pairs)]
    pallas_call x3, Pallas kernels: 17.9 us -> 16.5 us  [attend(): pl.pallas_call(functools.partial(attend_kernel, chunk, shifts, has), out_...]
  transfers between devices with their start and end apart: 18 -> 17, of which waited for: 6 -> 9; matrix products, arithmetic and copies ran while one was open for 0% -> 0% of each run, Pallas kernels for 21% -> 15%
where the time goes in v7:
time: 113 us; the launch traced here: 111 us
  waiting for transfers between devices  36 us (32%)
  Pallas kernels  26.6 us (24%)
  starting transfers between devices  25.6 us (23%)
  blocking collectives  20.8 us (18%)
    ppermute x6, waiting for transfers between devices, x_permute(): return lax.ppermute(a, 'store', pairs)  25.6 us
    all_to_all x1, blocking collectives, local(): lax.all_to_all(wanted, 'store', split_axis=0, concat_axis=0, tiled=True)  20.8 us
    pallas_call x3, Pallas kernels, attend(): pl.pallas_call(functools.partial(attend_kernel, chunk, shifts, has), out_...  16.5 us
    ppermute x6, starting transfers between devices, z_permute(): return lax.ppermute(a, 'store', pairs)  11.3 us
    ppermute x6, starting transfers between devices, x_permute(): return lax.ppermute(a, 'store', pairs)  6.51 us
    ppermute x3, waiting for transfers between devices, y_permute(): return lax.ppermute(a, 'head', pairs)  5.47 us
    all_to_all x1, starting transfers between devices, local(): lax.all_to_all(copies, 'store', split_axis=0, concat_axis=0, tiled=True,...  4.25 us
    pallas_call x1, Pallas kernels, pick_near(): pl.pallas_call(functools.partial(pick_near_kernel, shifts), out_shape=[ja...  3.99 us
  transfers between devices with their start and end apart: 17, of which 9 were waited for; matrix products, arithmetic and copies ran while one was open for 0% of the time, Pallas kernels for 15%

profile of v7, /device:TPU:24, one launch (start us, length us, event | category | flops | bytes accessed | tf_op | source)
XLA Modules:
  0.0 110.7 jit_solution(1349609292960646362)
XLA Ops:
  0.7 2.0 %wanted_slots.1 = (s32[32,1,128]{2,1,0:T(1,128)S(1)}, bf16[8,64,1024]{2,1,0:T(8,128)(2,1)}) custom-call(s32[1]{0:T(128)S(6)} %copy.10.length_ref, s32[1,128]{1,0:T(1,128)} %owner_hbm.1, s32[1,128]{1,0:T(1,128)} %slot_hbm.1, bf16[64,1024]{1,0:T(8,128)(2,1)} %refs_7_.2), custom_call_target="tpu_custom_call" | custom-call | tf_op jit(solution)/shard_map/wanted_slots/pallas_call | solution.py:101
  2.7 20.8 %all_to_all.10.table_ref.refs_1_ = s32[32,1,128]{2,1,0:T(1,128)S(1)} all-to-all(s32[32,1,128]{2,1,0:T(1,128)S(1)} %get-tuple-element.22), channel_id=1, replica_groups=mesh['store'=32,'head'=8] {'store'}, dimensions={0} | all-to-all | bytes 32768 | tf_op jit(solution)/shard_map/all_to_all | solution.py:421
  23.5 4.2 %all-to-all-start.1 = ((bf16[8,64,1024]{2,1,0:T(8,128)(2,1)}), bf16[8,64,1024]{2,1,0:T(8,128)(2,1)}, u32[]{:S(2)}, u32[]{:S(2)}) async-start(bf16[8,64,1024]{2,1,0:T(8,128)(2,1)} %get-tuple-element.23), calls=%async_computation.1 | async-start | bytes 2097152 | tf_op jit(solution)/shard_map/all_to_all | solution.py:433
  27.8 2.4 %pick_far.1 = (bf16[12,64,256]{2,1,0:T(8,128)(2,1)S(1)}, bf16[12,64,256]{2,1,0:T(8,128)(2,1)S(1)}, bf16[12,64,256]{2,1,0:T(8,128)(2,1)S(1)}) custom-call(s32[1]{0:T(128)} %bitcast.me_ref.refs_0_, s32[32,1,128]{2,1,0:T(1,128)S(1)} %all_to_all.10.table_ref.refs_1_, bf16[128,64,256]{2,1,0:T(8,128)(2,1)} %bitcast.24), custom_call_target="tpu_custom_call" | custom-call | tf_op jit(solution)/shard_map/pick_far/pallas_call | solution.py:150
  30.9 2.0 %collective-permute-start.4 = (bf16[12,64,256]{2,1,0:T(8,128)(2,1)S(1)}, bf16[12,64,256]{2,1,0:T(8,128)(2,1)S(1)}, u32[]{:S(2)}, u32[]{:S(2)}) collective-permute-start(bf16[12,64,256]{2,1,0:T(8,128)(2,1)S(1)} %get-tuple-element.28), channel_id=1, source_target_pairs={{0,16},{8,24},{16,0},{24,8},{32,48},{40,56},{48,32},{56,40},{64,80... | collective-permute-start | bytes 1179656 | tf_op jit(solution)/shard_map/ppermute | solution.py:386
  34.0 4.0 %pick_near.1 = (bf16[20,64,256]{2,1,0:T(8,128)(2,1)}, bf16[20,64,256]{2,1,0:T(8,128)(2,1)}, bf16[20,64,256]{2,1,0:T(8,128)(2,1)}) custom-call(s32[1]{0:T(128)} %bitcast.me_ref.refs_0_, s32[32,1,128]{2,1,0:T(1,128)S(1)} %all_to_all.10.table_ref.refs_1_, bf16[128,64,256]{2,1,0:T(8,128)(2,1)} %bitcast.25), custom_call_target="tpu_custom_call" | custom-call | tf_op jit(solution)/shard_map/pick_near/pallas_call | solution.py:176
  39.0 1.7 %collective-permute-start.1 = (bf16[20,64,256]{2,1,0:T(8,128)(2,1)}, bf16[20,64,256]{2,1,0:T(8,128)(2,1)S(1)}, u32[]{:S(2)}, u32[]{:S(2)}) collective-permute-start(bf16[20,64,256]{2,1,0:T(8,128)(2,1)} %get-tuple-element.25), channel_id=1, source_target_pairs={{0,16},{8,24},{16,0},{24,8},{32,48},{40,56},{48,32},{56,40},{64,80... | collective-permute-start | bytes 1966088 | tf_op jit(solution)/shard_map/ppermute | solution.py:386
  40.7 10.9 %collective-permute-done.3.refs_4_ = bf16[12,64,256]{2,1,0:T(8,128)(2,1)S(1)} collective-permute-done((bf16[12,64,256]{2,1,0:T(8,128)(2,1)S(1)}, bf16[12,64,256]{2,1,0:T(8,128)(2,1)S(1)}, u32[]{:S(2)}, u32[]{:S(2)}) %collective-permute-start.3) | collective-permute-done | bytes 393248 | tf_op jit(solution)/shard_map/ppermute | solution.py:386
  51.6 1.2 %collective-permute-done.5.refs_6_ = bf16[12,64,256]{2,1,0:T(8,128)(2,1)S(1)} collective-permute-done((bf16[12,64,256]{2,1,0:T(8,128)(2,1)S(1)}, bf16[12,64,256]{2,1,0:T(8,128)(2,1)S(1)}, u32[]{:S(2)}, u32[]{:S(2)}) %collective-permute-start.5) | collective-permute-done | bytes 393248 | tf_op jit(solution)/shard_map/ppermute | solution.py:386
  52.8 2.5 %all-to-all-done.1.refs_3_ = bf16[8,64,1024]{2,1,0:T(8,128)(2,1)} async-done(((bf16[8,64,1024]{2,1,0:T(8,128)(2,1)}), bf16[8,64,1024]{2,1,0:T(8,128)(2,1)}, u32[]{:S(2)}, u32[]{:S(2)}) %all-to-all-start.1) | async-done | bytes 1048608 | tf_op jit(solution)/shard_map/all_to_all | solution.py:433
  55.4 5.0 %attend_chunk.3 = (bf16[2,144,512]{2,1,0:T(8,128)(2,1)S(1)}, bf16[144,512]{1,0:T(8,128)(2,1)S(1)}, bf16[144,512]{1,0:T(8,128)(2,1)S(1)}) custom-call(s32[1]{0:T(128)} %bitcast.me_ref.refs_0_, s32[32,1,128]{2,1,0:T(1,128)S(1)} %all_to_all.10.table_ref.refs_1_, bf16[128,64,256]{2,1,0:T(8,128)(2,1)} %bitcast.26, bf16[8,64,1024]{2,1,0:T(8,128)(2,1)} %all-to-all-done.1.refs_3_, ...), custom_call_target="tpu_custom_call" | custom-call | flops 805306368 | bytes 1572864 | tf_op jit(solution)/shard_map/attend_chunk/pallas_call | solution.py:338
  60.6 4.0 %collective-permute-start.7 = (bf16[144,512]{1,0:T(8,128)(2,1)S(1)}, bf16[144,512]{1,0:T(8,128)(2,1)S(1)}, u32[]{:S(2)}, u32[]{:S(2)}) collective-permute-start(bf16[144,512]{1,0:T(8,128)(2,1)S(1)} %get-tuple-element.31), channel_id=1, source_target_pairs={{0,192},{8,200},{16,208},{24,216},{32,224},{40,232},{48,240},{56,2... | collective-permute-start | bytes 442376 | tf_op jit(solution)/shard_map/ppermute | solution.py:391
  64.6 12.8 %collective-permute-done.refs_4_ = bf16[20,64,256]{2,1,0:T(8,128)(2,1)S(1)} collective-permute-done((bf16[20,64,256]{2,1,0:T(8,128)(2,1)}, bf16[20,64,256]{2,1,0:T(8,128)(2,1)S(1)}, u32[]{:S(2)}, u32[]{:S(2)}) %collective-permute-start) | collective-permute-done | bytes 655392 | tf_op jit(solution)/shard_map/ppermute | solution.py:386
  78.1 6.0 %attend_chunk.4 = (bf16[144,512]{1,0:T(8,128)(2,1)S(1)}, bf16[144,512]{1,0:T(8,128)(2,1)S(1)}, bf16[144,512]{1,0:T(8,128)(2,1)}, bf16[144,512]{1,0:T(8,128)(2,1)S(1)}) custom-call(s32[1]{0:T(128)} %bitcast.me_ref.refs_0_, s32[32,1,128]{2,1,0:T(1,128)S(1)} %all_to_all.10.table_ref.refs_1_, bf16[128,64,256]{2,1,0:T(8,128)(2,1)} %bitcast.27, ...), custom_call_target="tpu_custom_call" | custom-call | flops 1073741824 | bytes 2097152 | tf_op jit(solution)/shard_map/attend_chunk/pallas_call | solution.py:338
  84.1 2.9 %collective-permute-start.10 = (bf16[144,512]{1,0:T(8,128)(2,1)}, bf16[144,512]{1,0:T(8,128)(2,1)S(1)}, u32[]{:S(2)}, u32[]{:S(2)}) collective-permute-start(bf16[144,512]{1,0:T(8,128)(2,1)} %get-tuple-element.35), channel_id=1, source_target_pairs={{0,224},{8,232},{16,240},{24,248},{32,0},{40,8},{48,16},{56,24},{6... | collective-permute-start | bytes 442376 | tf_op jit(solution)/shard_map/ppermute | solution.py:391
  87.0 1.6 %collective-permute-start.8 = (bf16[144,512]{1,0:T(8,128)(2,1)S(1)}, bf16[144,512]{1,0:T(8,128)(2,1)S(1)}, u32[]{:S(2)}, u32[]{:S(2)}) collective-permute-start(bf16[144,512]{1,0:T(8,128)(2,1)S(1)} %get-tuple-element.32.refs_8_), channel_id=1, source_target_pairs={{0,64},{8,72},{16,80},{24,88},{32,96},{40,104},{48,112},{56,120},{... | collective-permute-start | bytes 442376 | tf_op jit(solution)/shard_map/ppermute | solution.py:391
  88.6 2.6 %collective-permute-start.9 = (bf16[144,512]{1,0:T(8,128)(2,1)S(1)}, bf16[144,512]{1,0:T(8,128)(2,1)S(1)}, u32[]{:S(2)}, u32[]{:S(2)}) collective-permute-start(bf16[144,512]{1,0:T(8,128)(2,1)S(1)} %get-tuple-element.34), channel_id=1, source_target_pairs={{0,192},{8,200},{16,208},{24,216},{32,224},{40,232},{48,240},{56,2... | collective-permute-start | bytes 442376 | tf_op jit(solution)/shard_map/ppermute | solution.py:391
  91.1 5.4 %attend_chunk.5 = (bf16[144,512]{1,0:T(8,128)(2,1)S(1)}, bf16[1024,4096]{1,0:T(8,128)(2,1)S(1)}) custom-call(s32[1]{0:T(128)} %bitcast.me_ref.refs_0_, s32[32,1,128]{2,1,0:T(1,128)S(1)} %all_to_all.10.table_ref.refs_1_, bf16[128,64,256]{2,1,0:T(8,128)(2,1)} %bitcast.28, bf16[8,64,1024]{2,1,0:T(8,128)(2,1)} %all-to-all-done.1.refs_3_, ...), custom_call_target="tpu_custom_call" | custom-call | flops 268435456 | bytes 524288 | tf_op jit(solution)/shard_map/attend_chunk/pallas_call | solution.py:338
  97.5 1.8 %merge_project.1 = bf16[64,4096]{1,0:T(8,128)(2,1)S(1)} custom-call(bf16[1024,4096]{1,0:T(8,128)(2,1)S(1)} %get-tuple-element.33.wide_ref, bf16[144,512]{1,0:T(8,128)(2,1)S(1)} %collective-permute-done.8.rest_0_, bf16[144,512]{1,0:T(8,128)(2,1)S(1)} %collective-permute-done.9.rest_1_, bf16[144,512]{1,0:T(8,128)(2,1)S(1)} %collective-permute-done.10.rest_2_, ...), custom_call_target="tpu_custom_call" | custom-call | flops 536870912 | bytes 8388608 | tf_op jit(solution)/shard_map/merge_project/pallas_call | solution.py:373
  99.5 1.5 %collective-permute-done.12 = bf16[4,8,4096]{2,1,0:T(8,128)(2,1)S(1)} collective-permute-done((bf16[4,8,4096]{2,1,0:T(8,128)(2,1)S(1)}, bf16[4,8,4096]{2,1,0:T(8,128)(2,1)S(1)}, u32[]{:S(2)}, u32[]{:S(2)}) %collective-permute-start.12) | collective-permute-done | bytes 262176 | tf_op jit(solution)/shard_map/ppermute | solution.py:402
  101.0 1.3 %collective-permute-start.13 = (bf16[8,4096]{1,0:T(8,128)(2,1)S(1)}, bf16[8,4096]{1,0:T(8,128)(2,1)S(1)}, u32[]{:S(2)}, u32[]{:S(2)}) collective-permute-start(bf16[8,4096]{1,0:T(8,128)(2,1)S(1)} %get-tuple-element.39), channel_id=1, source_target_pairs={{0,4},{1,5},{2,6},{3,7},{4,0},{5,1},{6,2},{7,3},{8,12},{9,13},{10,... | collective-permute-start | bytes 196616 | tf_op jit(solution)/shard_map/ppermute | solution.py:398
  102.4 2.2 %collective-permute-start.14 = (bf16[8,4096]{1,0:T(8,128)(2,1)S(1)}, bf16[8,4096]{1,0:T(8,128)(2,1)S(1)}, u32[]{:S(2)}, u32[]{:S(2)}) collective-permute-start(bf16[8,4096]{1,0:T(8,128)(2,1)S(1)} %get-tuple-element.41), channel_id=1, source_target_pairs={{0,2},{1,3},{2,4},{3,5},{4,6},{5,7},{6,0},{7,1},{8,10},{9,11},{10,... | collective-permute-start | bytes 196616 | tf_op jit(solution)/shard_map/ppermute | solution.py:398
  104.5 2.5 %collective-permute-done.13 = bf16[8,4096]{1,0:T(8,128)(2,1)S(1)} collective-permute-done((bf16[8,4096]{1,0:T(8,128)(2,1)S(1)}, bf16[8,4096]{1,0:T(8,128)(2,1)S(1)}, u32[]{:S(2)}, u32[]{:S(2)}) %collective-permute-start.13) | collective-permute-done | bytes 65568 | tf_op jit(solution)/shard_map/ppermute | solution.py:398
  107.0 3.0 %collective-permute-done.15 = bf16[8,4096]{1,0:T(8,128)(2,1)S(1)} collective-permute-done((bf16[8,4096]{1,0:T(8,128)(2,1)S(1)}, bf16[8,4096]{1,0:T(8,128)(2,1)S(1)}, u32[]{:S(2)}, u32[]{:S(2)}) %collective-permute-start.15) | collective-permute-done | bytes 65568 | tf_op jit(solution)/shard_map/ppermute | solution.py:398
  (26 shorter events, 5.5 us)
Async XLA Ops:
  0.0 55.4 %copy-start = (bf16[64,1024]{1,0:T(8,128)(2,1)S(1)}, bf16[64,1024]{1,0:T(8,128)(2,1)}, u32[]{:S(2)}) copy-start(bf16[64,1024]{1,0:T(8,128)(2,1)} %refs_7_.2) | copy-start | bytes 393220
  0.0 55.4 %copy-start.1 = (bf16[64,1,256]{2,0,1:T(8,128)(2,1)S(1)}, bf16[64,1,256]{2,0,1:T(8,128)(2,1)}, u32[]{:S(2)}) copy-start(bf16[64,1,256]{2,0,1:T(8,128)(2,1)} %param.8) | copy-start | bytes 98308
  23.5 31.8 %all-to-all-start.1 = ((bf16[8,64,1024]{2,1,0:T(8,128)(2,1)}), bf16[8,64,1024]{2,1,0:T(8,128)(2,1)}, u32[]{:S(2)}, u32[]{:S(2)}) async-start(bf16[8,64,1024]{2,1,0:T(8,128)(2,1)} %get-tuple-element.23), calls=%async_computation.1 | async-start | bytes 2097152 | tf_op jit(solution)/shard_map/all_to_all | solution.py:433
  30.2 21.4 %collective-permute-start.3 = (bf16[12,64,256]{2,1,0:T(8,128)(2,1)S(1)}, bf16[12,64,256]{2,1,0:T(8,128)(2,1)S(1)}, u32[]{:S(2)}, u32[]{:S(2)}) collective-permute-start(bf16[12,64,256]{2,1,0:T(8,128)(2,1)S(1)} %get-tuple-element.27), channel_id=1, source_target_pairs={{0,8},{8,16},{16,24},{24,0},{32,40},{40,48},{48,56},{56,32},{64,72... | collective-permute-start | bytes 1179656 | tf_op jit(solution)/shard_map/ppermute | solution.py:386
  30.9 20.7 %collective-permute-start.4 = (bf16[12,64,256]{2,1,0:T(8,128)(2,1)S(1)}, bf16[12,64,256]{2,1,0:T(8,128)(2,1)S(1)}, u32[]{:S(2)}, u32[]{:S(2)}) collective-permute-start(bf16[12,64,256]{2,1,0:T(8,128)(2,1)S(1)} %get-tuple-element.28), channel_id=1, source_target_pairs={{0,16},{8,24},{16,0},{24,8},{32,48},{40,56},{48,32},{56,40},{64,80... | collective-permute-start | bytes 1179656 | tf_op jit(solution)/shard_map/ppermute | solution.py:386
  32.8 20.0 %collective-permute-start.5 = (bf16[12,64,256]{2,1,0:T(8,128)(2,1)S(1)}, bf16[12,64,256]{2,1,0:T(8,128)(2,1)S(1)}, u32[]{:S(2)}, u32[]{:S(2)}) collective-permute-start(bf16[12,64,256]{2,1,0:T(8,128)(2,1)S(1)} %get-tuple-element.29), channel_id=1, source_target_pairs={{0,24},{8,0},{16,8},{24,16},{32,56},{40,32},{48,40},{56,48},{64,88... | collective-permute-start | bytes 1179656 | tf_op jit(solution)/shard_map/ppermute | solution.py:386
  38.0 39.5 %collective-permute-start = (bf16[20,64,256]{2,1,0:T(8,128)(2,1)}, bf16[20,64,256]{2,1,0:T(8,128)(2,1)S(1)}, u32[]{:S(2)}, u32[]{:S(2)}) collective-permute-start(bf16[20,64,256]{2,1,0:T(8,128)(2,1)} %get-tuple-element.24), channel_id=1, source_target_pairs={{0,8},{8,16},{16,24},{24,0},{32,40},{40,48},{48,56},{56,32},{64,72... | collective-permute-start | bytes 1966088 | tf_op jit(solution)/shard_map/ppermute | solution.py:386
  39.0 38.4 %collective-permute-start.1 = (bf16[20,64,256]{2,1,0:T(8,128)(2,1)}, bf16[20,64,256]{2,1,0:T(8,128)(2,1)S(1)}, u32[]{:S(2)}, u32[]{:S(2)}) collective-permute-start(bf16[20,64,256]{2,1,0:T(8,128)(2,1)} %get-tuple-element.25), channel_id=1, source_target_pairs={{0,16},{8,24},{16,0},{24,8},{32,48},{40,56},{48,32},{56,40},{64,80... | collective-permute-start | bytes 1966088 | tf_op jit(solution)/shard_map/ppermute | solution.py:386
  51.6 26.5 %collective-permute-start.2 = (bf16[20,64,256]{2,1,0:T(8,128)(2,1)}, bf16[20,64,256]{2,1,0:T(8,128)(2,1)S(1)}, u32[]{:S(2)}, u32[]{:S(2)}) collective-permute-start(bf16[20,64,256]{2,1,0:T(8,128)(2,1)} %get-tuple-element.26), channel_id=1, source_target_pairs={{0,24},{8,0},{16,8},{24,16},{32,56},{40,32},{48,40},{56,48},{64,88... | collective-permute-start | bytes 1966088 | tf_op jit(solution)/shard_map/ppermute | solution.py:386
  60.4 17.7 %collective-permute-start.6 = (bf16[2,144,512]{2,1,0:T(8,128)(2,1)S(1)}, bf16[2,144,512]{2,1,0:T(8,128)(2,1)S(1)}, u32[]{:S(2)}, u32[]{:S(2)}) collective-permute-start(bf16[2,144,512]{2,1,0:T(8,128)(2,1)S(1)} %get-tuple-element.30), channel_id=1, source_target_pairs={{0,64},{8,72},{16,80},{24,88},{32,96},{40,104},{48,112},{56,120},{... | collective-permute-start | bytes 884744 | tf_op jit(solution)/shard_map/ppermute | solution.py:391
  60.6 17.5 %collective-permute-start.7 = (bf16[144,512]{1,0:T(8,128)(2,1)S(1)}, bf16[144,512]{1,0:T(8,128)(2,1)S(1)}, u32[]{:S(2)}, u32[]{:S(2)}) collective-permute-start(bf16[144,512]{1,0:T(8,128)(2,1)S(1)} %get-tuple-element.31), channel_id=1, source_target_pairs={{0,192},{8,200},{16,208},{24,216},{32,224},{40,232},{48,240},{56,2... | collective-permute-start | bytes 442376 | tf_op jit(solution)/shard_map/ppermute | solution.py:391
  84.1 12.5 %collective-permute-start.10 = (bf16[144,512]{1,0:T(8,128)(2,1)}, bf16[144,512]{1,0:T(8,128)(2,1)S(1)}, u32[]{:S(2)}, u32[]{:S(2)}) collective-permute-start(bf16[144,512]{1,0:T(8,128)(2,1)} %get-tuple-element.35), channel_id=1, source_target_pairs={{0,224},{8,232},{16,240},{24,248},{32,0},{40,8},{48,16},{56,24},{6... | collective-permute-start | bytes 442376 | tf_op jit(solution)/shard_map/ppermute | solution.py:391
  87.0 9.6 %collective-permute-start.11 = (bf16[144,512]{1,0:T(8,128)(2,1)S(1)}, bf16[144,512]{1,0:T(8,128)(2,1)S(1)}, u32[]{:S(2)}, u32[]{:S(2)}) collective-permute-start(bf16[144,512]{1,0:T(8,128)(2,1)S(1)} %get-tuple-element.36), channel_id=1, source_target_pairs={{0,32},{8,40},{16,48},{24,56},{32,64},{40,72},{48,80},{56,88},{64,... | collective-permute-start | bytes 442376 | tf_op jit(solution)/shard_map/ppermute | solution.py:391
  87.0 10.5 %collective-permute-start.8 = (bf16[144,512]{1,0:T(8,128)(2,1)S(1)}, bf16[144,512]{1,0:T(8,128)(2,1)S(1)}, u32[]{:S(2)}, u32[]{:S(2)}) collective-permute-start(bf16[144,512]{1,0:T(8,128)(2,1)S(1)} %get-tuple-element.32.refs_8_), channel_id=1, source_target_pairs={{0,64},{8,72},{16,80},{24,88},{32,96},{40,104},{48,112},{56,120},{... | collective-permute-start | bytes 442376 | tf_op jit(solution)/shard_map/ppermute | solution.py:391
  88.6 8.9 %collective-permute-start.9 = (bf16[144,512]{1,0:T(8,128)(2,1)S(1)}, bf16[144,512]{1,0:T(8,128)(2,1)S(1)}, u32[]{:S(2)}, u32[]{:S(2)}) collective-permute-start(bf16[144,512]{1,0:T(8,128)(2,1)S(1)} %get-tuple-element.34), channel_id=1, source_target_pairs={{0,192},{8,200},{16,208},{24,216},{32,224},{40,232},{48,240},{56,2... | collective-permute-start | bytes 442376 | tf_op jit(solution)/shard_map/ppermute | solution.py:391
  99.3 1.6 %collective-permute-start.12 = (bf16[4,8,4096]{2,1,0:T(8,128)(2,1)S(1)}, bf16[4,8,4096]{2,1,0:T(8,128)(2,1)S(1)}, u32[]{:S(2)}, u32[]{:S(2)}) collective-permute-start(bf16[4,8,4096]{2,1,0:T(8,128)(2,1)S(1)} %dynamic-slice_bitcast_fusion), channel_id=1, source_target_pairs={{0,1},{1,0},{2,3},{3,2},{4,5},{5,4},{6,7},{7,6},{8,9},{9,8},{10,11... | collective-permute-start | bytes 786440 | tf_op jit(solution)/shard_map/ppermute | solution.py:402
  101.0 6.0 %collective-permute-start.13 = (bf16[8,4096]{1,0:T(8,128)(2,1)S(1)}, bf16[8,4096]{1,0:T(8,128)(2,1)S(1)}, u32[]{:S(2)}, u32[]{:S(2)}) collective-permute-start(bf16[8,4096]{1,0:T(8,128)(2,1)S(1)} %get-tuple-element.39), channel_id=1, source_target_pairs={{0,4},{1,5},{2,6},{3,7},{4,0},{5,1},{6,2},{7,3},{8,12},{9,13},{10,... | collective-permute-start | bytes 196616 | tf_op jit(solution)/shard_map/ppermute | solution.py:398
  102.4 4.7 %collective-permute-start.14 = (bf16[8,4096]{1,0:T(8,128)(2,1)S(1)}, bf16[8,4096]{1,0:T(8,128)(2,1)S(1)}, u32[]{:S(2)}, u32[]{:S(2)}) collective-permute-start(bf16[8,4096]{1,0:T(8,128)(2,1)S(1)} %get-tuple-element.41), channel_id=1, source_target_pairs={{0,2},{1,3},{2,4},{3,5},{4,6},{5,7},{6,0},{7,1},{8,10},{9,11},{10,... | collective-permute-start | bytes 196616 | tf_op jit(solution)/shard_map/ppermute | solution.py:398
  104.5 5.5 %collective-permute-start.15 = (bf16[8,4096]{1,0:T(8,128)(2,1)S(1)}, bf16[8,4096]{1,0:T(8,128)(2,1)S(1)}, u32[]{:S(2)}, u32[]{:S(2)}) collective-permute-start(bf16[8,4096]{1,0:T(8,128)(2,1)S(1)} %get-tuple-element.40), channel_id=1, source_target_pairs={{0,6},{1,7},{2,0},{3,1},{4,2},{5,3},{6,4},{7,5},{8,14},{9,15},{10,... | collective-permute-start | bytes 196616 | tf_op jit(solution)/shard_map/ppermute | solution.py:398

commit v8 on v7

--- a/solution.py
+++ b/solution.py
@@ -240,13 +240,13 @@
     return stats[0:1], stats[1:2] + stats[2:3], ref[:HD, :].astype(jnp.float32)
 
 
-def cached_scores(shift, n, me_ref, table_ref, rows, blocks):
+def cached_scores(shift, me_ref, table_ref, rows, blocks):
     zo, xr = coordinates(me_ref)
     home = rem(zo + shift, NZ) * NX + xr
     scores, lives, values = [], [], []
     for k in (1, 2, 3, 0):
         owner = zo * NX + rem(xr - k, NX)
-        both = blocks[k][n * CAP : (n + 1) * CAP].reshape(CAP * BLK, 2 * HD)
+        both = blocks[k].reshape(CAP * BLK, 2 * HD)
         scores.append(
             lax.dot_general(both[:, :HD], rows, CONTRACT_LAST, preferred_element_type=jnp.float32)
         )
@@ -273,7 +273,7 @@
     packet_refs = take(2 if has["relay"] else len(shifts))
     own_packet = take(1)[0] if has["suffix"] else None
     wide_ref = take(1)[0] if has["weight"] else None
-    here, query_here, block_sems, query_sems, wide_sems = take(5)
+    here, query_here, block_sem, query_sems, wide_sems = take(5)
     zo, _ = coordinates(me_ref)
     wide = []
     if has["weight"]:
@@ -284,31 +284,26 @@
                 pltpu.make_async_copy(weight_ref.at[part, :], wide_ref.at[part, :], wide_sems.at[n])
             )
             wide[-1].start()
-    first = chunk.index(shifts[0]) * CAP
+    first = chunk.index(shifts[0])
     fetches = [
         pltpu.make_async_copy(
-            arrived[k - 1].at[pl.ds(first, len(shifts) * CAP)], here.at[k], block_sems.at[k]
+            z_query_ref.at[rem(zo + shift, NZ)], query_here.at[n], query_sems.at[n]
         )
-        for k in range(1, NX)
+        for n, shift in enumerate(shifts)
     ]
-    for n, shift in enumerate(shifts):
-        fetches.append(
-            pltpu.make_async_copy(
-                z_query_ref.at[rem(zo + shift, NZ)], query_here.at[n], query_sems.at[n]
-            )
-        )
     for fetch in fetches:
         fetch.start()
-    start_picks(shifts, 0, me_ref, table_ref, cache_ref, here.at[0], block_sems.at[0])
+    start_picks(shifts, 0, me_ref, table_ref, cache_ref, here, block_sem)
     if has["suffix"]:
         part = suffix_part(head_rows(own_refs[0][...]), own_refs[1][...])
         write_packet(own_packet, *part)
     for fetch in fetches:
         fetch.wait()
-    wait_picks(shifts, cache_ref, here.at[0], block_sems.at[0])
+    wait_picks(shifts, cache_ref, here, block_sem)
     def scores_of(n):
-        blocks = [here.at[k] for k in range(NX)]
-        return cached_scores(shifts[n], n, me_ref, table_ref, head_rows(query_here[n]), blocks)
+        there = slice((first + n) * CAP, (first + n + 1) * CAP)
+        blocks = [here[n * CAP : (n + 1) * CAP]] + [ref[there] for ref in arrived]
+        return cached_scores(shifts[n], me_ref, table_ref, head_rows(query_here[n]), blocks)
 
     following = scores_of(0)
     for n, shift in enumerate(shifts):
@@ -339,14 +334,14 @@
         functools.partial(attend_kernel, chunk, shifts, has),
         out_shape=packets + wide,
         in_specs=[IN_SMEM] * 2
-        + [IN_HBM] * (NX + 1)
-        + [IN_VMEM] * (len(own) + len(relayed))
+        + [IN_HBM] * 2
+        + [IN_VMEM] * (NX - 1 + len(own) + len(relayed))
         + [IN_HBM] * len(weight),
         out_specs=[IN_VMEM] * len(packets + wide),
         scratch_shapes=[
-            pltpu.VMEM((NX, len(shifts) * CAP, BLK, 2 * HD), cache.dtype),
+            pltpu.VMEM((len(shifts) * CAP, BLK, 2 * HD), cache.dtype),
             pltpu.VMEM((len(shifts), SUF, GROUP * HD), jnp.bfloat16),
-            pltpu.SemaphoreType.DMA((NX,)),
+            pltpu.SemaphoreType.DMA,
             pltpu.SemaphoreType.DMA((len(shifts),)),
             pltpu.SemaphoreType.DMA((WIDE_PARTS,)),
         ],

time: 113 us -> 113 us (level)
  transfers between devices with their start and end apart: 17 -> 17, of which waited for: 9 -> 10; matrix products, arithmetic and copies ran while one was open for 0% -> 0% of each run, Pallas kernels for 15% -> 15%
where the time goes in v8:
time: 113 us; the launch traced here: 111 us
  waiting for transfers between devices  36.7 us (32%)
  Pallas kernels  25.8 us (23%)
  starting transfers between devices  25.8 us (23%)
  blocking collectives  20.8 us (18%)
    ppermute x6, waiting for transfers between devices, x_permute(): return lax.ppermute(a, 'store', pairs)  26.3 us
    all_to_all x1, blocking collectives, local(): lax.all_to_all(wanted, 'store', split_axis=0, concat_axis=0, tiled=True)  20.8 us
    pallas_call x3, Pallas kernels, attend(): pl.pallas_call(functools.partial(attend_kernel, chunk, shifts, has), out_...  15.5 us
    ppermute x6, starting transfers between devices, z_permute(): return lax.ppermute(a, 'store', pairs)  11.4 us
    ppermute x6, starting transfers between devices, x_permute(): return lax.ppermute(a, 'store', pairs)  6.57 us
    ppermute x3, waiting for transfers between devices, y_permute(): return lax.ppermute(a, 'head', pairs)  5.47 us
    all_to_all x1, starting transfers between devices, local(): lax.all_to_all(copies, 'store', split_axis=0, concat_axis=0, tiled=True,...  4.25 us
    pallas_call x1, Pallas kernels, pick_near(): pl.pallas_call(functools.partial(pick_near_kernel, shifts), out_shape=[ja...  3.98 us
  transfers between devices with their start and end apart: 17, of which 10 were waited for; matrix products, arithmetic and copies ran while one was open for 0% of the time, Pallas kernels for 15%

profile of v8, /device:TPU:24, one launch (start us, length us, event | category | flops | bytes accessed | tf_op | source)
XLA Modules:
  0.0 110.8 jit_solution(17613902435479530308)
XLA Ops:
  0.7 2.0 %wanted_slots.1 = (s32[32,1,128]{2,1,0:T(1,128)S(1)}, bf16[8,64,1024]{2,1,0:T(8,128)(2,1)}) custom-call(s32[1]{0:T(128)S(6)} %copy.10.length_ref, s32[1,128]{1,0:T(1,128)} %owner_hbm.1, s32[1,128]{1,0:T(1,128)} %slot_hbm.1, bf16[64,1024]{1,0:T(8,128)(2,1)} %refs_7_.2), custom_call_target="tpu_custom_call" | custom-call | tf_op jit(solution)/shard_map/wanted_slots/pallas_call | solution.py:101
  2.7 20.8 %all_to_all.10.table_ref.refs_1_ = s32[32,1,128]{2,1,0:T(1,128)S(1)} all-to-all(s32[32,1,128]{2,1,0:T(1,128)S(1)} %get-tuple-element.22), channel_id=1, replica_groups=mesh['store'=32,'head'=8] {'store'}, dimensions={0} | all-to-all | bytes 32768 | tf_op jit(solution)/shard_map/all_to_all | solution.py:416
  23.5 4.2 %all-to-all-start.1 = ((bf16[8,64,1024]{2,1,0:T(8,128)(2,1)}), bf16[8,64,1024]{2,1,0:T(8,128)(2,1)}, u32[]{:S(2)}, u32[]{:S(2)}) async-start(bf16[8,64,1024]{2,1,0:T(8,128)(2,1)} %get-tuple-element.23), calls=%async_computation.1 | async-start | bytes 2097152 | tf_op jit(solution)/shard_map/all_to_all | solution.py:428
  27.8 2.5 %pick_far.1 = (bf16[12,64,256]{2,1,0:T(8,128)(2,1)S(1)}, bf16[12,64,256]{2,1,0:T(8,128)(2,1)S(1)}, bf16[12,64,256]{2,1,0:T(8,128)(2,1)S(1)}) custom-call(s32[1]{0:T(128)} %bitcast.me_ref.refs_0_, s32[32,1,128]{2,1,0:T(1,128)S(1)} %all_to_all.10.table_ref.refs_1_, bf16[128,64,256]{2,1,0:T(8,128)(2,1)} %bitcast.24), custom_call_target="tpu_custom_call" | custom-call | tf_op jit(solution)/shard_map/pick_far/pallas_call | solution.py:150
  30.9 2.0 %collective-permute-start.4 = (bf16[12,64,256]{2,1,0:T(8,128)(2,1)S(1)}, bf16[12,64,256]{2,1,0:T(8,128)(2,1)S(1)}, u32[]{:S(2)}, u32[]{:S(2)}) collective-permute-start(bf16[12,64,256]{2,1,0:T(8,128)(2,1)S(1)} %get-tuple-element.28), channel_id=1, source_target_pairs={{0,16},{8,24},{16,0},{24,8},{32,48},{40,56},{48,32},{56,40},{64,80... | collective-permute-start | bytes 1179656 | tf_op jit(solution)/shard_map/ppermute | solution.py:381
  32.9 1.3 %collective-permute-start.5 = (bf16[12,64,256]{2,1,0:T(8,128)(2,1)S(1)}, bf16[12,64,256]{2,1,0:T(8,128)(2,1)S(1)}, u32[]{:S(2)}, u32[]{:S(2)}) collective-permute-start(bf16[12,64,256]{2,1,0:T(8,128)(2,1)S(1)} %get-tuple-element.29), channel_id=1, source_target_pairs={{0,24},{8,0},{16,8},{24,16},{32,56},{40,32},{48,40},{56,48},{64,88... | collective-permute-start | bytes 1179656 | tf_op jit(solution)/shard_map/ppermute | solution.py:381
  34.2 4.0 %pick_near.1 = (bf16[20,64,256]{2,1,0:T(8,128)(2,1)}, bf16[20,64,256]{2,1,0:T(8,128)(2,1)}, bf16[20,64,256]{2,1,0:T(8,128)(2,1)}) custom-call(s32[1]{0:T(128)} %bitcast.me_ref.refs_0_, s32[32,1,128]{2,1,0:T(1,128)S(1)} %all_to_all.10.table_ref.refs_1_, bf16[128,64,256]{2,1,0:T(8,128)(2,1)} %bitcast.25), custom_call_target="tpu_custom_call" | custom-call | tf_op jit(solution)/shard_map/pick_near/pallas_call | solution.py:176
  39.1 1.8 %collective-permute-start.1 = (bf16[20,64,256]{2,1,0:T(8,128)(2,1)}, bf16[20,64,256]{2,1,0:T(8,128)(2,1)S(1)}, u32[]{:S(2)}, u32[]{:S(2)}) collective-permute-start(bf16[20,64,256]{2,1,0:T(8,128)(2,1)} %get-tuple-element.25), channel_id=1, source_target_pairs={{0,16},{8,24},{16,0},{24,8},{32,48},{40,56},{48,32},{56,40},{64,80... | collective-permute-start | bytes 1966088 | tf_op jit(solution)/shard_map/ppermute | solution.py:381
  40.9 10.8 %collective-permute-done.3.refs_4_ = bf16[12,64,256]{2,1,0:T(8,128)(2,1)S(1)} collective-permute-done((bf16[12,64,256]{2,1,0:T(8,128)(2,1)S(1)}, bf16[12,64,256]{2,1,0:T(8,128)(2,1)S(1)}, u32[]{:S(2)}, u32[]{:S(2)}) %collective-permute-start.3) | collective-permute-done | bytes 393248 | tf_op jit(solution)/shard_map/ppermute | solution.py:381
  53.0 2.4 %all-to-all-done.1.refs_3_ = bf16[8,64,1024]{2,1,0:T(8,128)(2,1)} async-done(((bf16[8,64,1024]{2,1,0:T(8,128)(2,1)}), bf16[8,64,1024]{2,1,0:T(8,128)(2,1)}, u32[]{:S(2)}, u32[]{:S(2)}) %all-to-all-start.1) | async-done | bytes 1048608 | tf_op jit(solution)/shard_map/all_to_all | solution.py:428
  55.4 4.4 %attend_chunk.3 = (bf16[2,144,512]{2,1,0:T(8,128)(2,1)S(1)}, bf16[144,512]{1,0:T(8,128)(2,1)S(1)}, bf16[144,512]{1,0:T(8,128)(2,1)S(1)}) custom-call(s32[1]{0:T(128)} %bitcast.me_ref.refs_0_, s32[32,1,128]{2,1,0:T(1,128)S(1)} %all_to_all.10.table_ref.refs_1_, bf16[128,64,256]{2,1,0:T(8,128)(2,1)} %bitcast.26, bf16[8,64,1024]{2,1,0:T(8,128)(2,1)} %all-to-all-done.1.refs_3_, ...), custom_call_target="tpu_custom_call" | custom-call | flops 805306368 | bytes 1572864 | tf_op jit(solution)/shard_map/attend_chunk/pallas_call | solution.py:333
  60.1 3.9 %collective-permute-start.7 = (bf16[144,512]{1,0:T(8,128)(2,1)S(1)}, bf16[144,512]{1,0:T(8,128)(2,1)S(1)}, u32[]{:S(2)}, u32[]{:S(2)}) collective-permute-start(bf16[144,512]{1,0:T(8,128)(2,1)S(1)} %get-tuple-element.31), channel_id=1, source_target_pairs={{0,192},{8,200},{16,208},{24,216},{32,224},{40,232},{48,240},{56,2... | collective-permute-start | bytes 442376 | tf_op jit(solution)/shard_map/ppermute | solution.py:386
  64.0 13.5 %collective-permute-done.refs_4_ = bf16[20,64,256]{2,1,0:T(8,128)(2,1)S(1)} collective-permute-done((bf16[20,64,256]{2,1,0:T(8,128)(2,1)}, bf16[20,64,256]{2,1,0:T(8,128)(2,1)S(1)}, u32[]{:S(2)}, u32[]{:S(2)}) %collective-permute-start) | collective-permute-done | bytes 655392 | tf_op jit(solution)/shard_map/ppermute | solution.py:381
  78.2 5.8 %attend_chunk.4 = (bf16[144,512]{1,0:T(8,128)(2,1)S(1)}, bf16[144,512]{1,0:T(8,128)(2,1)S(1)}, bf16[144,512]{1,0:T(8,128)(2,1)}, bf16[144,512]{1,0:T(8,128)(2,1)S(1)}) custom-call(s32[1]{0:T(128)} %bitcast.me_ref.refs_0_, s32[32,1,128]{2,1,0:T(1,128)S(1)} %all_to_all.10.table_ref.refs_1_, bf16[128,64,256]{2,1,0:T(8,128)(2,1)} %bitcast.27, ...), custom_call_target="tpu_custom_call" | custom-call | flops 1073741824 | bytes 2097152 | tf_op jit(solution)/shard_map/attend_chunk/pallas_call | solution.py:333
  84.0 3.0 %collective-permute-start.10 = (bf16[144,512]{1,0:T(8,128)(2,1)}, bf16[144,512]{1,0:T(8,128)(2,1)S(1)}, u32[]{:S(2)}, u32[]{:S(2)}) collective-permute-start(bf16[144,512]{1,0:T(8,128)(2,1)} %get-tuple-element.35), channel_id=1, source_target_pairs={{0,224},{8,232},{16,240},{24,248},{32,0},{40,8},{48,16},{56,24},{6... | collective-permute-start | bytes 442376 | tf_op jit(solution)/shard_map/ppermute | solution.py:386
  87.1 1.6 %collective-permute-start.8 = (bf16[144,512]{1,0:T(8,128)(2,1)S(1)}, bf16[144,512]{1,0:T(8,128)(2,1)S(1)}, u32[]{:S(2)}, u32[]{:S(2)}) collective-permute-start(bf16[144,512]{1,0:T(8,128)(2,1)S(1)} %get-tuple-element.32.refs_8_), channel_id=1, source_target_pairs={{0,64},{8,72},{16,80},{24,88},{32,96},{40,104},{48,112},{56,120},{... | collective-permute-start | bytes 442376 | tf_op jit(solution)/shard_map/ppermute | solution.py:386
  88.7 2.5 %collective-permute-start.9 = (bf16[144,512]{1,0:T(8,128)(2,1)S(1)}, bf16[144,512]{1,0:T(8,128)(2,1)S(1)}, u32[]{:S(2)}, u32[]{:S(2)}) collective-permute-start(bf16[144,512]{1,0:T(8,128)(2,1)S(1)} %get-tuple-element.34), channel_id=1, source_target_pairs={{0,192},{8,200},{16,208},{24,216},{32,224},{40,232},{48,240},{56,2... | collective-permute-start | bytes 442376 | tf_op jit(solution)/shard_map/ppermute | solution.py:386
  91.2 5.3 %attend_chunk.5 = (bf16[144,512]{1,0:T(8,128)(2,1)S(1)}, bf16[1024,4096]{1,0:T(8,128)(2,1)S(1)}) custom-call(s32[1]{0:T(128)} %bitcast.me_ref.refs_0_, s32[32,1,128]{2,1,0:T(1,128)S(1)} %all_to_all.10.table_ref.refs_1_, bf16[128,64,256]{2,1,0:T(8,128)(2,1)} %bitcast.28, bf16[8,64,1024]{2,1,0:T(8,128)(2,1)} %all-to-all-done.1.refs_3_, ...), custom_call_target="tpu_custom_call" | custom-call | flops 268435456 | bytes 524288 | tf_op jit(solution)/shard_map/attend_chunk/pallas_call | solution.py:333
  97.6 1.8 %merge_project.1 = bf16[64,4096]{1,0:T(8,128)(2,1)S(1)} custom-call(bf16[1024,4096]{1,0:T(8,128)(2,1)S(1)} %get-tuple-element.33.wide_ref, bf16[144,512]{1,0:T(8,128)(2,1)S(1)} %collective-permute-done.8.rest_0_, bf16[144,512]{1,0:T(8,128)(2,1)S(1)} %collective-permute-done.9.rest_1_, bf16[144,512]{1,0:T(8,128)(2,1)S(1)} %collective-permute-done.10.rest_2_, ...), custom_call_target="tpu_custom_call" | custom-call | flops 536870912 | bytes 8388608 | tf_op jit(solution)/shard_map/merge_project/pallas_call | solution.py:368
  99.6 1.5 %collective-permute-done.12 = bf16[4,8,4096]{2,1,0:T(8,128)(2,1)S(1)} collective-permute-done((bf16[4,8,4096]{2,1,0:T(8,128)(2,1)S(1)}, bf16[4,8,4096]{2,1,0:T(8,128)(2,1)S(1)}, u32[]{:S(2)}, u32[]{:S(2)}) %collective-permute-start.12) | collective-permute-done | bytes 262176 | tf_op jit(solution)/shard_map/ppermute | solution.py:397
  101.1 1.3 %collective-permute-start.13 = (bf16[8,4096]{1,0:T(8,128)(2,1)S(1)}, bf16[8,4096]{1,0:T(8,128)(2,1)S(1)}, u32[]{:S(2)}, u32[]{:S(2)}) collective-permute-start(bf16[8,4096]{1,0:T(8,128)(2,1)S(1)} %get-tuple-element.39), channel_id=1, source_target_pairs={{0,4},{1,5},{2,6},{3,7},{4,0},{5,1},{6,2},{7,3},{8,12},{9,13},{10,... | collective-permute-start | bytes 196616 | tf_op jit(solution)/shard_map/ppermute | solution.py:393
  102.5 2.2 %collective-permute-start.14 = (bf16[8,4096]{1,0:T(8,128)(2,1)S(1)}, bf16[8,4096]{1,0:T(8,128)(2,1)S(1)}, u32[]{:S(2)}, u32[]{:S(2)}) collective-permute-start(bf16[8,4096]{1,0:T(8,128)(2,1)S(1)} %get-tuple-element.41), channel_id=1, source_target_pairs={{0,2},{1,3},{2,4},{3,5},{4,6},{5,7},{6,0},{7,1},{8,10},{9,11},{10,... | collective-permute-start | bytes 196616 | tf_op jit(solution)/shard_map/ppermute | solution.py:393
  104.6 2.5 %collective-permute-done.13 = bf16[8,4096]{1,0:T(8,128)(2,1)S(1)} collective-permute-done((bf16[8,4096]{1,0:T(8,128)(2,1)S(1)}, bf16[8,4096]{1,0:T(8,128)(2,1)S(1)}, u32[]{:S(2)}, u32[]{:S(2)}) %collective-permute-start.13) | collective-permute-done | bytes 65568 | tf_op jit(solution)/shard_map/ppermute | solution.py:393
  107.1 3.0 %collective-permute-done.15 = bf16[8,4096]{1,0:T(8,128)(2,1)S(1)} collective-permute-done((bf16[8,4096]{1,0:T(8,128)(2,1)S(1)}, bf16[8,4096]{1,0:T(8,128)(2,1)S(1)}, u32[]{:S(2)}, u32[]{:S(2)}) %collective-permute-start.15) | collective-permute-done | bytes 65568 | tf_op jit(solution)/shard_map/ppermute | solution.py:393
  (26 shorter events, 5.6 us)
Async XLA Ops:
  0.0 55.4 %copy-start = (bf16[64,1024]{1,0:T(8,128)(2,1)S(1)}, bf16[64,1024]{1,0:T(8,128)(2,1)}, u32[]{:S(2)}) copy-start(bf16[64,1024]{1,0:T(8,128)(2,1)} %refs_7_.2) | copy-start | bytes 393220
  0.0 55.4 %copy-start.1 = (bf16[64,1,256]{2,0,1:T(8,128)(2,1)S(1)}, bf16[64,1,256]{2,0,1:T(8,128)(2,1)}, u32[]{:S(2)}) copy-start(bf16[64,1,256]{2,0,1:T(8,128)(2,1)} %param.8) | copy-start | bytes 98308
  23.5 31.8 %all-to-all-start.1 = ((bf16[8,64,1024]{2,1,0:T(8,128)(2,1)}), bf16[8,64,1024]{2,1,0:T(8,128)(2,1)}, u32[]{:S(2)}, u32[]{:S(2)}) async-start(bf16[8,64,1024]{2,1,0:T(8,128)(2,1)} %get-tuple-element.23), calls=%async_computation.1 | async-start | bytes 2097152 | tf_op jit(solution)/shard_map/all_to_all | solution.py:428
  30.3 21.3 %collective-permute-start.3 = (bf16[12,64,256]{2,1,0:T(8,128)(2,1)S(1)}, bf16[12,64,256]{2,1,0:T(8,128)(2,1)S(1)}, u32[]{:S(2)}, u32[]{:S(2)}) collective-permute-start(bf16[12,64,256]{2,1,0:T(8,128)(2,1)S(1)} %get-tuple-element.27), channel_id=1, source_target_pairs={{0,8},{8,16},{16,24},{24,0},{32,40},{40,48},{48,56},{56,32},{64,72... | collective-permute-start | bytes 1179656 | tf_op jit(solution)/shard_map/ppermute | solution.py:381
  30.9 20.8 %collective-permute-start.4 = (bf16[12,64,256]{2,1,0:T(8,128)(2,1)S(1)}, bf16[12,64,256]{2,1,0:T(8,128)(2,1)S(1)}, u32[]{:S(2)}, u32[]{:S(2)}) collective-permute-start(bf16[12,64,256]{2,1,0:T(8,128)(2,1)S(1)} %get-tuple-element.28), channel_id=1, source_target_pairs={{0,16},{8,24},{16,0},{24,8},{32,48},{40,56},{48,32},{56,40},{64,80... | collective-permute-start | bytes 1179656 | tf_op jit(solution)/shard_map/ppermute | solution.py:381
  32.9 20.0 %collective-permute-start.5 = (bf16[12,64,256]{2,1,0:T(8,128)(2,1)S(1)}, bf16[12,64,256]{2,1,0:T(8,128)(2,1)S(1)}, u32[]{:S(2)}, u32[]{:S(2)}) collective-permute-start(bf16[12,64,256]{2,1,0:T(8,128)(2,1)S(1)} %get-tuple-element.29), channel_id=1, source_target_pairs={{0,24},{8,0},{16,8},{24,16},{32,56},{40,32},{48,40},{56,48},{64,88... | collective-permute-start | bytes 1179656 | tf_op jit(solution)/shard_map/ppermute | solution.py:381
  38.2 39.4 %collective-permute-start = (bf16[20,64,256]{2,1,0:T(8,128)(2,1)}, bf16[20,64,256]{2,1,0:T(8,128)(2,1)S(1)}, u32[]{:S(2)}, u32[]{:S(2)}) collective-permute-start(bf16[20,64,256]{2,1,0:T(8,128)(2,1)} %get-tuple-element.24), channel_id=1, source_target_pairs={{0,8},{8,16},{16,24},{24,0},{32,40},{40,48},{48,56},{56,32},{64,72... | collective-permute-start | bytes 1966088 | tf_op jit(solution)/shard_map/ppermute | solution.py:381
  39.1 38.5 %collective-permute-start.1 = (bf16[20,64,256]{2,1,0:T(8,128)(2,1)}, bf16[20,64,256]{2,1,0:T(8,128)(2,1)S(1)}, u32[]{:S(2)}, u32[]{:S(2)}) collective-permute-start(bf16[20,64,256]{2,1,0:T(8,128)(2,1)} %get-tuple-element.25), channel_id=1, source_target_pairs={{0,16},{8,24},{16,0},{24,8},{32,48},{40,56},{48,32},{56,40},{64,80... | collective-permute-start | bytes 1966088 | tf_op jit(solution)/shard_map/ppermute | solution.py:381
  51.7 26.6 %collective-permute-start.2 = (bf16[20,64,256]{2,1,0:T(8,128)(2,1)}, bf16[20,64,256]{2,1,0:T(8,128)(2,1)S(1)}, u32[]{:S(2)}, u32[]{:S(2)}) collective-permute-start(bf16[20,64,256]{2,1,0:T(8,128)(2,1)} %get-tuple-element.26), channel_id=1, source_target_pairs={{0,24},{8,0},{16,8},{24,16},{32,56},{40,32},{48,40},{56,48},{64,88... | collective-permute-start | bytes 1966088 | tf_op jit(solution)/shard_map/ppermute | solution.py:381
  59.8 18.4 %collective-permute-start.6 = (bf16[2,144,512]{2,1,0:T(8,128)(2,1)S(1)}, bf16[2,144,512]{2,1,0:T(8,128)(2,1)S(1)}, u32[]{:S(2)}, u32[]{:S(2)}) collective-permute-start(bf16[2,144,512]{2,1,0:T(8,128)(2,1)S(1)} %get-tuple-element.30), channel_id=1, source_target_pairs={{0,64},{8,72},{16,80},{24,88},{32,96},{40,104},{48,112},{56,120},{... | collective-permute-start | bytes 884744 | tf_op jit(solution)/shard_map/ppermute | solution.py:386
  60.1 18.1 %collective-permute-start.7 = (bf16[144,512]{1,0:T(8,128)(2,1)S(1)}, bf16[144,512]{1,0:T(8,128)(2,1)S(1)}, u32[]{:S(2)}, u32[]{:S(2)}) collective-permute-start(bf16[144,512]{1,0:T(8,128)(2,1)S(1)} %get-tuple-element.31), channel_id=1, source_target_pairs={{0,192},{8,200},{16,208},{24,216},{32,224},{40,232},{48,240},{56,2... | collective-permute-start | bytes 442376 | tf_op jit(solution)/shard_map/ppermute | solution.py:386
  84.0 12.5 %collective-permute-start.10 = (bf16[144,512]{1,0:T(8,128)(2,1)}, bf16[144,512]{1,0:T(8,128)(2,1)S(1)}, u32[]{:S(2)}, u32[]{:S(2)}) collective-permute-start(bf16[144,512]{1,0:T(8,128)(2,1)} %get-tuple-element.35), channel_id=1, source_target_pairs={{0,224},{8,232},{16,240},{24,248},{32,0},{40,8},{48,16},{56,24},{6... | collective-permute-start | bytes 442376 | tf_op jit(solution)/shard_map/ppermute | solution.py:386
  87.1 9.7 %collective-permute-start.11 = (bf16[144,512]{1,0:T(8,128)(2,1)S(1)}, bf16[144,512]{1,0:T(8,128)(2,1)S(1)}, u32[]{:S(2)}, u32[]{:S(2)}) collective-permute-start(bf16[144,512]{1,0:T(8,128)(2,1)S(1)} %get-tuple-element.36), channel_id=1, source_target_pairs={{0,32},{8,40},{16,48},{24,56},{32,64},{40,72},{48,80},{56,88},{64,... | collective-permute-start | bytes 442376 | tf_op jit(solution)/shard_map/ppermute | solution.py:386
  87.1 10.5 %collective-permute-start.8 = (bf16[144,512]{1,0:T(8,128)(2,1)S(1)}, bf16[144,512]{1,0:T(8,128)(2,1)S(1)}, u32[]{:S(2)}, u32[]{:S(2)}) collective-permute-start(bf16[144,512]{1,0:T(8,128)(2,1)S(1)} %get-tuple-element.32.refs_8_), channel_id=1, source_target_pairs={{0,64},{8,72},{16,80},{24,88},{32,96},{40,104},{48,112},{56,120},{... | collective-permute-start | bytes 442376 | tf_op jit(solution)/shard_map/ppermute | solution.py:386
  88.7 9.0 %collective-permute-start.9 = (bf16[144,512]{1,0:T(8,128)(2,1)S(1)}, bf16[144,512]{1,0:T(8,128)(2,1)S(1)}, u32[]{:S(2)}, u32[]{:S(2)}) collective-permute-start(bf16[144,512]{1,0:T(8,128)(2,1)S(1)} %get-tuple-element.34), channel_id=1, source_target_pairs={{0,192},{8,200},{16,208},{24,216},{32,224},{40,232},{48,240},{56,2... | collective-permute-start | bytes 442376 | tf_op jit(solution)/shard_map/ppermute | solution.py:386
  99.4 1.6 %collective-permute-start.12 = (bf16[4,8,4096]{2,1,0:T(8,128)(2,1)S(1)}, bf16[4,8,4096]{2,1,0:T(8,128)(2,1)S(1)}, u32[]{:S(2)}, u32[]{:S(2)}) collective-permute-start(bf16[4,8,4096]{2,1,0:T(8,128)(2,1)S(1)} %dynamic-slice_bitcast_fusion), channel_id=1, source_target_pairs={{0,1},{1,0},{2,3},{3,2},{4,5},{5,4},{6,7},{7,6},{8,9},{9,8},{10,11... | collective-permute-start | bytes 786440 | tf_op jit(solution)/shard_map/ppermute | solution.py:397
  101.1 6.0 %collective-permute-start.13 = (bf16[8,4096]{1,0:T(8,128)(2,1)S(1)}, bf16[8,4096]{1,0:T(8,128)(2,1)S(1)}, u32[]{:S(2)}, u32[]{:S(2)}) collective-permute-start(bf16[8,4096]{1,0:T(8,128)(2,1)S(1)} %get-tuple-element.39), channel_id=1, source_target_pairs={{0,4},{1,5},{2,6},{3,7},{4,0},{5,1},{6,2},{7,3},{8,12},{9,13},{10,... | collective-permute-start | bytes 196616 | tf_op jit(solution)/shard_map/ppermute | solution.py:393
  102.5 4.7 %collective-permute-start.14 = (bf16[8,4096]{1,0:T(8,128)(2,1)S(1)}, bf16[8,4096]{1,0:T(8,128)(2,1)S(1)}, u32[]{:S(2)}, u32[]{:S(2)}) collective-permute-start(bf16[8,4096]{1,0:T(8,128)(2,1)S(1)} %get-tuple-element.41), channel_id=1, source_target_pairs={{0,2},{1,3},{2,4},{3,5},{4,6},{5,7},{6,0},{7,1},{8,10},{9,11},{10,... | collective-permute-start | bytes 196616 | tf_op jit(solution)/shard_map/ppermute | solution.py:393
  104.6 5.5 %collective-permute-start.15 = (bf16[8,4096]{1,0:T(8,128)(2,1)S(1)}, bf16[8,4096]{1,0:T(8,128)(2,1)S(1)}, u32[]{:S(2)}, u32[]{:S(2)}) collective-permute-start(bf16[8,4096]{1,0:T(8,128)(2,1)S(1)} %get-tuple-element.40), channel_id=1, source_target_pairs={{0,6},{1,7},{2,0},{3,1},{4,2},{5,3},{6,4},{7,5},{8,14},{9,15},{10,... | collective-permute-start | bytes 196616 | tf_op jit(solution)/shard_map/ppermute | solution.py:393

commit v9 on v8

--- a/solution.py
+++ b/solution.py
@@ -354,26 +354,35 @@
     return outs
 
 
-def finish_kernel(wide_ref, *rest):
-    packet_refs, out_ref = rest[:-1], rest[-1]
+def finish_kernel(core_ref, wide_ref, *rest):
+    packet_refs, send_ref, keep_ref = rest[:-2], rest[-2], rest[-1]
     _, row_sum, summed = merge_parts([read_packet(ref) for ref in packet_refs])
     rows = (summed / row_sum).T.astype(jnp.bfloat16)
     attended = jnp.concatenate([rows[i * SUF : (i + 1) * SUF] for i in range(GROUP)], axis=1)
-    out_ref[...] = jnp.dot(
-        attended, wide_ref[...], preferred_element_type=jnp.float32
-    ).astype(jnp.bfloat16)
-
-
-def finish(wide, packets):
+    partial = jnp.dot(attended, wide_ref[...], preferred_element_type=jnp.float32)
+    groups = [partial[n * HEAD_ROWS : (n + 1) * HEAD_ROWS] for n in range(NY * CORES)]
+    halves = [jnp.concatenate(groups[c::CORES], axis=0) for c in range(CORES)]
+    first = core_ref[0] == 0
+    send_ref[...] = jnp.where(first, halves[1], halves[0]).astype(jnp.bfloat16)
+    keep_ref[...] = jnp.where(first, halves[0], halves[1])
+
+
+def finish(core, wide, packets):
+    half = (NY * HEAD_ROWS, wide.shape[1])
     return pl.pallas_call(
         finish_kernel,
-        out_shape=jax.ShapeDtypeStruct((SUF, wide.shape[1]), jnp.bfloat16),
+        out_shape=[
+            jax.ShapeDtypeStruct(half, jnp.bfloat16),
+            jax.ShapeDtypeStruct(half, jnp.float32),
+        ],
+        in_specs=[IN_SMEM] + [IN_VMEM] * (1 + len(packets)),
+        out_specs=[IN_VMEM] * 2,
         compiler_params=pltpu.CompilerParams(vmem_limit_bytes=VMEM_LIMIT),
         cost_estimate=pl.CostEstimate(
             flops=2 * SUF * wide.size, bytes_accessed=2 * wide.size, transcendentals=0
         ),
         name="merge_project",
-    )(wide, *packets)
+    )(core, wide, *packets)
 
 
 def x_permute(a, step):
@@ -397,13 +406,9 @@
     return lax.ppermute(a, "head", [(h, h ^ 1) for h in range(NY * CORES)])
 
 
-def sum_heads(partial):
-    core = lax.rem(lax.axis_index("head"), CORES)
+def sum_heads(send, keep):
     y = lax.div(lax.axis_index("head"), CORES)
-    parts = partial.reshape(NY, CORES, HEAD_ROWS, partial.shape[1])
-    pick_core = lambda which: lax.dynamic_index_in_dim(parts, which, 1, keepdims=False)
-    other = core_swap(pick_core(1 - core))
-    both = pick_core(core).astype(jnp.float32) + other.astype(jnp.float32)
+    both = (keep + core_swap(send).astype(jnp.float32)).reshape(NY, HEAD_ROWS, keep.shape[1])
     pick_y = lambda step: lax.dynamic_index_in_dim(both, rem(y + step, NY), 0, keepdims=False)
     arrived = [y_permute(pick_y(step).astype(jnp.bfloat16), step) for step in (2, 1, 3)]
     return (pick_y(0) + sum(a.astype(jnp.float32) for a in arrived)).astype(jnp.bfloat16)
@@ -437,7 +442,8 @@
     home, wide = attend(
         near, near[-1:], *common, near_blocks, weight=(keep_in_hbm(out_weight), parts[0])
     )
-    return sum_heads(finish(wide, packets + [home]))
+    core = lax.rem(lax.axis_index("head"), CORES).astype(jnp.int32).reshape(1)
+    return sum_heads(*finish(core, wide, packets + [home]))
 
 
 def solution(mesh):

time: 113 us -> 112 us (level)
  transfers between devices with their start and end apart: 17 -> 17, of which waited for: 10 -> 11; matrix products, arithmetic and copies ran while one was open for 0% -> 0% of each run, Pallas kernels for 15% -> 15%
where the time goes in v9:
time: 112 us; the launch traced here: 110 us
  waiting for transfers between devices  37 us (33%)
  starting transfers between devices  25.6 us (23%)
  Pallas kernels  25.3 us (23%)
  blocking collectives  20.8 us (19%)
    ppermute x6, waiting for transfers between devices, x_permute(): return lax.ppermute(a, 'store', pairs)  26.2 us
    all_to_all x1, blocking collectives, local(): lax.all_to_all(wanted, 'store', split_axis=0, concat_axis=0, tiled=True)  20.8 us
    pallas_call x3, Pallas kernels, attend(): pl.pallas_call(functools.partial(attend_kernel, chunk, shifts, has), out_...  15 us
    ppermute x6, starting transfers between devices, z_permute(): return lax.ppermute(a, 'store', pairs)  11.4 us
    ppermute x6, starting transfers between devices, x_permute(): return lax.ppermute(a, 'store', pairs)  6.38 us
    ppermute x3, waiting for transfers between devices, y_permute(): return lax.ppermute(a, 'head', pairs)  5.47 us
    all_to_all x1, starting transfers between devices, local(): lax.all_to_all(copies, 'store', split_axis=0, concat_axis=0, tiled=True,...  4.24 us
    pallas_call x1, Pallas kernels, pick_near(): pl.pallas_call(functools.partial(pick_near_kernel, shifts), out_shape=[ja...  4.11 us
  transfers between devices with their start and end apart: 17, of which 11 were waited for; matrix products, arithmetic and copies ran while one was open for 0% of the time, Pallas kernels for 15%

profile of v9, /device:TPU:24, one launch (start us, length us, event | category | flops | bytes accessed | tf_op | source)
XLA Modules:
  0.0 110.4 jit_solution(8000961640481818017)
XLA Ops:
  0.7 2.0 %wanted_slots.1 = (s32[32,1,128]{2,1,0:T(1,128)S(1)}, bf16[8,64,1024]{2,1,0:T(8,128)(2,1)}) custom-call(s32[1]{0:T(128)S(6)} %copy.8.length_ref, s32[1,128]{1,0:T(1,128)} %owner_hbm.1, s32[1,128]{1,0:T(1,128)} %slot_hbm.1, bf16[64,1024]{1,0:T(8,128)(2,1)} %refs_7_.2), custom_call_target="tpu_custom_call" | custom-call | tf_op jit(solution)/shard_map/wanted_slots/pallas_call | solution.py:101
  2.7 20.8 %all_to_all.10.table_ref.refs_1_ = s32[32,1,128]{2,1,0:T(1,128)S(1)} all-to-all(s32[32,1,128]{2,1,0:T(1,128)S(1)} %get-tuple-element.24), channel_id=1, replica_groups=mesh['store'=32,'head'=8] {'store'}, dimensions={0} | all-to-all | bytes 32768 | tf_op jit(solution)/shard_map/all_to_all | solution.py:421
  23.5 4.2 %all-to-all-start.1 = ((bf16[8,64,1024]{2,1,0:T(8,128)(2,1)}), bf16[8,64,1024]{2,1,0:T(8,128)(2,1)}, u32[]{:S(2)}, u32[]{:S(2)}) async-start(bf16[8,64,1024]{2,1,0:T(8,128)(2,1)} %get-tuple-element.25), calls=%async_computation.1 | async-start | bytes 2097152 | tf_op jit(solution)/shard_map/all_to_all | solution.py:433
  27.8 2.4 %pick_far.1 = (bf16[12,64,256]{2,1,0:T(8,128)(2,1)S(1)}, bf16[12,64,256]{2,1,0:T(8,128)(2,1)S(1)}, bf16[12,64,256]{2,1,0:T(8,128)(2,1)S(1)}) custom-call(s32[1]{0:T(128)} %bitcast.1.me_ref.refs_0_, s32[32,1,128]{2,1,0:T(1,128)S(1)} %all_to_all.10.table_ref.refs_1_, bf16[128,64,256]{2,1,0:T(8,128)(2,1)} %bitcast.17), custom_call_target="tpu_custom_call" | custom-call | tf_op jit(solution)/shard_map/pick_far/pallas_call | solution.py:150
  30.8 2.2 %collective-permute-start.4 = (bf16[12,64,256]{2,1,0:T(8,128)(2,1)S(1)}, bf16[12,64,256]{2,1,0:T(8,128)(2,1)S(1)}, u32[]{:S(2)}, u32[]{:S(2)}) collective-permute-start(bf16[12,64,256]{2,1,0:T(8,128)(2,1)S(1)} %get-tuple-element.30), channel_id=1, source_target_pairs={{0,16},{8,24},{16,0},{24,8},{32,48},{40,56},{48,32},{56,40},{64,80... | collective-permute-start | bytes 1179656 | tf_op jit(solution)/shard_map/ppermute | solution.py:390
  34.1 4.1 %pick_near.1 = (bf16[20,64,256]{2,1,0:T(8,128)(2,1)}, bf16[20,64,256]{2,1,0:T(8,128)(2,1)}, bf16[20,64,256]{2,1,0:T(8,128)(2,1)}) custom-call(s32[1]{0:T(128)} %bitcast.1.me_ref.refs_0_, s32[32,1,128]{2,1,0:T(1,128)S(1)} %all_to_all.10.table_ref.refs_1_, bf16[128,64,256]{2,1,0:T(8,128)(2,1)} %bitcast.18), custom_call_target="tpu_custom_call" | custom-call | tf_op jit(solution)/shard_map/pick_near/pallas_call | solution.py:176
  39.2 1.5 %collective-permute-start.1 = (bf16[20,64,256]{2,1,0:T(8,128)(2,1)}, bf16[20,64,256]{2,1,0:T(8,128)(2,1)S(1)}, u32[]{:S(2)}, u32[]{:S(2)}) collective-permute-start(bf16[20,64,256]{2,1,0:T(8,128)(2,1)} %get-tuple-element.27), channel_id=1, source_target_pairs={{0,16},{8,24},{16,0},{24,8},{32,48},{40,56},{48,32},{56,40},{64,80... | collective-permute-start | bytes 1966088 | tf_op jit(solution)/shard_map/ppermute | solution.py:390
  40.7 10.6 %collective-permute-done.3.refs_4_ = bf16[12,64,256]{2,1,0:T(8,128)(2,1)S(1)} collective-permute-done((bf16[12,64,256]{2,1,0:T(8,128)(2,1)S(1)}, bf16[12,64,256]{2,1,0:T(8,128)(2,1)S(1)}, u32[]{:S(2)}, u32[]{:S(2)}) %collective-permute-start.3) | collective-permute-done | bytes 393248 | tf_op jit(solution)/shard_map/ppermute | solution.py:390
  51.5 1.3 %collective-permute-done.5.refs_6_ = bf16[12,64,256]{2,1,0:T(8,128)(2,1)S(1)} collective-permute-done((bf16[12,64,256]{2,1,0:T(8,128)(2,1)S(1)}, bf16[12,64,256]{2,1,0:T(8,128)(2,1)S(1)}, u32[]{:S(2)}, u32[]{:S(2)}) %collective-permute-start.5) | collective-permute-done | bytes 393248 | tf_op jit(solution)/shard_map/ppermute | solution.py:390
  52.8 2.5 %all-to-all-done.1.refs_3_ = bf16[8,64,1024]{2,1,0:T(8,128)(2,1)} async-done(((bf16[8,64,1024]{2,1,0:T(8,128)(2,1)}), bf16[8,64,1024]{2,1,0:T(8,128)(2,1)}, u32[]{:S(2)}, u32[]{:S(2)}) %all-to-all-start.1) | async-done | bytes 1048608 | tf_op jit(solution)/shard_map/all_to_all | solution.py:433
  55.4 4.4 %attend_chunk.3 = (bf16[2,144,512]{2,1,0:T(8,128)(2,1)S(1)}, bf16[144,512]{1,0:T(8,128)(2,1)S(1)}, bf16[144,512]{1,0:T(8,128)(2,1)S(1)}) custom-call(s32[1]{0:T(128)} %bitcast.1.me_ref.refs_0_, s32[32,1,128]{2,1,0:T(1,128)S(1)} %all_to_all.10.table_ref.refs_1_, bf16[128,64,256]{2,1,0:T(8,128)(2,1)} %bitcast.19, bf16[8,64,1024]{2,1,0:T(8,128)(2,1)} %all-to-all-done.1.refs_3_, ...), custom_call_target="tpu_custom_call" | custom-call | flops 805306368 | bytes 1572864 | tf_op jit(solution)/shard_map/attend_chunk/pallas_call | solution.py:333
  60.2 3.8 %collective-permute-start.7 = (bf16[144,512]{1,0:T(8,128)(2,1)S(1)}, bf16[144,512]{1,0:T(8,128)(2,1)S(1)}, u32[]{:S(2)}, u32[]{:S(2)}) collective-permute-start(bf16[144,512]{1,0:T(8,128)(2,1)S(1)} %get-tuple-element.33), channel_id=1, source_target_pairs={{0,192},{8,200},{16,208},{24,216},{32,224},{40,232},{48,240},{56,2... | collective-permute-start | bytes 442376 | tf_op jit(solution)/shard_map/ppermute | solution.py:395
  64.0 13.4 %collective-permute-done.refs_4_ = bf16[20,64,256]{2,1,0:T(8,128)(2,1)S(1)} collective-permute-done((bf16[20,64,256]{2,1,0:T(8,128)(2,1)}, bf16[20,64,256]{2,1,0:T(8,128)(2,1)S(1)}, u32[]{:S(2)}, u32[]{:S(2)}) %collective-permute-start) | collective-permute-done | bytes 655392 | tf_op jit(solution)/shard_map/ppermute | solution.py:390
  78.1 5.3 %attend_chunk.4 = (bf16[144,512]{1,0:T(8,128)(2,1)S(1)}, bf16[144,512]{1,0:T(8,128)(2,1)S(1)}, bf16[144,512]{1,0:T(8,128)(2,1)S(1)}, bf16[144,512]{1,0:T(8,128)(2,1)S(1)}) custom-call(s32[1]{0:T(128)} %bitcast.1.me_ref.refs_0_, s32[32,1,128]{2,1,0:T(1,128)S(1)} %all_to_all.10.table_ref.refs_1_, bf16[128,64,256]{2,1,0:T(8,128)(2,1)} %bitcast.20, ...), custom_call_target="tpu_custom_call" | custom-call | flops 1073741824 | bytes 2097152 | tf_op jit(solution)/shard_map/attend_chunk/pallas_call | solution.py:333
  83.4 3.1 %collective-permute-start.10 = (bf16[144,512]{1,0:T(8,128)(2,1)S(1)}, bf16[144,512]{1,0:T(8,128)(2,1)S(1)}, u32[]{:S(2)}, u32[]{:S(2)}) collective-permute-start(bf16[144,512]{1,0:T(8,128)(2,1)S(1)} %get-tuple-element.37), channel_id=1, source_target_pairs={{0,224},{8,232},{16,240},{24,248},{32,0},{40,8},{48,16},{56,24},{6... | collective-permute-start | bytes 442376 | tf_op jit(solution)/shard_map/ppermute | solution.py:395
  86.5 1.8 %collective-permute-start.8 = (bf16[144,512]{1,0:T(8,128)(2,1)S(1)}, bf16[144,512]{1,0:T(8,128)(2,1)S(1)}, u32[]{:S(2)}, u32[]{:S(2)}) collective-permute-start(bf16[144,512]{1,0:T(8,128)(2,1)S(1)} %get-tuple-element.34.refs_8_), channel_id=1, source_target_pairs={{0,64},{8,72},{16,80},{24,88},{32,96},{40,104},{48,112},{56,120},{... | collective-permute-start | bytes 442376 | tf_op jit(solution)/shard_map/ppermute | solution.py:395
  88.3 2.4 %collective-permute-start.9 = (bf16[144,512]{1,0:T(8,128)(2,1)S(1)}, bf16[144,512]{1,0:T(8,128)(2,1)S(1)}, u32[]{:S(2)}, u32[]{:S(2)}) collective-permute-start(bf16[144,512]{1,0:T(8,128)(2,1)S(1)} %get-tuple-element.36), channel_id=1, source_target_pairs={{0,192},{8,200},{16,208},{24,216},{32,224},{40,232},{48,240},{56,2... | collective-permute-start | bytes 442376 | tf_op jit(solution)/shard_map/ppermute | solution.py:395
  90.6 5.3 %attend_chunk.5 = (bf16[144,512]{1,0:T(8,128)(2,1)S(1)}, bf16[1024,4096]{1,0:T(8,128)(2,1)S(1)}) custom-call(s32[1]{0:T(128)} %bitcast.1.me_ref.refs_0_, s32[32,1,128]{2,1,0:T(1,128)S(1)} %all_to_all.10.table_ref.refs_1_, bf16[128,64,256]{2,1,0:T(8,128)(2,1)} %bitcast.21, bf16[8,64,1024]{2,1,0:T(8,128)(2,1)} %all-to-all-done.1.refs_3_, ...), custom_call_target="tpu_custom_call" | custom-call | flops 268435456 | bytes 524288 | tf_op jit(solution)/shard_map/attend_chunk/pallas_call | solution.py:333
  97.3 1.8 %merge_project.1 = (bf16[32,4096]{1,0:T(8,128)(2,1)S(1)}, f32[32,4096]{1,0:T(8,128)S(1)}) custom-call(s32[1]{0:T(128)} %bitcast.core_ref, bf16[1024,4096]{1,0:T(8,128)(2,1)S(1)} %get-tuple-element.35.wide_ref, bf16[144,512]{1,0:T(8,128)(2,1)S(1)} %collective-permute-done.8.rest_0_, bf16[144,512]{1,0:T(8,128)(2,1)S(1)} %collective-permute-done.9.rest_1_, ...), custom_call_target="tpu_custom_call" | custom-call | flops 536870912 | bytes 8388608 | tf_op jit(solution)/shard_map/merge_project/pallas_call | solution.py:372
  99.2 1.5 %collective-permute-done.12 = bf16[32,4096]{1,0:T(8,128)(2,1)S(1)} collective-permute-done((bf16[32,4096]{1,0:T(8,128)(2,1)S(1)}, bf16[32,4096]{1,0:T(8,128)(2,1)S(1)}, u32[]{:S(2)}, u32[]{:S(2)}) %collective-permute-start.12) | collective-permute-done | bytes 262176 | tf_op jit(solution)/shard_map/ppermute | solution.py:406
  100.7 1.3 %collective-permute-start.13 = (bf16[8,4096]{1,0:T(8,128)(2,1)S(1)}, bf16[8,4096]{1,0:T(8,128)(2,1)S(1)}, u32[]{:S(2)}, u32[]{:S(2)}) collective-permute-start(bf16[8,4096]{1,0:T(8,128)(2,1)S(1)} %get-tuple-element.43), channel_id=1, source_target_pairs={{0,4},{1,5},{2,6},{3,7},{4,0},{5,1},{6,2},{7,3},{8,12},{9,13},{10,... | collective-permute-start | bytes 196616 | tf_op jit(solution)/shard_map/ppermute | solution.py:402
  102.1 2.2 %collective-permute-start.14 = (bf16[8,4096]{1,0:T(8,128)(2,1)S(1)}, bf16[8,4096]{1,0:T(8,128)(2,1)S(1)}, u32[]{:S(2)}, u32[]{:S(2)}) collective-permute-start(bf16[8,4096]{1,0:T(8,128)(2,1)S(1)} %get-tuple-element.45), channel_id=1, source_target_pairs={{0,2},{1,3},{2,4},{3,5},{4,6},{5,7},{6,0},{7,1},{8,10},{9,11},{10,... | collective-permute-start | bytes 196616 | tf_op jit(solution)/shard_map/ppermute | solution.py:402
  104.3 2.5 %collective-permute-done.13 = bf16[8,4096]{1,0:T(8,128)(2,1)S(1)} collective-permute-done((bf16[8,4096]{1,0:T(8,128)(2,1)S(1)}, bf16[8,4096]{1,0:T(8,128)(2,1)S(1)}, u32[]{:S(2)}, u32[]{:S(2)}) %collective-permute-start.13) | collective-permute-done | bytes 65568 | tf_op jit(solution)/shard_map/ppermute | solution.py:402
  106.7 3.0 %collective-permute-done.15 = bf16[8,4096]{1,0:T(8,128)(2,1)S(1)} collective-permute-done((bf16[8,4096]{1,0:T(8,128)(2,1)S(1)}, bf16[8,4096]{1,0:T(8,128)(2,1)S(1)}, u32[]{:S(2)}, u32[]{:S(2)}) %collective-permute-start.15) | collective-permute-done | bytes 65568 | tf_op jit(solution)/shard_map/ppermute | solution.py:402
  (25 shorter events, 6.2 us)
Async XLA Ops:
  0.0 55.3 %copy-start = (bf16[64,1024]{1,0:T(8,128)(2,1)S(1)}, bf16[64,1024]{1,0:T(8,128)(2,1)}, u32[]{:S(2)}) copy-start(bf16[64,1024]{1,0:T(8,128)(2,1)} %refs_7_.2) | copy-start | bytes 393220
  0.0 55.3 %copy-start.1 = (bf16[64,1,256]{2,0,1:T(8,128)(2,1)S(1)}, bf16[64,1,256]{2,0,1:T(8,128)(2,1)}, u32[]{:S(2)}) copy-start(bf16[64,1,256]{2,0,1:T(8,128)(2,1)} %param.8) | copy-start | bytes 98308
  23.5 31.8 %all-to-all-start.1 = ((bf16[8,64,1024]{2,1,0:T(8,128)(2,1)}), bf16[8,64,1024]{2,1,0:T(8,128)(2,1)}, u32[]{:S(2)}, u32[]{:S(2)}) async-start(bf16[8,64,1024]{2,1,0:T(8,128)(2,1)} %get-tuple-element.25), calls=%async_computation.1 | async-start | bytes 2097152 | tf_op jit(solution)/shard_map/all_to_all | solution.py:433
  30.2 21.0 %collective-permute-start.3 = (bf16[12,64,256]{2,1,0:T(8,128)(2,1)S(1)}, bf16[12,64,256]{2,1,0:T(8,128)(2,1)S(1)}, u32[]{:S(2)}, u32[]{:S(2)}) collective-permute-start(bf16[12,64,256]{2,1,0:T(8,128)(2,1)S(1)} %get-tuple-element.29), channel_id=1, source_target_pairs={{0,8},{8,16},{16,24},{24,0},{32,40},{40,48},{48,56},{56,32},{64,72... | collective-permute-start | bytes 1179656 | tf_op jit(solution)/shard_map/ppermute | solution.py:390
  30.8 20.7 %collective-permute-start.4 = (bf16[12,64,256]{2,1,0:T(8,128)(2,1)S(1)}, bf16[12,64,256]{2,1,0:T(8,128)(2,1)S(1)}, u32[]{:S(2)}, u32[]{:S(2)}) collective-permute-start(bf16[12,64,256]{2,1,0:T(8,128)(2,1)S(1)} %get-tuple-element.30), channel_id=1, source_target_pairs={{0,16},{8,24},{16,0},{24,8},{32,48},{40,56},{48,32},{56,40},{64,80... | collective-permute-start | bytes 1179656 | tf_op jit(solution)/shard_map/ppermute | solution.py:390
  33.0 19.8 %collective-permute-start.5 = (bf16[12,64,256]{2,1,0:T(8,128)(2,1)S(1)}, bf16[12,64,256]{2,1,0:T(8,128)(2,1)S(1)}, u32[]{:S(2)}, u32[]{:S(2)}) collective-permute-start(bf16[12,64,256]{2,1,0:T(8,128)(2,1)S(1)} %get-tuple-element.31), channel_id=1, source_target_pairs={{0,24},{8,0},{16,8},{24,16},{32,56},{40,32},{48,40},{56,48},{64,88... | collective-permute-start | bytes 1179656 | tf_op jit(solution)/shard_map/ppermute | solution.py:390
  38.2 39.2 %collective-permute-start = (bf16[20,64,256]{2,1,0:T(8,128)(2,1)}, bf16[20,64,256]{2,1,0:T(8,128)(2,1)S(1)}, u32[]{:S(2)}, u32[]{:S(2)}) collective-permute-start(bf16[20,64,256]{2,1,0:T(8,128)(2,1)} %get-tuple-element.26), channel_id=1, source_target_pairs={{0,8},{8,16},{16,24},{24,0},{32,40},{40,48},{48,56},{56,32},{64,72... | collective-permute-start | bytes 1966088 | tf_op jit(solution)/shard_map/ppermute | solution.py:390
  39.2 38.3 %collective-permute-start.1 = (bf16[20,64,256]{2,1,0:T(8,128)(2,1)}, bf16[20,64,256]{2,1,0:T(8,128)(2,1)S(1)}, u32[]{:S(2)}, u32[]{:S(2)}) collective-permute-start(bf16[20,64,256]{2,1,0:T(8,128)(2,1)} %get-tuple-element.27), channel_id=1, source_target_pairs={{0,16},{8,24},{16,0},{24,8},{32,48},{40,56},{48,32},{56,40},{64,80... | collective-permute-start | bytes 1966088 | tf_op jit(solution)/shard_map/ppermute | solution.py:390
  51.2 26.9 %collective-permute-start.2 = (bf16[20,64,256]{2,1,0:T(8,128)(2,1)}, bf16[20,64,256]{2,1,0:T(8,128)(2,1)S(1)}, u32[]{:S(2)}, u32[]{:S(2)}) collective-permute-start(bf16[20,64,256]{2,1,0:T(8,128)(2,1)} %get-tuple-element.28), channel_id=1, source_target_pairs={{0,24},{8,0},{16,8},{24,16},{32,56},{40,32},{48,40},{56,48},{64,88... | collective-permute-start | bytes 1966088 | tf_op jit(solution)/shard_map/ppermute | solution.py:390
  59.8 18.3 %collective-permute-start.6 = (bf16[2,144,512]{2,1,0:T(8,128)(2,1)S(1)}, bf16[2,144,512]{2,1,0:T(8,128)(2,1)S(1)}, u32[]{:S(2)}, u32[]{:S(2)}) collective-permute-start(bf16[2,144,512]{2,1,0:T(8,128)(2,1)S(1)} %get-tuple-element.32), channel_id=1, source_target_pairs={{0,64},{8,72},{16,80},{24,88},{32,96},{40,104},{48,112},{56,120},{... | collective-permute-start | bytes 884744 | tf_op jit(solution)/shard_map/ppermute | solution.py:395
  60.2 17.9 %collective-permute-start.7 = (bf16[144,512]{1,0:T(8,128)(2,1)S(1)}, bf16[144,512]{1,0:T(8,128)(2,1)S(1)}, u32[]{:S(2)}, u32[]{:S(2)}) collective-permute-start(bf16[144,512]{1,0:T(8,128)(2,1)S(1)} %get-tuple-element.33), channel_id=1, source_target_pairs={{0,192},{8,200},{16,208},{24,216},{32,224},{40,232},{48,240},{56,2... | collective-permute-start | bytes 442376 | tf_op jit(solution)/shard_map/ppermute | solution.py:395
  83.4 12.5 %collective-permute-start.10 = (bf16[144,512]{1,0:T(8,128)(2,1)S(1)}, bf16[144,512]{1,0:T(8,128)(2,1)S(1)}, u32[]{:S(2)}, u32[]{:S(2)}) collective-permute-start(bf16[144,512]{1,0:T(8,128)(2,1)S(1)} %get-tuple-element.37), channel_id=1, source_target_pairs={{0,224},{8,232},{16,240},{24,248},{32,0},{40,8},{48,16},{56,24},{6... | collective-permute-start | bytes 442376 | tf_op jit(solution)/shard_map/ppermute | solution.py:395
  86.5 9.6 %collective-permute-start.11 = (bf16[144,512]{1,0:T(8,128)(2,1)S(1)}, bf16[144,512]{1,0:T(8,128)(2,1)S(1)}, u32[]{:S(2)}, u32[]{:S(2)}) collective-permute-start(bf16[144,512]{1,0:T(8,128)(2,1)S(1)} %get-tuple-element.38), channel_id=1, source_target_pairs={{0,32},{8,40},{16,48},{24,56},{32,64},{40,72},{48,80},{56,88},{64,... | collective-permute-start | bytes 442376 | tf_op jit(solution)/shard_map/ppermute | solution.py:395
  86.5 10.8 %collective-permute-start.8 = (bf16[144,512]{1,0:T(8,128)(2,1)S(1)}, bf16[144,512]{1,0:T(8,128)(2,1)S(1)}, u32[]{:S(2)}, u32[]{:S(2)}) collective-permute-start(bf16[144,512]{1,0:T(8,128)(2,1)S(1)} %get-tuple-element.34.refs_8_), channel_id=1, source_target_pairs={{0,64},{8,72},{16,80},{24,88},{32,96},{40,104},{48,112},{56,120},{... | collective-permute-start | bytes 442376 | tf_op jit(solution)/shard_map/ppermute | solution.py:395
  88.3 9.0 %collective-permute-start.9 = (bf16[144,512]{1,0:T(8,128)(2,1)S(1)}, bf16[144,512]{1,0:T(8,128)(2,1)S(1)}, u32[]{:S(2)}, u32[]{:S(2)}) collective-permute-start(bf16[144,512]{1,0:T(8,128)(2,1)S(1)} %get-tuple-element.36), channel_id=1, source_target_pairs={{0,192},{8,200},{16,208},{24,216},{32,224},{40,232},{48,240},{56,2... | collective-permute-start | bytes 442376 | tf_op jit(solution)/shard_map/ppermute | solution.py:395
  99.0 1.6 %collective-permute-start.12 = (bf16[32,4096]{1,0:T(8,128)(2,1)S(1)}, bf16[32,4096]{1,0:T(8,128)(2,1)S(1)}, u32[]{:S(2)}, u32[]{:S(2)}) collective-permute-start(bf16[32,4096]{1,0:T(8,128)(2,1)S(1)} %get-tuple-element.42), channel_id=1, source_target_pairs={{0,1},{1,0},{2,3},{3,2},{4,5},{5,4},{6,7},{7,6},{8,9},{9,8},{10,11... | collective-permute-start | bytes 786440 | tf_op jit(solution)/shard_map/ppermute | solution.py:406
  100.7 6.0 %collective-permute-start.13 = (bf16[8,4096]{1,0:T(8,128)(2,1)S(1)}, bf16[8,4096]{1,0:T(8,128)(2,1)S(1)}, u32[]{:S(2)}, u32[]{:S(2)}) collective-permute-start(bf16[8,4096]{1,0:T(8,128)(2,1)S(1)} %get-tuple-element.43), channel_id=1, source_target_pairs={{0,4},{1,5},{2,6},{3,7},{4,0},{5,1},{6,2},{7,3},{8,12},{9,13},{10,... | collective-permute-start | bytes 196616 | tf_op jit(solution)/shard_map/ppermute | solution.py:402
  102.1 4.7 %collective-permute-start.14 = (bf16[8,4096]{1,0:T(8,128)(2,1)S(1)}, bf16[8,4096]{1,0:T(8,128)(2,1)S(1)}, u32[]{:S(2)}, u32[]{:S(2)}) collective-permute-start(bf16[8,4096]{1,0:T(8,128)(2,1)S(1)} %get-tuple-element.45), channel_id=1, source_target_pairs={{0,2},{1,3},{2,4},{3,5},{4,6},{5,7},{6,0},{7,1},{8,10},{9,11},{10,... | collective-permute-start | bytes 196616 | tf_op jit(solution)/shard_map/ppermute | solution.py:402
  104.2 5.5 %collective-permute-start.15 = (bf16[8,4096]{1,0:T(8,128)(2,1)S(1)}, bf16[8,4096]{1,0:T(8,128)(2,1)S(1)}, u32[]{:S(2)}, u32[]{:S(2)}) collective-permute-start(bf16[8,4096]{1,0:T(8,128)(2,1)S(1)} %get-tuple-element.44), channel_id=1, source_target_pairs={{0,6},{1,7},{2,0},{3,1},{4,2},{5,3},{6,4},{7,5},{8,14},{9,15},{10,... | collective-permute-start | bytes 196616 | tf_op jit(solution)/shard_map/ppermute | solution.py:402
